TPU v7x, 128 devices: a whole 4x4x4 slice. The times are simulated.
128 devices in a mesh: section: 2 (over x_hi), dp: 8 (over z, core), fsdp: 8 (over x_lo, y).
Axes of the slice: x: 4 (x_hi: 2, x_lo: 2; x = x_hi * 2 + x_lo), y: 4, z: 4, core: 2. Of those that a mesh axis runs over, the one named last changes fastest.
Arguments:
- inputs: bfloat16 [2, 8, 1024, 960], P(None, 'dp', 'fsdp'), may hold values from -6 to 6
- positions: int32 [2, 8, 1024], P(None, 'dp', 'fsdp'), may hold values from 0 to 2046, as said below
- plan: int32 [8, 2], P('dp'), may hold values from 0 to 1, as said below
- attend_in: bfloat16 [2, 960, 1600], P('section', 'fsdp'), may hold values from -0.1875 to 0.1875
- attend_out: bfloat16 [2, 960, 960], P('section', 'fsdp'), may hold values from -1 to 1
- gate_up: bfloat16 [2, 960, 5120], P('section', 'fsdp'), may hold values from -0.1875 to 0.1875
- down_weight: bfloat16 [2, 2560, 960], P('section', 'fsdp'), may hold values from -0.25 to 0.25
- norm_gains: bfloat16 [2, 2, 960], P('section', None, 'fsdp'), may hold values from 0.25 to 1.75
- cotangent: bfloat16 [2, 8, 1024, 960], P(None, 'dp', 'fsdp'), may hold values from -6 to 6
Outputs:
- activations: bfloat16 [2, 2, 8, 1024, 960], P('section', None, 'dp', 'fsdp')
- input_grads: float32 [2, 2, 8, 1024, 960], P('section', None, 'dp', 'fsdp')
- attend_in_gradient: float32 [2, 960, 1600], P('section', 'fsdp')
- attend_out_gradient: float32 [2, 960, 960], P('section', 'fsdp')
- gate_up_gradient: float32 [2, 960, 5120], P('section', 'fsdp')
- down_gradient: float32 [2, 2560, 960], P('section', 'fsdp')
- gains_gradient: float32 [2, 2, 960], P('section', None, 'fsdp')
Inputs may be any that keep to these rules, and one draw needn't show every extreme that they name: Along each sequence the positions start at 0, rise by 1 to 3 from token to token, and end at 2046. `plan`: each row is a permutation of 0 .. 1.
All inputs are finite; a program needn't handle non-finite values.
Results may differ from a plain program's by a relative error of at most 0.025.
Values may be sent and summed in bfloat16 or wider, within the bound.
A program may use at most 256 MiB of HBM per device.

v0:
```python
import jax
import jax.numpy as jnp
from jax import lax
from jax.sharding import PartitionSpec as P

D = 960
QUERY_HEADS = 15
KEY_VALUE_HEADS = 5
HEAD_WIDTH = 64
FF = 2560


EPSILON = 1e-05
BASE = 10000.0


def passed_along(value, axis, steps):
    count = lax.axis_size(axis)
    first, last = (max(0, -steps), min(count, count - steps))
    return lax.ppermute(value, axis, [(source, source + steps) for source in range(first, last)])


def rotary_tables(places):
    half = HEAD_WIDTH // 2
    frequency = BASE ** (-(jnp.arange(half).astype(jnp.float32) * (2.0 / HEAD_WIDTH)))
    angle = places.astype(jnp.float32)[:, None] * frequency[None, :]
    cosine_table = jnp.cos(angle)
    sine_table = jnp.sin(angle)
    return (
        jnp.concatenate([cosine_table, cosine_table], -1),
        jnp.concatenate([sine_table, sine_table], -1),
    )


def apply_rotation(values, cosine_table, sine_table):
    half = values.shape[-1] // 2
    turned = jnp.concatenate([-values[..., half:], values[..., :half]], -1)
    return values * cosine_table[:, None, :] + turned * sine_table[:, None, :]


def reverse_rotation(values, cosine_table, sine_table):
    half = values.shape[-1] // 2
    shifted = values * sine_table[:, None, :]
    turned = jnp.concatenate([-shifted[..., half:], shifted[..., :half]], -1)
    return values * cosine_table[:, None, :] - turned


def normed(values, gain):
    return values * lax.rsqrt(jnp.mean(values * values, -1, keepdims=True) + EPSILON) * gain


def norm_backward(values, gain, upstream):
    row_scale = lax.rsqrt(jnp.mean(values * values, -1, keepdims=True) + EPSILON)
    unit = values * row_scale
    gain_slope = jnp.sum(upstream * unit, 0)
    inner = upstream * gain
    return (row_scale * (inner - unit * jnp.mean(inner * unit, -1, keepdims=True)), gain_slope)


def masked_scores(query_matrix, key_value_pair, shard_index):
    local_count = query_matrix.shape[0]
    token_length = key_value_pair.shape[0]
    grouped_heads = query_matrix.reshape(
        local_count, KEY_VALUE_HEADS, QUERY_HEADS // KEY_VALUE_HEADS, HEAD_WIDTH
    )
    key_rows = key_value_pair[:, : KEY_VALUE_HEADS * HEAD_WIDTH].reshape(
        token_length, KEY_VALUE_HEADS, HEAD_WIDTH
    )
    scores = jnp.einsum(
        "tgqd,sgd->gqts", grouped_heads, key_rows, preferred_element_type=jnp.float32
    ) * HEAD_WIDTH ** (-0.5)
    query_rows = shard_index * local_count + jnp.arange(local_count)
    causal = query_rows[:, None] >= jnp.arange(token_length)[None, :]
    return jnp.where(causal[None, None], scores, -1e30)


def forward_layer(layer_in, places, weights, shard_index):
    attend_in, attend_out, gate_up, down_weight, gains = weights
    local_count = layer_in.shape[0]
    values = layer_in.astype(jnp.float32)
    first_norm = normed(values, gains[0]).astype(jnp.bfloat16)
    projected_output = jnp.dot(first_norm, attend_in, preferred_element_type=jnp.float32)
    cosine_table, sine_table = rotary_tables(places)
    query_width = QUERY_HEADS * HEAD_WIDTH
    key_width = KEY_VALUE_HEADS * HEAD_WIDTH
    query_matrix = apply_rotation(
        projected_output[:, :query_width].reshape(local_count, QUERY_HEADS, HEAD_WIDTH),
        cosine_table,
        sine_table,
    )
    query_matrix = query_matrix.astype(jnp.bfloat16).reshape(local_count, query_width)
    key_rows = apply_rotation(
        projected_output[:, query_width : query_width + key_width].reshape(
            local_count, KEY_VALUE_HEADS, HEAD_WIDTH
        ),
        cosine_table,
        sine_table,
    )
    key_rows = key_rows.astype(jnp.bfloat16).reshape(local_count, key_width)
    value_rows = projected_output[:, query_width + key_width :].astype(jnp.bfloat16)
    key_value_pair = lax.all_gather(
        jnp.concatenate([key_rows, value_rows], 1), "fsdp", axis=0, tiled=True
    )
    scores = masked_scores(query_matrix, key_value_pair, shard_index)
    highest = jnp.max(scores, -1)
    totals = highest + jnp.log(jnp.sum(jnp.exp(scores - highest[..., None]), -1))
    probs = jnp.exp(scores - totals[..., None]).astype(jnp.bfloat16)
    complete_values = key_value_pair[:, key_width:].reshape(
        key_value_pair.shape[0], KEY_VALUE_HEADS, HEAD_WIDTH
    )
    mixed = jnp.einsum("gqts,sgd->tgqd", probs, complete_values, preferred_element_type=jnp.float32)
    mixed = mixed.astype(jnp.bfloat16).reshape(local_count, query_width)
    hidden = values + jnp.dot(mixed, attend_out, preferred_element_type=jnp.float32)
    second_norm = normed(hidden, gains[1]).astype(jnp.bfloat16)
    gated = jnp.dot(second_norm, gate_up, preferred_element_type=jnp.float32)
    act = (jax.nn.silu(gated[:, :FF]) * gated[:, FF:]).astype(jnp.bfloat16)
    result = hidden + jnp.dot(act, down_weight, preferred_element_type=jnp.float32)
    kept = (
        layer_in,
        first_norm,
        query_matrix,
        key_value_pair,
        totals,
        mixed,
        hidden,
        second_norm,
        gated,
        act,
    )
    return (result, kept)


def backward_layer(upstream, kept, places, weights, shard_index):
    attend_in, attend_out, gate_up, down_weight, gains = weights
    (
        layer_in,
        first_norm,
        query_matrix,
        key_value_pair,
        totals,
        mixed,
        hidden,
        second_norm,
        gated,
        act,
    ) = kept
    local_count = layer_in.shape[0]
    token_length = key_value_pair.shape[0]
    query_width = QUERY_HEADS * HEAD_WIDTH
    key_width = KEY_VALUE_HEADS * HEAD_WIDTH
    scale = HEAD_WIDTH ** (-0.5)
    down_in = upstream.astype(jnp.bfloat16)
    down_slope = jnp.einsum("tf,td->fd", act, down_in, preferred_element_type=jnp.float32)
    act_slope = jnp.einsum("td,fd->tf", down_in, down_weight, preferred_element_type=jnp.float32)
    gate_part = gated[:, :FF]
    up_part = gated[:, FF:]
    sigma = jax.nn.sigmoid(gate_part)
    gate_slope = act_slope * up_part * sigma * (1.0 + gate_part * (1.0 - sigma))
    up_slope = act_slope * gate_part * sigma
    gated_slope = jnp.concatenate([gate_slope, up_slope], 1).astype(jnp.bfloat16)
    gate_up_slope = jnp.einsum(
        "td,tf->df", second_norm, gated_slope, preferred_element_type=jnp.float32
    )
    second_slope = jnp.einsum("tf,df->td", gated_slope, gate_up, preferred_element_type=jnp.float32)
    hidden_part, second_gain = norm_backward(hidden, gains[1], second_slope)
    hidden_slope = upstream + hidden_part
    branch_slope = hidden_slope.astype(jnp.bfloat16)
    out_slope = jnp.einsum("tq,td->qd", mixed, branch_slope, preferred_element_type=jnp.float32)
    mixed_gradient = jnp.einsum(
        "td,qd->tq", branch_slope, attend_out, preferred_element_type=jnp.float32
    )
    mixed_gradient = mixed_gradient.astype(jnp.bfloat16).reshape(
        local_count, KEY_VALUE_HEADS, QUERY_HEADS // KEY_VALUE_HEADS, HEAD_WIDTH
    )
    scores = masked_scores(query_matrix, key_value_pair, shard_index)
    probs = jnp.exp(scores - totals[..., None])
    probs_low = probs.astype(jnp.bfloat16)
    complete_keys = key_value_pair[:, :key_width].reshape(token_length, KEY_VALUE_HEADS, HEAD_WIDTH)
    complete_values = key_value_pair[:, key_width:].reshape(
        token_length, KEY_VALUE_HEADS, HEAD_WIDTH
    )
    prob_slope = jnp.einsum(
        "tgqd,sgd->gqts", mixed_gradient, complete_values, preferred_element_type=jnp.float32
    )
    score_slope = probs * (prob_slope - jnp.sum(probs * prob_slope, -1, keepdims=True))
    score_slope = score_slope.astype(jnp.bfloat16)
    query_slope = (
        jnp.einsum("gqts,sgd->tgqd", score_slope, complete_keys, preferred_element_type=jnp.float32)
        * scale
    )
    grouped_heads = query_matrix.reshape(
        local_count, KEY_VALUE_HEADS, QUERY_HEADS // KEY_VALUE_HEADS, HEAD_WIDTH
    )
    key_part = (
        jnp.einsum("gqts,tgqd->sgd", score_slope, grouped_heads, preferred_element_type=jnp.float32)
        * scale
    )
    val_part = jnp.einsum(
        "gqts,tgqd->sgd", probs_low, mixed_gradient, preferred_element_type=jnp.float32
    )
    owned_part = lax.psum_scatter(
        jnp.concatenate(
            [
                key_part.reshape(lax.axis_size("fsdp") * local_count, key_width),
                val_part.reshape(lax.axis_size("fsdp") * local_count, key_width),
            ],
            1,
        ).astype(jnp.bfloat16),
        "fsdp",
        scatter_dimension=0,
        tiled=True,
    ).astype(jnp.float32)
    cosine_table, sine_table = rotary_tables(places)
    query_raw = reverse_rotation(
        query_slope.reshape(local_count, QUERY_HEADS, HEAD_WIDTH), cosine_table, sine_table
    ).reshape(local_count, query_width)
    unrotated_key = reverse_rotation(
        owned_part[:, :key_width].reshape(local_count, KEY_VALUE_HEADS, HEAD_WIDTH),
        cosine_table,
        sine_table,
    ).reshape(local_count, key_width)
    projected_slope = jnp.concatenate(
        [query_raw, unrotated_key, owned_part[:, key_width:]], 1
    ).astype(jnp.bfloat16)
    in_slope = jnp.einsum(
        "td,tf->df", first_norm, projected_slope, preferred_element_type=jnp.float32
    )
    first_slope = jnp.einsum(
        "tf,df->td", projected_slope, attend_in, preferred_element_type=jnp.float32
    )
    input_part, first_gain = norm_backward(layer_in.astype(jnp.float32), gains[0], first_slope)
    input_slope = hidden_slope + input_part
    gain_slopes = jnp.stack([first_gain, second_gain])
    return (input_slope, (in_slope, out_slope, gate_up_slope, down_slope, gain_slopes))


def pick(buffer, index):
    return lax.dynamic_index_in_dim(buffer, index, 0, keepdims=False)


def store(buffer, index, value, valid):
    previous = pick(buffer, index)
    return lax.dynamic_update_index_in_dim(buffer, jnp.where(valid, value, previous), index, 0)


def regroup(array, axis_dim, shards, groups):
    array_shape = array.shape
    pieces = array_shape[axis_dim] // (shards * groups)
    split = array_shape[:axis_dim] + (shards, groups, pieces) + array_shape[axis_dim + 1 :]
    return jnp.swapaxes(array.reshape(split), axis_dim, axis_dim + 1).reshape(array_shape)


def body(
    inputs, positions, plan, attend_in, attend_out, gate_up, down_weight, norm_gains, cotangent
):
    section_index = lax.axis_index("section")
    section_count = lax.axis_size("section")
    shard_index = lax.axis_index("fsdp")
    batches = inputs.shape[0]
    local_count = inputs.shape[2]
    ticks = batches + section_count - 1
    gathered = (
        lax.all_gather(attend_in[0], "fsdp", axis=0, tiled=True),
        lax.all_gather(attend_out[0], "fsdp", axis=0, tiled=True),
        lax.all_gather(gate_up[0], "fsdp", axis=0, tiled=True),
        lax.all_gather(down_weight[0], "fsdp", axis=0, tiled=True),
        lax.all_gather(norm_gains[0], "fsdp", axis=1, tiled=True),
    )
    weights = (gathered[0], gathered[1], gathered[2], gathered[3], gathered[4].astype(jnp.float32))
    plan_row = plan[0]
    received = jnp.zeros((local_count, D), jnp.bfloat16)
    outputs = jnp.zeros((batches, local_count, D), jnp.bfloat16)
    kept_buffer = None
    for tick_index in range(ticks):
        slot = tick_index - section_index
        valid = (slot >= 0) & (slot < batches)
        place = jnp.clip(slot, 0, batches - 1)
        batch_index = pick(plan_row, place)
        fresh = pick(inputs[:, 0], batch_index)
        places = pick(positions[:, 0], batch_index)
        layer_in = jnp.where(section_index == 0, fresh, received)
        result, kept = forward_layer(layer_in, places, weights, shard_index)
        result_low = result.astype(jnp.bfloat16)
        outputs = store(outputs, place, result_low, valid)
        if kept_buffer is None:
            kept_buffer = jax.tree.map(
                lambda item: jnp.zeros((batches,) + item.shape, item.dtype), kept
            )
        kept_buffer = jax.tree.map(
            lambda buffer, item: store(buffer, place, item, valid), kept_buffer, kept
        )
        if tick_index < ticks - 1:
            received = passed_along(result_low, "section", 1)
    coming_back = jnp.zeros((local_count, D), jnp.bfloat16)
    input_slopes = jnp.zeros((batches, local_count, D), jnp.float32)
    totals = jax.tree.map(lambda weight: jnp.zeros(weight.shape, jnp.float32), weights)
    for tick_index in range(ticks):
        slot = tick_index - (section_count - 1 - section_index)
        valid = (slot >= 0) & (slot < batches)
        place = jnp.clip(slot, 0, batches - 1)
        batch_index = pick(plan_row, place)
        given = pick(cotangent[:, 0], place)
        upstream = jnp.where(section_index == section_count - 1, given, coming_back).astype(
            jnp.float32
        )
        kept = jax.tree.map(lambda buffer: pick(buffer, place), kept_buffer)
        places = pick(positions[:, 0], batch_index)
        input_slope, slopes = backward_layer(upstream, kept, places, weights, shard_index)
        slope_low = input_slope.astype(jnp.bfloat16)
        reported = jnp.where(section_index == 0, input_slope, slope_low.astype(jnp.float32))
        input_slopes = store(input_slopes, batch_index, reported, valid)
        totals = jax.tree.map(
            lambda total, term: total + jnp.where(valid, term, 0.0), totals, slopes
        )
        if tick_index < ticks - 1:
            coming_back = passed_along(slope_low, "section", -1)
    shards = lax.axis_size("fsdp")
    groups = lax.axis_size("dp")
    reordered = (
        regroup(totals[0], 0, shards, groups),
        regroup(totals[1], 0, shards, groups),
        regroup(totals[2], 0, shards, groups),
        regroup(totals[3], 0, shards, groups),
        regroup(totals[4], 1, shards, groups),
    )
    shares = (
        lax.psum_scatter(reordered[0], ("dp", "fsdp"), scatter_dimension=0, tiled=True),
        lax.psum_scatter(reordered[1], ("dp", "fsdp"), scatter_dimension=0, tiled=True),
        lax.psum_scatter(reordered[2], ("dp", "fsdp"), scatter_dimension=0, tiled=True),
        lax.psum_scatter(reordered[3], ("dp", "fsdp"), scatter_dimension=0, tiled=True),
        lax.psum_scatter(reordered[4], ("dp", "fsdp"), scatter_dimension=1, tiled=True),
    )
    summed = (
        lax.all_gather(shares[0].astype(jnp.bfloat16), "dp", axis=0, tiled=True).astype(
            jnp.float32
        ),
        lax.all_gather(shares[1].astype(jnp.bfloat16), "dp", axis=0, tiled=True).astype(
            jnp.float32
        ),
        lax.all_gather(shares[2].astype(jnp.bfloat16), "dp", axis=0, tiled=True).astype(
            jnp.float32
        ),
        lax.all_gather(shares[3].astype(jnp.bfloat16), "dp", axis=0, tiled=True).astype(
            jnp.float32
        ),
        lax.all_gather(shares[4].astype(jnp.bfloat16), "dp", axis=1, tiled=True).astype(
            jnp.float32
        ),
    )
    return (
        outputs[None, :, None],
        input_slopes[None, :, None],
        summed[0][None],
        summed[1][None],
        summed[2][None],
        summed[3][None],
        summed[4][None],
    )


def solution(mesh):
    in_specs = (
        P(None, "dp", "fsdp", None),
        P(None, "dp", "fsdp"),
        P("dp", None),
        P("section", "fsdp", None),
        P("section", "fsdp", None),
        P("section", "fsdp", None),
        P("section", "fsdp", None),
        P("section", None, "fsdp"),
        P(None, "dp", "fsdp", None),
    )
    out_specs = (
        P("section", None, "dp", "fsdp", None),
        P("section", None, "dp", "fsdp", None),
        P("section", "fsdp", None),
        P("section", "fsdp", None),
        P("section", "fsdp", None),
        P("section", "fsdp", None),
        P("section", None, "fsdp"),
    )
    return jax.shard_map(body, mesh=mesh, in_specs=in_specs, out_specs=out_specs, check_vma=False)
```

profile of v0, /device:TPU:1, one launch (start us, length us, event | category | flops | bytes accessed | tf_op | source)
XLA Modules:
  0.0 1516.9 jit_solution(11764287665816268756)
XLA Ops:
  18.0 27.6 %all-gather = bf16[1,2,960]{1,0,2:T(2,128)(2,1)S(1)} all-gather(bf16[1,2,120]{1,0,2:T(2,128)(2,1)S(1)} %copy.115), channel_id=2, replica_groups=mesh['section'=2,'dp'=8,'fsdp'=8] {'fsdp'}, dimensions={2}, use_global_device_ids=true | all-gather | bytes 4320 | tf_op jit(solution)/shard_map/all_gather | solution.py:267
  76.7 26.9 %all-gather.18.cloned.1.call-done = bf16[1024,640]{0,1:T(8,128)(2,1)} async-done(((bf16[128,640]{0,1:T(8,128)(2,1)}), bf16[1024,640]{0,1:T(8,128)(2,1)}) %all-gather.18.cloned.1.call-update) | async-done | bytes 1310736 | tf_op jit(solution)/shard_map/all_gather | solution.py:101
  110.8 35.7 %all-gather.26.cloned.1.call-done = bf16[1,960,960]{2,1,0:T(8,128)(2,1)} async-done(((bf16[1,120,960]{2,1,0:T(8,128)(2,1)}), bf16[1,960,960]{2,1,0:T(8,128)(2,1)}) %all-gather.26.cloned.1.call-update) | async-done | bytes 1843216 | tf_op jit(solution)/shard_map/all_gather | solution.py:264
  149.4 108.5 %all-gather.28.cloned.1.call-done = bf16[1,960,5120]{2,1,0:T(8,128)(2,1)} async-done(((bf16[1,120,5120]{2,1,0:T(8,128)(2,1)}), bf16[1,960,5120]{2,1,0:T(8,128)(2,1)}) %all-gather.28.cloned.1.call-update) | async-done | bytes 9830416 | tf_op jit(solution)/shard_map/all_gather | solution.py:265
  260.8 7.0 bitcast_dynamic-update-slice_fusion.2
  269.2 51.5 %all-gather.30.cloned.1.call-done = bf16[1,2560,960]{2,1,0:T(8,128)(2,1)} async-done(((bf16[1,320,960]{2,1,0:T(8,128)(2,1)}), bf16[1,2560,960]{2,1,0:T(8,128)(2,1)}) %all-gather.30.cloned.1.call-update) | async-done | bytes 4915216 | tf_op jit(solution)/shard_map/all_gather | solution.py:266
  349.9 24.3 %all-gather.20.cloned.1.call-done = bf16[1024,640]{0,1:T(8,128)(2,1)} async-done(((bf16[128,640]{0,1:T(8,128)(2,1)}), bf16[1024,640]{0,1:T(8,128)(2,1)}) %all-gather.20.cloned.1.call-update) | async-done | bytes 1310736 | tf_op jit(solution)/shard_map/all_gather | solution.py:101
  413.2 31.6 %all-gather.22.cloned.1.call-done = bf16[1024,640]{0,1:T(8,128)(2,1)} async-done(((bf16[128,640]{0,1:T(8,128)(2,1)}), bf16[1024,640]{0,1:T(8,128)(2,1)}) %all-gather.22.cloned.1.call-update) | async-done | bytes 1310736 | tf_op jit(solution)/shard_map/all_gather | solution.py:101
  458.7 6.5 dynamic-slice_bitcast_fusion
  508.6 8.2 fusion.172
  516.8 13.3 reduce-scatter.20.cloned.1.call-done
  575.4 8.3 fusion.171
  583.7 23.6 %reduce-scatter.22.cloned.1.call-done = bf16[128,640]{1,0:T(8,128)(2,1)} async-done(((bf16[1024,640]{1,0:T(8,128)(2,1)}), bf16[128,640]{1,0:T(8,128)(2,1)}) %reduce-scatter.22.cloned.1.call-update) | async-done | bytes 163856
  645.0 12.7 select_add_fusion
  676.9 16.2 %reshape.750 = f32[8,8,15,5120]{3,2,1,0:T(8,128)} reshape(f32[960,5120]{1,0:T(8,128)} %select_add_fusion) | data formatting | bytes 39321600 | tf_op jit(solution)/shard_map/reshape | solution.py:250
  693.1 16.4 %copy.131 = f32[8,8,15,5120]{3,2,1,0:T(8,128)} copy(f32[8,8,15,5120]{3,2,0,1:T(8,128)} %bitcast.934) | data formatting | bytes 39321600 | tf_op jit(solution)/shard_map/transpose | solution.py:250
  709.6 16.1 %reshape.751 = f32[960,5120]{1,0:T(8,128)} reshape(f32[8,8,15,5120]{3,2,1,0:T(8,128)} %copy.131) | data formatting | bytes 39321600 | tf_op jit(solution)/shard_map/reshape | solution.py:250
  730.3 6.8 select_add_fusion.2
  737.1 6.2 reshape.744
  743.4 6.4 copy.129
  749.8 6.2 reshape.745
  755.9 352.9 %fusion.369 = (f32[16,1600]{1,0:T(8,128)S(1)}, f32[16,960]{1,0:T(8,128)S(1)}, f32[16,5120]{1,0:T(8,128)S(1)}) fusion(f32[960,1600]{1,0:T(8,128)} %reshape.745, f32[960,960]{1,0:T(8,128)} %reshape.749, f32[960,5120]{1,0:T(8,128)} %reshape.751), kind=kCustom, calls=%all-reduce-scatter.3 | all-reduce-scatter fusion | flops 7864321 | bytes 29983232
  1127.2 12.4 concatenate.206
  1152.3 11.2 copy.132
  1163.5 10.2 copy.133
  1191.8 6.3 collective-permute-start.10
  1216.1 129.5 %all-reduce.3 = bf16[2,960]{1,0:T(2,128)(2,1)S(1)} all-reduce(f32[2,960]{1,0:T(2,128)S(1)} %reshape.754), channel_id=14, replica_groups=mesh['section'=2,'dp'=8,'fsdp'=8] {'dp','fsdp'}, use_global_device_ids=true, to_apply=%region_40.41.clone | all-reduce | flops 1920 | bytes 11520
  1345.7 19.1 %all-gather.8 = bf16[8,15,2]{1,2,0:T(2,128)(2,1)S(1)} all-gather(bf16[1,15,2]{1,2,0:T(2,128)(2,1)S(1)} %fusion.324), channel_id=1, replica_groups=mesh['section'=2,'dp'=8,'fsdp'=8] {'dp'}, dimensions={0}, use_global_device_ids=true | all-gather | bytes 540 | tf_op jit(solution)/shard_map/all_gather | solution.py:346
  1379.2 12.5 all-gather.6
  1394.1 13.2 all-gather.5
  1411.5 70.7 %reduce-scatter.18.cloned.1.call-done = f32[40,960]{1,0:T(8,128)} async-done(((f32[2560,960]{1,0:T(8,128)}), f32[40,960]{1,0:T(8,128)}) %reduce-scatter.18.cloned.1.call-update) | async-done | bytes 153616 | tf_op jit(solution)/shard_map/reduce_scatter | solution.py:330
  1483.2 25.4 %all_gather.50 = bf16[320,960]{1,0:T(8,128)(2,1)S(1)} all-gather(bf16[40,960]{1,0:T(8,128)(2,1)S(1)} %convert_element_type.414), channel_id=1, replica_groups=mesh['section'=2,'dp'=8,'fsdp'=8] {'dp'}, dimensions={0}, use_global_device_ids=true | all-gather | bytes 691200 | tf_op jit(solution)/shard_map/all_gather | solution.py:343
  (677 shorter events, 362.7 us)
Async XLA Ops:
  7.2 53.3 %all-gather.24.cloned.1.call-start = ((), (), s32[]{:S(2)}) async-start(), calls=%async_computation.8 | async-start | bytes 3594240 | tf_op jit(solution)/shard_map/all_gather | solution.py:263
  7.9 95.8 %all-gather.18.cloned.1.call-start = ((), (), s32[]{:S(2)}) async-start(), calls=%async_computation.4 | async-start | bytes 1474560 | tf_op jit(solution)/shard_map/all_gather | solution.py:101
  58.2 557.3 %copy-start.110 = (f32[960]{0:T(1024)}, f32[960]{0:T(1024)S(1)}, u32[]{:S(2)}) copy-start(f32[960]{0:T(1024)S(1)} %get-tuple-element.66) | copy-start | bytes 11524
  65.0 81.5 %all-gather.26.cloned.1.call-start = ((), (), s32[]{:S(2)}) async-start(), calls=%async_computation.9 | async-start | bytes 2211840 | tf_op jit(solution)/shard_map/all_gather | solution.py:264
  65.7 192.2 %all-gather.28.cloned.1.call-start = ((), (), s32[]{:S(2)}) async-start(), calls=%async_computation.10 | async-start | bytes 11059200 | tf_op jit(solution)/shard_map/all_gather | solution.py:265
  66.3 254.4 %all-gather.30.cloned.1.call-start = ((), (), s32[]{:S(2)}) async-start(), calls=%async_computation.11 | async-start | bytes 5898240 | tf_op jit(solution)/shard_map/all_gather | solution.py:266
  66.9 307.4 %all-gather.20.cloned.1.call-start = ((), (), s32[]{:S(2)}) async-start(), calls=%async_computation.5 | async-start | bytes 1474560 | tf_op jit(solution)/shard_map/all_gather | solution.py:101
  149.3 180.9 %copy-start.35 = (bf16[2,128,960]{1,2,0:T(8,128)(2,1)}, bf16[2,128,960]{1,2,0:T(8,128)(2,1)S(1)}, u32[]{:S(2)}) copy-start(bf16[2,128,960]{1,2,0:T(8,128)(2,1)S(1)} %bitcast_dynamic-update-slice_fusion.17) | copy-start | bytes 1474564
  149.4 181.6 %copy-start.12 = (f32[2,128,960]{1,2,0:T(8,128)}, f32[2,128,960]{1,2,0:T(8,128)S(1)}, u32[]{:S(2)}) copy-start(f32[2,128,960]{1,2,0:T(8,128)S(1)} %bitcast_dynamic-update-slice_fusion.14) | copy-start | bytes 2949124
  325.4 8.9 collective-permute-start
  337.8 107.1 %all-gather.22.cloned.1.call-start = ((), (), s32[]{:S(2)}) async-start(), calls=%async_computation.6 | async-start | bytes 1474560 | tf_op jit(solution)/shard_map/all_gather | solution.py:101
  390.0 8.0 collective-permute-start.1
  403.5 126.6 %reduce-scatter.20.cloned.1.call-start = ((), (), s32[]{:S(2)}) async-start(), calls=%async_computation.13 | async-start | bytes 1474560
  489.9 117.4 %reduce-scatter.22.cloned.1.call-start = ((), (), s32[]{:S(2)}) async-start(), calls=%async_computation.14 | async-start | bytes 1474560
  539.8 8.7 collective-permute-start.2
  568.9 160.0 %reduce-scatter.24.cloned.1.call-start = ((), (), s32[]{:S(2)}) async-start(), calls=%async_computation.15 | async-start | bytes 1474560
  617.6 8.7 collective-permute-start.3
  644.8 763.6 %all-gather.32.cloned.1.call-start = ((), (), s32[]{:S(2)}) async-start(), calls=%async_computation.12 | async-start | bytes 1474560 | tf_op jit(solution)/shard_map/all_gather | solution.py:340
  755.9 366.8 %copy-start.11 = (bf16[2,128,2560]{2,1,0:T(8,128)(2,1)S(1)}, bf16[2,128,2560]{2,1,0:T(8,128)(2,1)}, u32[]{:S(2)}) copy-start(bf16[2,128,2560]{2,1,0:T(8,128)(2,1)} %copy-done.10) | copy-start | bytes 3932164
  1109.0 17.8 %collective-permute-start.14 = (bf16[16,5120]{1,0:T(8,128)(2,1)S(1)}, bf16[16,5120]{1,0:T(8,128)(2,1)S(1)}, u32[]{:S(2)}, u32[]{:S(2)}) collective-permute-start(bf16[16,5120]{1,0:T(8,128)(2,1)S(1)} %convert.239), channel_id=1, source_target_pairs={{0,3},{1,4},{2,5},{3,6},{4,7},{5,8},{6,9},{7,10},{8,11},{9,12},{10... | collective-permute-start | bytes 491528
  1110.9 15.8 %collective-permute-start.13 = (bf16[16,5120]{1,0:T(8,128)(2,1)S(1)}, bf16[16,5120]{1,0:T(8,128)(2,1)S(1)}, u32[]{:S(2)}, u32[]{:S(2)}) collective-permute-start(bf16[16,5120]{1,0:T(8,128)(2,1)S(1)} %convert.239), channel_id=1, source_target_pairs={{0,2},{1,3},{2,4},{3,5},{4,6},{5,7},{6,8},{7,9},{8,10},{9,11},{10,... | collective-permute-start | bytes 491528
  1112.8 14.3 collective-permute-start.12
  1116.7 10.0 collective-permute-start.15
  1141.2 341.0 %reduce-scatter.18.cloned.1.call-start = ((), (), s32[]{:S(2)}) async-start(), calls=%async_computation.7 | async-start | bytes 10649600 | tf_op jit(solution)/shard_map/reduce_scatter | solution.py:330
  1191.8 178.0 %collective-permute-start.10 = (bf16[16,960]{1,0:T(8,128)(2,1)}, bf16[16,960]{1,0:T(8,128)(2,1)}, u32[]{:S(2)}, u32[]{:S(2)}) collective-permute-start(bf16[16,960]{1,0:T(8,128)(2,1)} %convert.241), channel_id=1, source_target_pairs={{0,3},{1,4},{2,5},{3,6},{4,7},{5,8},{6,9},{7,10},{8,11},{9,12},{10... | collective-permute-start | bytes 92168
  1198.1 175.7 %collective-permute-start.9 = (bf16[16,960]{1,0:T(8,128)(2,1)}, bf16[16,960]{1,0:T(8,128)(2,1)}, u32[]{:S(2)}, u32[]{:S(2)}) collective-permute-start(bf16[16,960]{1,0:T(8,128)(2,1)} %convert.241), channel_id=1, source_target_pairs={{0,2},{1,3},{2,4},{3,5},{4,6},{5,7},{6,8},{7,9},{8,10},{9,11},{10,... | collective-permute-start | bytes 92168
  1200.1 175.7 %collective-permute-start.8 = (bf16[16,960]{1,0:T(8,128)(2,1)}, bf16[16,960]{1,0:T(8,128)(2,1)}, u32[]{:S(2)}, u32[]{:S(2)}) collective-permute-start(bf16[16,960]{1,0:T(8,128)(2,1)} %convert.241), channel_id=1, source_target_pairs={{0,1},{1,2},{2,3},{3,4},{4,5},{5,6},{6,7},{7,8},{8,9},{9,10},{10,1... | collective-permute-start | bytes 92168
  1203.2 189.4 %collective-permute-start.6 = (bf16[16,1600]{1,0:T(8,128)(2,1)}, bf16[16,1600]{1,0:T(8,128)(2,1)}, u32[]{:S(2)}, u32[]{:S(2)}) collective-permute-start(bf16[16,1600]{1,0:T(8,128)(2,1)} %convert.240), channel_id=1, source_target_pairs={{0,3},{1,4},{2,5},{3,6},{4,7},{5,8},{6,9},{7,10},{8,11},{9,12},{10... | collective-permute-start | bytes 153608
  1208.2 159.7 %collective-permute-start.11 = (bf16[15,960]{1,0:T(8,128)(2,1)}, bf16[15,960]{1,0:T(8,128)(2,1)}, u32[]{:S(2)}, u32[]{:S(2)}) collective-permute-start(bf16[15,960]{1,0:T(8,128)(2,1)} %slice.359), channel_id=1, source_target_pairs={{0,4},{1,5},{2,6},{3,7},{4,8},{5,9},{6,10},{7,11},{8,12},{9,13},{1... | collective-permute-start | bytes 86408
  1367.9 24.7 %collective-permute-start.5 = (bf16[16,1600]{1,0:T(8,128)(2,1)}, bf16[16,1600]{1,0:T(8,128)(2,1)S(1)}, u32[]{:S(2)}, u32[]{:S(2)}) collective-permute-start(bf16[16,1600]{1,0:T(8,128)(2,1)} %convert.240), channel_id=1, source_target_pairs={{0,2},{1,3},{2,4},{3,5},{4,6},{5,7},{6,8},{7,9},{8,10},{9,11},{10,... | collective-permute-start | bytes 153608
  1369.8 22.8 %collective-permute-start.4 = (bf16[16,1600]{1,0:T(8,128)(2,1)}, bf16[16,1600]{1,0:T(8,128)(2,1)S(1)}, u32[]{:S(2)}, u32[]{:S(2)}) collective-permute-start(bf16[16,1600]{1,0:T(8,128)(2,1)} %convert.240), channel_id=1, source_target_pairs={{0,1},{1,2},{2,3},{3,4},{4,5},{5,6},{6,7},{7,8},{8,9},{9,10},{10,1... | collective-permute-start | bytes 153608
  1373.8 18.8 %collective-permute-start.7 = (bf16[15,1600]{1,0:T(8,128)(2,1)S(1)}, bf16[15,1600]{1,0:T(8,128)(2,1)S(1)}, u32[]{:S(2)}, u32[]{:S(2)}) collective-permute-start(bf16[15,1600]{1,0:T(8,128)(2,1)S(1)} %slice.358), channel_id=1, source_target_pairs={{0,4},{1,5},{2,6},{3,7},{4,8},{5,9},{6,10},{7,11},{8,12},{9,13},{1... | collective-permute-start | bytes 144008
  (164 other events, 1049.4 us)
Sparse Core Ops, SparseCore 0:
  9.6 50.7 all-gather.23
  65.1 38.5 all-gather.17
  105.3 41.1 all-gather.25
  148.0 109.8 all-gather.27
  259.4 61.1 all-gather.29
  337.9 36.3 all-gather.19
  403.6 41.1 all-gather.21
  490.0 40.0 reduce-scatter.19
  569.0 38.2 reduce-scatter.21
  644.9 38.1 reduce-scatter.23
  1141.3 37.1 all-gather.31
  1180.8 301.4 reduce-scatter.17
where the time goes:
time: 1530 us; the launch traced here: 1520 us
  blocking collectives  580 us (38%)
  waiting for transfers between devices  403 us (26%)
  local copies, waits for them, and re-layouts  212 us (14%)
  matrix products  177 us (12%)
  other arithmetic  58 us (4%)
  starting transfers between devices  55.5 us (4%)
  between operations  30.6 us (2%)
    unnamed x2, blocking collectives  482 us
    all_gather x1, waiting for transfers between devices, body(): lax.all_gather(gate_up[0], 'fsdp', axis=0, tiled=True)  109 us
    all_gather x3, waiting for transfers between devices, forward_layer(): lax.all_gather(jnp.concatenate([key_rows, value_rows], 1), 'fsdp', axis=0...  82.9 us
    reduce_scatter x1, waiting for transfers between devices, body(): lax.psum_scatter(reordered[3], ('dp', 'fsdp'), scatter_dimension=0, tiled...  70.7 us
    all_gather x1, waiting for transfers between devices, body(): lax.all_gather(down_weight[0], 'fsdp', axis=0, tiled=True)  51.5 us
    unnamed x359, local copies, waits for them, and re-layouts  44.9 us
    unnamed x27, waiting for transfers between devices  43.8 us
    unnamed x15, starting transfers between devices  41.7 us
  transfers between devices with their start and end apart: 28, of which 15 were waited for; matrix products, arithmetic and copies ran while one was open for 17% of the time, Pallas kernels for 0%

commit v1 on v0

v1 whole, which is shorter than its diff:
```python
import functools

import jax
import jax.numpy as jnp
from jax import lax
from jax.experimental import pallas as pl
from jax.experimental.pallas import tpu as pltpu
from jax.sharding import PartitionSpec as P

D = 960
QUERY_HEADS = 15
KEY_VALUE_HEADS = 5
HEAD_WIDTH = 64
FF = 2560
QUERY_WIDTH = QUERY_HEADS * HEAD_WIDTH
KEY_WIDTH = KEY_VALUE_HEADS * HEAD_WIDTH
QKV = QUERY_WIDTH + 2 * KEY_WIDTH
SHARDS = 8
ROWS = D // SHARDS
PADDED = 128
DOWN_COLUMNS = 1024

EPSILON = 1e-05
BASE = 10000.0

MESH = pl.DeviceIdType.MESH
ANY = pl.BlockSpec(memory_space=pl.ANY)

GATE_UP = (PADDED, 2 * FF, "columns")
DOWN = (FF // SHARDS, DOWN_COLUMNS, "columns")
ATTEND_IN = (PADDED, QKV, "rows")
ATTEND_OUT = (PADDED, D, "rows")
SHAPES = (GATE_UP, DOWN, ATTEND_IN, ATTEND_OUT)


def half_shape(shape):
    rows, columns, kind = shape
    return (rows // 2, columns) if kind == "rows" else (rows, columns // 2)


def half_view(shape, core, start, count):
    rows, columns, kind = shape
    if kind == "rows":
        first = pl.multiple_of(core * (rows // 2) + start, 16)
        return (pl.ds(first, count), slice(None))
    first = pl.multiple_of(core * (columns // 2), 128)
    return (pl.ds(pl.multiple_of(start, 16), count), pl.ds(first, columns // 2))


def places():
    dp = lax.axis_index("dp")
    fsdp = lax.axis_index("fsdp")
    return dp // 2, dp % 2, fsdp // 4, fsdp % 4


def peer_ids():
    z, core, x, y = places()
    return {
        "X": {"fsdp": (1 - x) * 4 + y},
        "Yp": {"fsdp": x * 4 + (y + 1) % 4},
        "Ym": {"fsdp": x * 4 + (y + 3) % 4},
        "C": {"dp": z * 2 + 1 - core},
        "Z1": {"dp": ((z + 1) % 4) * 2 + core},
        "Z2": {"dp": ((z + 2) % 4) * 2 + core},
        "Z3": {"dp": ((z + 3) % 4) * 2 + core},
    }


def greet(ids, names):
    barrier = pltpu.get_barrier_semaphore()
    for name in names:
        pl.semaphore_signal(barrier, inc=1, device_id=ids[name], device_id_type=MESH)
    pl.semaphore_wait(barrier, len(names))


GATHER = (
    ("X", 0, 0, "f"),
    ("Yp", 0, 0, "f"),
    ("Ym", 0, 0, "f"),
    ("Ym", 0, 1, 0),
    ("X", 0, 1, 0),
    ("Yp", 0, 3, 1),
    ("X", 0, 3, 0),
    ("Yp", 1, 0, 1),
    ("Ym", 1, 0, 1),
    ("Ym", 1, 1, 0),
    ("Yp", 1, 3, 1),
)
GATHER_NEXT = {1: (5, 6), 2: (3, 4), 0: (7, 8), 4: (9,), 7: (10,)}
GATHER_ORDER = (1, 2, 0, 4, 7, 3, 5, 6, 8, 9, 10)


def seen_by_receiver(peer, column, step):
    if peer == "X":
        return 1 - column, step
    if peer == "Yp":
        return column, (step + 3) % 4
    if peer == "Ym":
        return column, (step + 1) % 4
    return column, step


def part_rows(shape, part):
    rows = half_shape(shape)[0]
    return (0, rows) if part == "f" else (part * (rows // 2), rows // 2)


def gather_kernel(*refs):
    count = len(SHAPES)
    shards, outs = refs[:count], refs[count : 2 * count]
    local_sem, send_sem, recv_sem = refs[2 * count :]
    z, core, x, y = places()
    ids = peer_ids()
    mine = x * 4 + y

    def owner(column, step):
        return ((x + column) % 2) * 4 + (y + step) % 4

    def view(array, column, step, part, which):
        start, rows = part_rows(SHAPES[array], part)
        return outs[array].at[(owner(column, step),) + half_view(SHAPES[array], which, start, rows)]

    def copy(array, edge):
        peer, column, step, part = GATHER[edge % 11]
        if edge < 11:
            target = view(array, column, step, part, core)
            source = target
            if (column, step) == (0, 0):
                start, rows = part_rows(SHAPES[array], part)
                source = shards[array].at[half_view(SHAPES[array], core, start, rows)]
        else:
            peer, (column, step) = "C", seen_by_receiver(peer, column, step)
            source = target = view(array, column, step, part, core)
        return pltpu.make_async_remote_copy(
            src_ref=source,
            dst_ref=target,
            send_sem=send_sem.at[array, edge],
            recv_sem=recv_sem.at[array, edge],
            device_id=ids[peer],
            device_id_type=MESH,
        )

    def wait_for(array, edge):
        peer, column, step, part = GATHER[edge % 11]
        column, step = seen_by_receiver(peer, column, step)
        which = core if edge < 11 else 1 - core
        landed = view(array, column, step, part, which)
        pltpu.make_async_remote_copy(
            src_ref=landed,
            dst_ref=landed,
            send_sem=send_sem.at[array, edge],
            recv_sem=recv_sem.at[array, edge],
            device_id=ids["C"],
            device_id_type=MESH,
        ).wait_recv()

    greet(ids, ("X", "Yp", "Ym", "C"))
    own = [
        pltpu.make_async_copy(shards[array], outs[array].at[mine], local_sem.at[array])
        for array in range(count)
    ]
    for array in range(count):
        for edge in (0, 1, 2):
            copy(array, edge).start()
        own[array].start()
    for array in range(count):
        for edge in GATHER_ORDER:
            wait_for(array, edge)
            for later in GATHER_NEXT.get(edge, ()):
                copy(array, later).start()
            copy(array, 11 + edge).start()
    for array in range(count):
        for edge in range(11):
            wait_for(array, 11 + edge)
        for edge in range(22):
            copy(array, edge).wait_send()
        own[array].wait()


def gather_weights(shards):
    count = len(SHAPES)
    return pl.pallas_call(
        gather_kernel,
        name="gather_weights",
        out_shape=[
            jax.ShapeDtypeStruct((SHARDS, rows, columns), jnp.bfloat16)
            for rows, columns, _ in SHAPES
        ],
        in_specs=[ANY] * count,
        out_specs=[ANY] * count,
        scratch_shapes=[
            pltpu.SemaphoreType.DMA((count,)),
            pltpu.SemaphoreType.DMA((count, 22)),
            pltpu.SemaphoreType.DMA((count, 22)),
        ],
        compiler_params=pltpu.CompilerParams(collective_id=0, has_side_effects=True),
    )(*shards)


REDUCE = (
    ("Yp", 0, 2, 0, ()),
    ("Ym", 0, 2, 1, ()),
    ("Yp", 1, 2, 0, ()),
    ("Ym", 1, 2, 1, ()),
    ("X", 1, 3, 0, ()),
    ("Yp", 1, 1, 1, ()),
    ("X", 1, 1, 0, (2,)),
    ("Ym", 1, 3, 1, (3,)),
    ("Yp", 0, 1, "f", (0, 6)),
    ("Ym", 0, 3, "f", (1, 4)),
    ("X", 1, 0, "f", (5, 7)),
)
REDUCE_STAGES = ((0, 1, 2, 3, 4, 5), (6, 7), (8, 9, 10))


def reduce_kernel(*refs):
    count = len(SHAPES)
    terms, outs = refs[:count], refs[count : 2 * count]
    scratch = refs[2 * count :]
    totals = scratch[:count]
    wholes = scratch[count : 2 * count]
    parts = scratch[2 * count : 3 * count]
    quarters = scratch[3 * count : 4 * count]
    local_sem, send_sem, recv_sem = scratch[4 * count :]
    z, core, x, y = places()
    ids = peer_ids()
    mine = x * 4 + y

    def owner(column, step):
        return ((x + column) % 2) * 4 + (y + step) % 4

    def piece(array, edge):
        _, column, step, part, _ = REDUCE[edge]
        start, rows = part_rows(SHAPES[array], part)
        return totals[array].at[owner(column, step), pl.ds(start, rows), :]

    def slot(array, edge):
        return parts[array].at[edge] if edge < 8 else wholes[array].at[edge - 8]

    def add(array, into, start, rows, source):
        @pl.loop(0, rows // 16)
        def _(index):
            offset = pl.multiple_of(index * 16, 16)
            at = pl.ds(pl.multiple_of(start + offset, 16), 16)
            totals[array][into, at, :] = (
                totals[array][into, at, :].astype(jnp.float32)
                + source[pl.ds(offset, 16), :].astype(jnp.float32)
            ).astype(jnp.bfloat16)

    def quarter(array, index):
        rows = half_shape(SHAPES[array])[0] // 4
        return pl.multiple_of(index * rows, 16), rows

    def out_view(array, index, which):
        start, rows = quarter(array, index)
        return outs[array].at[half_view(SHAPES[array], which, start, rows)]

    def copy(array, edge):
        if edge < 11:
            peer, source, target = REDUCE[edge][0], piece(array, edge), slot(array, edge)
        elif edge < 14:
            step = edge - 10
            peer = f"Z{step}"
            start, rows = quarter(array, (z + step) % 4)
            source = totals[array].at[mine, pl.ds(start, rows), :]
            target = quarters[array].at[step - 1]
        elif edge < 17:
            peer = f"Z{edge - 13}"
            start, rows = quarter(array, z)
            source = totals[array].at[mine, pl.ds(start, rows), :]
            target = out_view(array, z, core)
        else:
            peer = "C"
            at = (z + edge - 17) % 4
            source = target = out_view(array, at, core)
            if edge == 17:
                start, rows = quarter(array, z)
                source = totals[array].at[mine, pl.ds(start, rows), :]
        return pltpu.make_async_remote_copy(
            src_ref=source,
            dst_ref=target,
            send_sem=send_sem.at[array, edge],
            recv_sem=recv_sem.at[array, edge],
            device_id=ids[peer],
            device_id_type=MESH,
        )

    def wait_for(array, edge):
        if edge < 11:
            landed = slot(array, edge)
        elif edge < 14:
            landed = quarters[array].at[edge - 11]
        elif edge < 17:
            landed = out_view(array, (z + 4 - (edge - 13)) % 4, core)
        else:
            landed = out_view(array, (z + edge - 17) % 4, 1 - core)
        pltpu.make_async_remote_copy(
            src_ref=landed,
            dst_ref=landed,
            send_sem=send_sem.at[array, edge],
            recv_sem=recv_sem.at[array, edge],
            device_id=ids["C"],
            device_id_type=MESH,
        ).wait_recv()

    def receive(array, edge):
        wait_for(array, edge)
        peer, column, step, part, _ = REDUCE[edge]
        column, step = seen_by_receiver(peer, column, step)
        start, rows = part_rows(SHAPES[array], part)
        add(array, owner(column, step), start, rows, slot(array, edge))

    loads = [
        pltpu.make_async_copy(terms[array], totals[array], local_sem.at[array])
        for array in range(count)
    ]
    for load in loads:
        load.start()
    greet(ids, ("X", "Yp", "Ym", "C", "Z1", "Z2", "Z3"))
    for stage in REDUCE_STAGES:
        for array in range(count):
            if stage == REDUCE_STAGES[0]:
                loads[array].wait()
            for edge in stage:
                for earlier in REDUCE[edge][4]:
                    receive(array, earlier)
                copy(array, edge).start()
    for array in range(count):
        for edge in (8, 9, 10):
            receive(array, edge)
        for edge in (11, 12, 13):
            copy(array, edge).start()
    stores = []
    for array in range(count):
        start, rows = quarter(array, z)
        for edge in (11, 12, 13):
            wait_for(array, edge)
            add(array, mine, start, rows, quarters[array].at[edge - 11])
        for edge in (14, 15, 16, 17):
            copy(array, edge).start()
        store = pltpu.make_async_copy(
            totals[array].at[mine, pl.ds(start, rows), :],
            out_view(array, z, core),
            local_sem.at[array],
        )
        store.start()
        stores.append(store)
    for array in range(count):
        for edge in (14, 15, 16):
            wait_for(array, edge)
            copy(array, 17 + (17 - edge)).start()
    for array in range(count):
        for edge in range(17, 21):
            wait_for(array, edge)
        for edge in range(21):
            copy(array, edge).wait_send()
        stores[array].wait()


def reduce_gradients(terms):
    count = len(SHAPES)
    halves = [half_shape(shape) for shape in SHAPES]
    return pl.pallas_call(
        reduce_kernel,
        name="reduce_gradients",
        out_shape=[
            jax.ShapeDtypeStruct((rows, columns), jnp.bfloat16) for rows, columns, _ in SHAPES
        ],
        in_specs=[ANY] * count,
        out_specs=[ANY] * count,
        scratch_shapes=[pltpu.VMEM((SHARDS,) + half, jnp.bfloat16) for half in halves]
        + [pltpu.VMEM((3,) + half, jnp.bfloat16) for half in halves]
        + [pltpu.VMEM((8, half[0] // 2, half[1]), jnp.bfloat16) for half in halves]
        + [pltpu.VMEM((3, half[0] // 4, half[1]), jnp.bfloat16) for half in halves]
        + [
            pltpu.SemaphoreType.DMA((count,)),
            pltpu.SemaphoreType.DMA((count, 21)),
            pltpu.SemaphoreType.DMA((count, 21)),
        ],
        compiler_params=pltpu.CompilerParams(
            collective_id=1, has_side_effects=True, vmem_limit_bytes=48 * 2**20
        ),
    )(*terms)


def rotary_tables(positions):
    half = HEAD_WIDTH // 2
    frequency = BASE ** (-(jnp.arange(half).astype(jnp.float32) * (2.0 / HEAD_WIDTH)))
    angle = positions.astype(jnp.float32)[..., None] * frequency
    cosine_table = jnp.cos(angle)
    sine_table = jnp.sin(angle)
    return (
        jnp.concatenate([cosine_table, cosine_table], -1)[..., None, :],
        jnp.concatenate([sine_table, sine_table], -1)[..., None, :],
    )


def apply_rotation(values, cosine_table, sine_table):
    half = values.shape[-1] // 2
    turned = jnp.concatenate([-values[..., half:], values[..., :half]], -1)
    return values * cosine_table + turned * sine_table


def reverse_rotation(values, cosine_table, sine_table):
    half = values.shape[-1] // 2
    shifted = values * sine_table
    turned = jnp.concatenate([-shifted[..., half:], shifted[..., :half]], -1)
    return values * cosine_table - turned


def normed(values, gain):
    return values * lax.rsqrt(jnp.mean(values * values, -1, keepdims=True) + EPSILON) * gain


def norm_backward(values, gain, upstream):
    row_scale = lax.rsqrt(jnp.mean(values * values, -1, keepdims=True) + EPSILON)
    unit = values * row_scale
    gain_slope = jnp.sum(upstream * unit, 0)
    inner = upstream * gain
    return (row_scale * (inner - unit * jnp.mean(inner * unit, -1, keepdims=True)), gain_slope)


def pad_shards(values):
    split = values.reshape(values.shape[0], SHARDS, ROWS)
    return jnp.pad(split, ((0, 0), (0, 0), (0, PADDED - ROWS))).reshape(values.shape[0], -1)


def unpad_shards(values):
    split = values.reshape(values.shape[0], SHARDS, PADDED)
    return split[:, :, :ROWS].reshape(values.shape[0], D)


def heads(values):
    return values.reshape(values.shape[:-1] + (-1, HEAD_WIDTH))


def masked_scores(query_matrix, key_value_pair, shard_index):
    batches, local_count = query_matrix.shape[:2]
    token_length = key_value_pair.shape[1]
    grouped_heads = query_matrix.reshape(
        batches, local_count, KEY_VALUE_HEADS, QUERY_HEADS // KEY_VALUE_HEADS, HEAD_WIDTH
    )
    key_rows = heads(key_value_pair[..., :KEY_WIDTH])
    scores = jnp.einsum(
        "btgqd,bsgd->bgqts", grouped_heads, key_rows, preferred_element_type=jnp.float32
    ) * HEAD_WIDTH ** (-0.5)
    query_rows = shard_index * local_count + jnp.arange(local_count)
    causal = query_rows[:, None] >= jnp.arange(token_length)[None, :]
    return jnp.where(causal, scores, -1e30)


def forward_layer(layer_in, tables, weights, shard_index):
    attend_in, attend_out, gate_up, down_weight, gains = weights
    batches, local_count = layer_in.shape[:2]
    rows = batches * local_count
    values = layer_in.reshape(rows, D).astype(jnp.float32)
    first_norm = pad_shards(normed(values, gains[0]).astype(jnp.bfloat16))
    projected = jnp.dot(first_norm, attend_in, preferred_element_type=jnp.float32)
    projected = projected.reshape(batches, local_count, QKV)
    rotated = apply_rotation(heads(projected[..., : QUERY_WIDTH + KEY_WIDTH]), *tables)
    rotated = rotated.astype(jnp.bfloat16).reshape(batches, local_count, -1)
    query_matrix = rotated[..., :QUERY_WIDTH]
    own_pair = jnp.concatenate(
        [rotated[..., QUERY_WIDTH:], projected[..., QUERY_WIDTH + KEY_WIDTH :].astype(jnp.bfloat16)],
        -1,
    )
    key_value_pair = lax.all_gather(own_pair, "fsdp", axis=1, tiled=True)
    scores = masked_scores(query_matrix, key_value_pair, shard_index)
    highest = jnp.max(scores, -1)
    totals = highest + jnp.log(jnp.sum(jnp.exp(scores - highest[..., None]), -1))
    probs = jnp.exp(scores - totals[..., None]).astype(jnp.bfloat16)
    mixed = jnp.einsum(
        "bgqts,bsgd->btgqd",
        probs,
        heads(key_value_pair[..., KEY_WIDTH:]),
        preferred_element_type=jnp.float32,
    )
    mixed = pad_shards(mixed.astype(jnp.bfloat16).reshape(rows, QUERY_WIDTH))
    hidden = values + jnp.dot(mixed, attend_out, preferred_element_type=jnp.float32)
    second_norm = pad_shards(normed(hidden, gains[1]).astype(jnp.bfloat16))
    gated = jnp.dot(second_norm, gate_up, preferred_element_type=jnp.float32)
    act = (jax.nn.silu(gated[:, :FF]) * gated[:, FF:]).astype(jnp.bfloat16)
    result = hidden + jnp.dot(act, down_weight, preferred_element_type=jnp.float32)[:, :D]
    kept = (
        values,
        first_norm,
        query_matrix,
        key_value_pair,
        totals,
        mixed,
        hidden,
        second_norm,
        gated,
        act,
    )
    return (result.astype(jnp.bfloat16).reshape(layer_in.shape), kept)


def backward_layer(upstream, kept, tables, weights, shard_index):
    attend_in, attend_out, gate_up, down_weight, gains = weights
    (
        values,
        first_norm,
        query_matrix,
        key_value_pair,
        totals,
        mixed,
        hidden,
        second_norm,
        gated,
        act,
    ) = kept
    batches, local_count = upstream.shape[:2]
    rows = batches * local_count
    token_length = key_value_pair.shape[1]
    scale = HEAD_WIDTH ** (-0.5)
    upstream = upstream.reshape(rows, D)
    down_in = jnp.pad(upstream, ((0, 0), (0, DOWN_COLUMNS - D)))
    upstream = upstream.astype(jnp.float32)
    act_slope = jnp.einsum("td,fd->tf", down_in, down_weight, preferred_element_type=jnp.float32)
    gate_part = gated[:, :FF]
    up_part = gated[:, FF:]
    sigma = jax.nn.sigmoid(gate_part)
    gate_slope = act_slope * up_part * sigma * (1.0 + gate_part * (1.0 - sigma))
    up_slope = act_slope * gate_part * sigma
    gated_slope = jnp.concatenate([gate_slope, up_slope], 1).astype(jnp.bfloat16)
    second_slope = unpad_shards(
        jnp.einsum("tf,df->td", gated_slope, gate_up, preferred_element_type=jnp.float32)
    )
    hidden_part, second_gain = norm_backward(hidden, gains[1], second_slope)
    hidden_slope = upstream + hidden_part
    branch_slope = hidden_slope.astype(jnp.bfloat16)
    mixed_gradient = unpad_shards(
        jnp.einsum(
            "td,qd->tq", branch_slope, attend_out, preferred_element_type=jnp.float32
        ).astype(jnp.bfloat16)
    )
    mixed_gradient = mixed_gradient.reshape(
        batches, local_count, KEY_VALUE_HEADS, QUERY_HEADS // KEY_VALUE_HEADS, HEAD_WIDTH
    )
    scores = masked_scores(query_matrix, key_value_pair, shard_index)
    probs = jnp.exp(scores - totals[..., None])
    probs_low = probs.astype(jnp.bfloat16)
    complete_keys = heads(key_value_pair[..., :KEY_WIDTH])
    complete_values = heads(key_value_pair[..., KEY_WIDTH:])
    prob_slope = jnp.einsum(
        "btgqd,bsgd->bgqts", mixed_gradient, complete_values, preferred_element_type=jnp.float32
    )
    score_slope = probs * (prob_slope - jnp.sum(probs * prob_slope, -1, keepdims=True))
    score_slope = score_slope.astype(jnp.bfloat16)
    query_slope = (
        jnp.einsum(
            "bgqts,bsgd->btgqd", score_slope, complete_keys, preferred_element_type=jnp.float32
        )
        * scale
    )
    grouped_heads = query_matrix.reshape(mixed_gradient.shape)
    key_part = (
        jnp.einsum(
            "bgqts,btgqd->bsgd", score_slope, grouped_heads, preferred_element_type=jnp.float32
        )
        * scale
    )
    val_part = jnp.einsum(
        "bgqts,btgqd->bsgd", probs_low, mixed_gradient, preferred_element_type=jnp.float32
    )
    owned_part = lax.psum_scatter(
        jnp.concatenate(
            [
                key_part.reshape(batches, token_length, KEY_WIDTH),
                val_part.reshape(batches, token_length, KEY_WIDTH),
            ],
            -1,
        ).astype(jnp.bfloat16),
        "fsdp",
        scatter_dimension=1,
        tiled=True,
    ).astype(jnp.float32)
    query_raw = reverse_rotation(
        query_slope.reshape(batches, local_count, QUERY_HEADS, HEAD_WIDTH), *tables
    ).reshape(rows, QUERY_WIDTH)
    unrotated_key = reverse_rotation(heads(owned_part[..., :KEY_WIDTH]), *tables)
    projected_slope = jnp.concatenate(
        [
            query_raw,
            unrotated_key.reshape(rows, KEY_WIDTH),
            owned_part[..., KEY_WIDTH:].reshape(rows, KEY_WIDTH),
        ],
        1,
    ).astype(jnp.bfloat16)
    first_slope = unpad_shards(
        jnp.einsum("tf,df->td", projected_slope, attend_in, preferred_element_type=jnp.float32)
    )
    input_part, first_gain = norm_backward(values, gains[0], first_slope)
    input_slope = hidden_slope + input_part
    slopes = (projected_slope, branch_slope, gated_slope, down_in)
    return (
        input_slope.reshape(batches, local_count, D),
        slopes,
        jnp.stack([first_gain, second_gain]),
    )


def passed_along(value, steps):
    return lax.ppermute(value, "section", [(0, 1)] if steps > 0 else [(1, 0)])


def with_other_core(value):
    size = lax.axis_size("dp")
    other = lax.ppermute(value, "dp", [(index, index ^ 1) for index in range(size)])
    return other


def weight_terms(kept, slopes, gain_slopes):
    core = lax.axis_index("dp") % 2
    first_norm, mixed, second_norm, act = (kept[1], kept[5], kept[7], kept[9])
    projected_slope, branch_slope, gated_slope, down_in = slopes
    tokens = act.shape[0]

    def halved(values, axis):
        extent = values.shape[axis] // 2
        keep = lax.dynamic_slice_in_dim(values, core * extent, extent, axis)
        send = lax.dynamic_slice_in_dim(values, (1 - core) * extent, extent, axis)
        return jnp.concatenate([keep, with_other_core(send)], 0)

    def whole(values):
        return jnp.concatenate([values, with_other_core(values)], 0)

    def term(left, right):
        split = left.reshape(2 * tokens, SHARDS, -1)
        return jnp.einsum(
            "tkr,tn->krn", split, right, preferred_element_type=jnp.float32
        ).astype(jnp.bfloat16)

    in_rows = halved(first_norm.reshape(tokens, SHARDS, PADDED), 2)
    out_rows = halved(mixed.reshape(tokens, SHARDS, PADDED), 2)
    in_term = term(in_rows, whole(projected_slope))
    gains = (gain_slopes + with_other_core(gain_slopes)).reshape(2, SHARDS, ROWS).swapaxes(0, 1)
    spare = PADDED // 2 - (PADDED - ROWS)
    in_term = in_term.at[:, spare : spare + 2, :ROWS].add(
        jnp.where(core == 1, gains, 0.0).astype(jnp.bfloat16)
    )
    return (
        term(whole(second_norm), halved(gated_slope, 1)),
        term(whole(act), halved(down_in, 1)),
        in_term,
        term(out_rows, whole(branch_slope)),
    )


def body(
    inputs, positions, plan, attend_in, attend_out, gate_up, down_weight, norm_gains, cotangent
):
    section_index = lax.axis_index("section")
    shard_index = lax.axis_index("fsdp")
    extra = PADDED - ROWS
    in_shard = jnp.concatenate(
        [
            attend_in[0],
            jnp.pad(norm_gains[0], ((0, extra - 2), (0, QKV - ROWS))),
        ],
        0,
    )
    gathered = gather_weights(
        (
            jnp.pad(gate_up[0], ((0, extra), (0, 0))),
            jnp.pad(down_weight[0], ((0, 0), (0, DOWN_COLUMNS - D))),
            in_shard,
            jnp.pad(attend_out[0], ((0, extra), (0, 0))),
        )
    )
    gains = gathered[2][:, ROWS : ROWS + 2, :ROWS].swapaxes(0, 1).reshape(2, D)
    weights = (
        gathered[2].reshape(-1, QKV),
        gathered[3].reshape(-1, D),
        gathered[0].reshape(-1, 2 * FF),
        gathered[1].reshape(-1, DOWN_COLUMNS),
        gains.astype(jnp.float32),
    )
    plan_row = plan[0]
    fresh = jnp.take(inputs[:, 0], plan_row, axis=0)
    tables = rotary_tables(jnp.take(positions[:, 0], plan_row, axis=0))
    given = cotangent[:, 0]
    result, _ = forward_layer(fresh, tables, weights, shard_index)
    layer_in = jnp.where(section_index == 0, fresh, passed_along(result, 1))
    outputs, kept = forward_layer(layer_in, tables, weights, shard_index)
    input_slope, _, _ = backward_layer(given, kept, tables, weights, shard_index)
    back = passed_along(input_slope.astype(jnp.bfloat16), -1)
    upstream = jnp.where(section_index == 1, given, back)
    input_slope, slopes, gain_slopes = backward_layer(upstream, kept, tables, weights, shard_index)
    reported = jnp.where(
        section_index == 0, input_slope, input_slope.astype(jnp.bfloat16).astype(jnp.float32)
    )
    input_slopes = jnp.take(reported, plan_row, axis=0)
    summed = reduce_gradients(weight_terms(kept, slopes, gain_slopes))
    full = [value.astype(jnp.float32) for value in summed]
    return (
        outputs[None, :, None],
        input_slopes[None, :, None],
        full[2][None, :ROWS],
        full[3][None, :ROWS],
        full[0][None, :ROWS],
        full[1][None, :, :D],
        full[2][None, ROWS : ROWS + 2, :ROWS],
    )


def solution(mesh):
    in_specs = (
        P(None, "dp", "fsdp", None),
        P(None, "dp", "fsdp"),
        P("dp", None),
        P("section", "fsdp", None),
        P("section", "fsdp", None),
        P("section", "fsdp", None),
        P("section", "fsdp", None),
        P("section", None, "fsdp"),
        P(None, "dp", "fsdp", None),
    )
    out_specs = (
        P("section", None, "dp", "fsdp", None),
        P("section", None, "dp", "fsdp", None),
        P("section", "fsdp", None),
        P("section", "fsdp", None),
        P("section", "fsdp", None),
        P("section", "fsdp", None),
        P("section", None, "fsdp"),
    )
    return jax.shard_map(body, mesh=mesh, in_specs=in_specs, out_specs=out_specs, check_vma=False)
```

time: 1530 us -> 710 us (0.46)
  blocking collectives: 580 us -> 0 us
  waiting for transfers between devices: 403 us -> 145 us
  Pallas kernels: 0 us -> 193 us
  local copies, waits for them, and re-layouts: 212 us -> 94.6 us
  starting transfers between devices: 55.5 us -> 15 us
  other arithmetic: 58 us -> 79.4 us
  matrix products: 177 us -> 160 us
    unnamed x2 -> x0, blocking collectives: 482 us -> none
    pallas_call x0 -> x2, Pallas kernels: none -> 193 us  [the longest x1 100 us: reduce_gradients(): pl.pallas_call(reduce_kernel, name='reduce_gradients', out_shape=[jax.Sha...]
    all_gather x8 -> x2, waiting for transfers between devices: 281 us -> 93.2 us  [forward_layer(): key_value_pair = lax.all_gather(own_pair, 'fsdp', axis=1, tiled=True)]
    all_gather x5 -> x0, blocking collectives: 97.9 us -> none  [the longest x1 27.6 us: body(): lax.all_gather(norm_gains[0], 'fsdp', axis=1, tiled=True)]
    reduce_scatter x1 -> x0, waiting for transfers between devices: 70.7 us -> none  [body(): lax.psum_scatter(reordered[3], ('dp', 'fsdp'), scatter_dimension=0, tiled...]
    reshape x7 -> x5, local copies, waits for them, and re-layouts: 54.5 us -> 2.82 us  [the longest x2 2.24 us: unpad_shards(): split = values.reshape(values.shape[0], SHARDS, PADDED)]
    unnamed x15 -> x2, starting transfers between devices: 41.7 us -> 0.08 us
    transpose x5 -> x0, local copies, waits for them, and re-layouts: 37.8 us -> none  [regroup(): jnp.swapaxes(array.reshape(split), axis_dim, axis_dim + 1)]
  transfers between devices with their start and end apart: 28 -> 15, of which waited for: 15 -> 5; matrix products, arithmetic and copies ran while one was open for 17% -> 11% of each run, Pallas kernels for 0% -> 0%
where the time goes in v1:
time: 710 us; the launch traced here: 703 us
  Pallas kernels  193 us (27%)
  matrix products  160 us (23%)
  waiting for transfers between devices  145 us (20%)
  local copies, waits for them, and re-layouts  94.6 us (13%)
  other arithmetic  79.4 us (11%)
  between operations  15.6 us (2%)
  starting transfers between devices  15 us (2%)
    pallas_call x1, Pallas kernels, reduce_gradients(): pl.pallas_call(reduce_kernel, name='reduce_gradients', out_shape=[jax.Sha...  100 us
    pallas_call x1, Pallas kernels, gather_weights(): pl.pallas_call(gather_kernel, name='gather_weights', out_shape=[jax.Shape...  93.4 us
    all_gather x2, waiting for transfers between devices, forward_layer(): key_value_pair = lax.all_gather(own_pair, 'fsdp', axis=1, tiled=True)  93.2 us
    unnamed x157, local copies, waits for them, and re-layouts  39.7 us
    unnamed x6, waiting for transfers between devices  35.8 us
    dot_general x2, matrix products, backward_layer(): jnp.einsum('td,fd->tf', down_in, down_weight, preferred_element_type=jnp....  17.5 us
    reduce_sum x2, other arithmetic, forward_layer(): jnp.sum(jnp.exp(scores - highest[..., None]), -1)  17.5 us
    dot_general x2, matrix products, backward_layer(): jnp.einsum('btgqd,bsgd->bgqts', mixed_gradient, complete_values, preferre...  17.4 us
  transfers between devices with their start and end apart: 15, of which 5 were waited for; matrix products, arithmetic and copies ran while one was open for 11% of the time, Pallas kernels for 0%

profile of v1, /device:TPU:1, one launch (start us, length us, event | category | flops | bytes accessed | tf_op | source)
XLA Modules:
  0.0 703.3 jit_solution(5623709988434434259)
XLA Ops:
  13.9 93.4 %gather_weights.1 = (bf16[8,128,5120]{2,1,0:T(8,128)(2,1)}, bf16[8,320,1024]{2,1,0:T(8,128)(2,1)}, bf16[8,128,1600]{2,1,0:T(8,128)(2,1)}, bf16[8,128,960]{2,1,0:T(8,128)(2,1)}) custom-call(bf16[128,5120]{1,0:T(8,128)(2,1)} %pad.46.refs_0_, bf16[320,1024]{1,0:T(8,128)(2,1)} %pad.47.refs_1_, bf16[128,1600]{1,0:T(8,128)(2,1)} %fusion.116.refs_2_, ...), custom_call_target="tpu_custom_call" | custom-call | tf_op jit(solution)/shard_map/gather_weights/pallas_call | solution.py:182
  119.5 44.1 %all-gather.3.cloned.1.call-done = bf16[2,1024,640]{1,2,0:T(8,128)(2,1)} async-done(((bf16[2,128,640]{1,2,0:T(8,128)(2,1)}), bf16[2,1024,640]{1,2,0:T(8,128)(2,1)}) %all-gather.3.cloned.1.call-update) | async-done | bytes 2621456 | tf_op jit(solution)/shard_map/all_gather | solution.py:467
  165.6 6.8 fusion.6
  172.4 8.7 %exponential_reduce_fusion.1 = f32[2,5,3,128]{3,2,1,0:T(4,128)S(1)} fusion(f32[2,5,1024,128,3]{3,2,4,1,0:T(8,128)} %get-tuple-element.101, f32[2,5,3,128]{3,2,1,0:T(4,128)S(1)} %get-tuple-element.100, pred[128,1024]{0,1:T(8,128)(4,1)S(1)} %iota_compare_fusion.1), kind=kLoop, calls=%fused_computation.18 | loop fusion | flops 15724800 | bytes 15890432 | tf_op jit(solution)/shard_map/reduce_sum | solution.py:470
  181.1 7.4 %fusion.63 = bf16[2,128,5,3,64]{1,4,3,2,0:T(8,128)(2,1)S(1)} fusion(bf16[2,1024,5,64,1]{1,3,4,2,0:T(8,128)(2,1)S(1)} %bitcast.518, f32[2,5,1024,128,3]{3,2,4,1,0:T(8,128)} %get-tuple-element.101, f32[2,5,3,128]{3,2,1,0:T(4,128)S(1)} %log_add_fusion.1, pred[128,1024]{0,1:T(8,128)(4,1)S(1)} %iota_compare_fusion.1), kind=kOutput, calls=%fused_computation.105 | convolution fusion | flops 519290880 | bytes 17677312 | tf_op jit(solution)/shard_map/bgqts,bsgd->btgqd/dot_general | solution.py:472
  197.3 5.9 convolution_bitcast_fusion.1
  208.0 4.8 collective-permute-start
  212.8 5.9 collective-permute-done
  228.8 49.1 %all-gather.5.cloned.1.call-done = bf16[2,1024,640]{1,2,0:T(8,128)(2,1)} async-done(((bf16[2,128,640]{1,2,0:T(8,128)(2,1)}), bf16[2,1024,640]{1,2,0:T(8,128)(2,1)}) %all-gather.5.cloned.1.call-update) | async-done | bytes 2621456 | tf_op jit(solution)/shard_map/all_gather | solution.py:467
  279.9 7.2 %fusion.7 = (f32[2,5,3,128]{3,2,1,0:T(4,128)S(1)}, f32[2,5,1024,128,3]{3,2,4,1,0:T(8,128)}) fusion(pred[128,1024]{0,1:T(8,128)(4,1)S(1)} %iota_compare_fusion.1, bf16[2,1024,5,64,1]{1,3,4,2,0:T(8,128)(2,1)S(1)} %bitcast.471, bf16[2,128,5,3,64]{1,4,3,2,0:T(8,128)(2,1)S(1)} %bitcast.490), kind=kOutput, calls=%fused_computation.20 | convolution fusion | flops 515109120 | bytes 17677312 | tf_op jit(solution)/shard_map/btgqd,bsgd->bgqts/dot_general | solution.py:444
  287.1 8.7 %exponential_reduce_fusion = f32[2,5,3,128]{3,2,1,0:T(4,128)S(1)} fusion(f32[2,5,1024,128,3]{3,2,4,1,0:T(8,128)} %get-tuple-element.105, f32[2,5,3,128]{3,2,1,0:T(4,128)S(1)} %get-tuple-element.104, pred[128,1024]{0,1:T(8,128)(4,1)S(1)} %iota_compare_fusion.1), kind=kLoop, calls=%fused_computation.16 | loop fusion | flops 15724800 | bytes 15890432 | tf_op jit(solution)/shard_map/reduce_sum | solution.py:470
  295.9 7.4 %fusion.92 = bf16[2,5,3,128,1024]{3,4,2,1,0:T(8,128)(2,1)S(1)} fusion(f32[2,5,3,128]{3,2,1,0:T(4,128)S(1)} %log_add_fusion, f32[2,5,1024,128,3]{3,2,4,1,0:T(8,128)} %get-tuple-element.105, pred[128,1024]{0,1:T(8,128)(4,1)S(1)} %iota_compare_fusion.1), kind=kLoop, calls=%fused_computation.167 | loop fusion | flops 15728640 | bytes 23739392 | tf_op jit(solution)/shard_map/convert_element_type | solution.py:471
  310.8 6.0 convolution_bitcast_fusion
  316.8 8.6 %multiply_convert_fusion.3 = (bf16[256,2560]{1,0:T(8,128)(2,1)}, bf16[256,2560]{1,0:T(8,128)(2,1)}) fusion(f32[256,5120]{1,0:T(8,128)S(1)} %convolution_bitcast_fusion, bf16[2560,1024]{1,0:T(8,128)(2,1)} %bitcast.546, bf16[256,960]{0,1:T(8,128)(2,1)S(1)} %bitcast.530), kind=kOutput, calls=%fused_computation.65 | convolution fusion | flops 1350696960 | bytes 13598720 | tf_op jit(solution)/shard_map/td,fd->tf/dot_general | solution.py:520
  339.2 8.3 %fusion.3 = (f32[2,5,3,128]{3,2,1,0:T(4,128)S(1)}, f32[2,5,1024,128,3]{3,2,4,1,0:T(8,128)S(1)}) fusion(f32[2,5,3,128]{3,2,1,0:T(4,128)S(1)} %log_add_fusion, f32[2,5,1024,128,3]{3,2,4,1,0:T(8,128)} %get-tuple-element.105, pred[128,1024]{0,1:T(8,128)(4,1)S(1)} %iota_compare_fusion.1, bf16[2,1024,5,64,1]{1,3,4,2,0:T(8,128)(2,1)} %bitcast.475, ...), kind=kOutput, calls=%fused_computation.10 | convolution fusion | flops 522973440 | bytes 33421312 | tf_op jit(solution)/shard_map/btgqd,bsgd->bgqts/dot_general | solution.py:546
  347.5 6.9 bitcast_convert_fusion.1
  354.4 8.2 %fusion.5 = bf16[2,5,3,128,1024]{3,4,2,1,0:T(8,128)(2,1)S(1)} fusion(f32[2,5,1024,128,3]{3,2,4,1,0:T(8,128)S(1)} %get-tuple-element.109, f32[2,5,3,128]{3,2,1,0:T(4,128)S(1)} %get-tuple-element.108, f32[2,5,3,128]{3,2,1,0:T(4,128)S(1)} %log_add_fusion, f32[2,5,1024,128,3]{3,2,4,1,0:T(8,128)} %get-tuple-element.105, pred[128,1024]{0,1:T(8,128)(4,1)S(1)} %iota_compare_fusion.1), kind=kLoop, calls=%fused_computation.12 | loop fusion | flops 23592960 | bytes 39483392 | tf_op jit(solution)/shard_map/convert_element_type | solution.py:550
  368.5 7.5 %copy.210 = bf16[2,1024,640]{2,0,1:T(2,128)(2,1)} copy(bf16[2,1024,640]{1,2,0:T(8,128)(2,1)} %pad_maximum_fusion.1) | data formatting | bytes 5242880
  380.6 5.0 convolution_multiply_fusion.1
  389.8 35.7 %reduce-scatter.7.cloned.1.call-done = bf16[128,1280]{1,0:T(8,128)(2,1)} async-done(((bf16[1024,1280]{1,0:T(8,128)(2,1)}), bf16[128,1280]{1,0:T(8,128)(2,1)}) %reduce-scatter.7.cloned.1.call-update) | async-done | bytes 327696
  440.8 9.8 %collective-permute-done.1 = bf16[2,128,960]{1,2,0:T(8,128)(2,1)S(1)} collective-permute-done((bf16[2,128,960]{1,2,0:T(8,128)(2,1)S(1)}, bf16[2,128,960]{1,2,0:T(8,128)(2,1)S(1)}, u32[]{:S(2)}, u32[]{:S(2)}) %collective-permute-start.1) | collective-permute-done | bytes 491552 | tf_op jit(solution)/shard_map/ppermute | solution.py:605
  450.7 8.9 %multiply_convert_fusion.1 = (bf16[256,2560]{1,0:T(8,128)(2,1)S(1)}, bf16[256,2560]{1,0:T(8,128)(2,1)S(1)}, bf16[256,2560]{1,0:T(8,128)(2,1)}) fusion(f32[256,5120]{1,0:T(8,128)} %copy-done.19, bf16[2560,1024]{1,0:T(8,128)(2,1)} %bitcast.547, bf16[256,960]{0,1:T(8,128)(2,1)S(1)} %copy_bitcast_fusion.1), kind=kOutput, calls=%fused_computation.63 | convolution fusion | flops 1352663040 | bytes 14909440 | tf_op jit(solution)/shard_map/td,fd->tf/dot_general | solution.py:520
  459.7 7.5 %fusion.8 = f32[256,8,120]{0,2,1:T(8,128)S(1)} fusion(bf16[8,128,5120]{2,1,0:T(8,128)(2,1)} %get-tuple-element.29, bf16[256,2560]{1,0:T(8,128)(2,1)S(1)} %get-tuple-element.65, bf16[256,2560]{1,0:T(8,128)(2,1)S(1)} %get-tuple-element.64), kind=kOutput, calls=%fused_computation.21 | convolution fusion | flops 2521825280 | bytes 13434880 | tf_op jit(solution)/shard_map/tf,df->td/dot_general | solution.py:528
  471.0 9.1 %fusion = (f32[2,5,3,128]{3,2,1,0:T(4,128)S(1)}, f32[2,5,1024,128,3]{3,2,4,1,0:T(8,128)S(1)}) fusion(f32[2,5,3,128]{3,2,1,0:T(4,128)S(1)} %log_add_fusion, f32[2,5,1024,128,3]{3,2,4,1,0:T(8,128)} %get-tuple-element.105, pred[128,1024]{0,1:T(8,128)(4,1)S(1)} %iota_compare_fusion.1, bf16[2,1024,5,64,1]{1,3,4,2,0:T(8,128)(2,1)} %bitcast.476, ...), kind=kOutput, calls=%fused_computation.5 | convolution fusion | flops 522973440 | bytes 33421312 | tf_op jit(solution)/shard_map/btgqd,bsgd->bgqts/dot_general | solution.py:546
  480.0 6.9 bitcast_convert_fusion
  486.9 8.0 %fusion.2 = bf16[2,5,3,128,1024]{3,4,2,1,0:T(8,128)(2,1)S(1)} fusion(f32[2,5,1024,128,3]{3,2,4,1,0:T(8,128)S(1)} %get-tuple-element.113, f32[2,5,3,128]{3,2,1,0:T(4,128)S(1)} %get-tuple-element.112, f32[2,5,3,128]{3,2,1,0:T(4,128)S(1)} %log_add_fusion, f32[2,5,1024,128,3]{3,2,4,1,0:T(8,128)} %get-tuple-element.105, pred[128,1024]{0,1:T(8,128)(4,1)S(1)} %iota_compare_fusion.1), kind=kLoop, calls=%fused_computation.7 | loop fusion | flops 23592960 | bytes 39483392 | tf_op jit(solution)/shard_map/convert_element_type | solution.py:550
  499.9 7.6 %copy.212 = bf16[2,1024,640]{2,0,1:T(2,128)(2,1)} copy(bf16[2,1024,640]{1,2,0:T(8,128)(2,1)} %pad_maximum_fusion.2) | data formatting | bytes 5242880
  515.3 6.5 collective-permute-start.2
  526.1 5.2 convolution_multiply_fusion
  556.4 7.5 %convolution_convert_fusion.refs_0_ = bf16[8,128,2560]{2,1,0:T(8,128)(2,1)} fusion(bf16[256,2560]{1,0:T(8,128)(2,1)} %collective-permute-done.3, bf16[256,2560]{1,0:T(8,128)(2,1)} %get-tuple-element.69, bf16[256,8,128]{2,0,1:T(8,128)(2,1)} %copy.171, bf16[256,8,128]{2,0,1:T(8,128)(2,1)} %pad.55), kind=kOutput, calls=%fused_computation.29 | convolution fusion | flops 2694316032 | bytes 8912896 | tf_op jit(solution)/shard_map/tkr,tn->krn/dot_general | solution.py:631
  576.2 5.1 multiply_reduce_fusion.1
  591.1 100.1 %reduce_gradients.1 = (bf16[128,5120]{1,0:T(8,128)(2,1)S(1)}, bf16[320,1024]{1,0:T(8,128)(2,1)S(1)}, bf16[128,1600]{1,0:T(8,128)(2,1)S(1)}, bf16[128,960]{1,0:T(8,128)(2,1)S(1)}) custom-call(bf16[8,128,2560]{2,1,0:T(8,128)(2,1)} %convolution_convert_fusion.refs_0_, bf16[8,320,512]{2,1,0:T(8,128)(2,1)} %convolution_convert_fusion.2.refs_1_, ...), custom_call_target="tpu_custom_call" | custom-call | tf_op jit(solution)/shard_map/reduce_gradients/pallas_call | solution.py:363
  (344 shorter events, 170.0 us)
Async XLA Ops:
  7.2 156.4 %all-gather.3.cloned.1.call-start = ((), (), s32[]{:S(2)}) async-start(), calls=%async_computation.2 | async-start | bytes 2949120 | tf_op jit(solution)/shard_map/all_gather | solution.py:467
  8.7 210.1 %copy-start.63 = (pred[2]{0:T(512)(128)(4,1)}, pred[2]{0:T(512)(128)(4,1)S(1)}, u32[]{:S(2)}) copy-start(pred[2]{0:T(512)(128)(4,1)S(1)} %compare_and_fusion) | copy-start | bytes 10
  8.7 106.3 %copy-start.65 = (s32[1024]{0:T(1024)}, s32[1024]{0:T(1024)S(1)}, u32[]{:S(2)}) copy-start(s32[1024]{0:T(1024)S(1)} %pad_clamp_fusion) | copy-start | bytes 12292
  115.9 269.7 %copy-start.37 = (f32[2,128,64]{1,2,0:T(8,128)}, f32[2,128,64]{1,2,0:T(8,128)S(1)}, u32[]{:S(2)}) copy-start(f32[2,128,64]{1,2,0:T(8,128)S(1)} %get-tuple-element.116) | copy-start | bytes 196612
  119.1 158.8 %all-gather.5.cloned.1.call-start = ((), (), s32[]{:S(2)}) async-start(), calls=%async_computation.3 | async-start | bytes 2949120 | tf_op jit(solution)/shard_map/all_gather | solution.py:467
  119.5 46.1 %slice-start.3 = ((bf16[2,128,1280]{1,2,0:T(8,128)(2,1)}), bf16[2,128,960]{1,2,0:T(8,128)(2,1)S(1)}, s32[]{:S(2)}) async-start(bf16[2,128,1280]{1,2,0:T(8,128)(2,1)} %copy-done.35), calls=%async_computation.9 | async-start | bytes 983040 | tf_op jit(solution)/shard_map/slice | solution.py:462
  208.0 10.8 %collective-permute-start = (bf16[2,128,960]{1,2,0:T(8,128)(2,1)S(1)}, bf16[2,128,960]{1,2,0:T(8,128)(2,1)S(1)}, u32[]{:S(2)}, u32[]{:S(2)}) collective-permute-start(bf16[2,128,960]{1,2,0:T(8,128)(2,1)S(1)} %bitcast.531), channel_id=1, source_target_pairs={{0,64},{1,65},{2,66},{3,67},{4,68},{5,69},{6,70},{7,71},{8,72},{9,... | collective-permute-start | bytes 1474568 | tf_op jit(solution)/shard_map/ppermute | solution.py:605
  219.1 220.1 %copy-start.7 = (bf16[2,128,960]{1,2,0:T(8,128)(2,1)}, bf16[2,128,960]{1,2,0:T(8,128)(2,1)S(1)}, u32[]{:S(2)}) copy-start(bf16[2,128,960]{1,2,0:T(8,128)(2,1)S(1)} %get-tuple-element.63) | copy-start | bytes 1474564
  226.5 199.0 %reduce-scatter.7.cloned.1.call-start = ((), (), s32[]{:S(2)}) async-start(), calls=%async_computation.4 | async-start | bytes 2949120
  228.8 51.1 %copy-start.15 = (bf16[2,128,960]{1,2,0:T(8,128)(2,1)}, bf16[2,128,960]{1,2,0:T(8,128)(2,1)S(1)}, u32[]{:S(2)}) copy-start(bf16[2,128,960]{1,2,0:T(8,128)(2,1)S(1)} %slice.288) | copy-start | bytes 1474564
  279.9 23.4 %copy-start.6 = (bf16[2,1024,320]{1,2,0:T(8,128)(2,1)}, bf16[2,1024,320]{1,2,0:T(8,128)(2,1)S(1)}, u32[]{:S(2)}) copy-start(bf16[2,1024,320]{1,2,0:T(8,128)(2,1)S(1)} %get-tuple-element.72) | copy-start | bytes 3932164
  310.7 14.6 %slice-start = ((s8[10485760]{0:T(1024)(128)(4,1)}), s8[4194304]{0:T(1024)(128)(4,1)S(1)}, s32[]{:S(2)}) async-start(s8[10485760]{0:T(1024)(128)(4,1)} %bitcast.469), calls=%async_computation.6 | async-start | bytes 8388608
  310.7 14.6 %slice-start.1 = ((s8[10485760]{0:T(1024)(128)(4,1)}), s8[4194304]{0:T(1024)(128)(4,1)S(1)}, s32[]{:S(2)}) async-start(s8[10485760]{0:T(1024)(128)(4,1)} %bitcast.469), calls=%async_computation.7 | async-start | bytes 8388608
  316.7 8.6 %copy-start.19 = (f32[256,5120]{1,0:T(8,128)}, f32[256,5120]{1,0:T(8,128)S(1)}, u32[]{:S(2)}) copy-start(f32[256,5120]{1,0:T(8,128)S(1)} %convolution_bitcast_fusion) | copy-start | bytes 15728644
  316.8 8.6 %slice-start.2 = ((s8[10485760]{0:T(1024)(128)(4,1)}), s8[2097152]{0:T(1024)(128)(4,1)S(1)}, s32[]{:S(2)}) async-start(s8[10485760]{0:T(1024)(128)(4,1)} %bitcast.469), calls=%async_computation.8 | async-start | bytes 4194304
  339.2 8.3 %copy-start.24 = (bf16[2,128,5,3,64]{1,0,4,3,2:T(2,128)(2,1)S(1)}, bf16[2,128,5,3,64]{1,0,4,3,2:T(2,128)(2,1)}, u32[]{:S(2)}) copy-start(bf16[2,128,5,3,64]{1,0,4,3,2:T(2,128)(2,1)} %reshape_reshape.14) | copy-start | bytes 1474564
  379.8 188.1 %reduce-scatter.9.cloned.1.call-start = ((), (), s32[]{:S(2)}) async-start(), calls=%async_computation.5 | async-start | bytes 2949120
  439.5 11.1 %collective-permute-start.1 = (bf16[2,128,960]{1,2,0:T(8,128)(2,1)S(1)}, bf16[2,128,960]{1,2,0:T(8,128)(2,1)S(1)}, u32[]{:S(2)}, u32[]{:S(2)}) collective-permute-start(bf16[2,128,960]{1,2,0:T(8,128)(2,1)S(1)} %copy_bitcast_fusion.2), channel_id=1, source_target_pairs={{64,0},{65,1},{66,2},{67,3},{68,4},{69,5},{70,6},{71,7},{72,8},{73... | collective-permute-start | bytes 1474568 | tf_op jit(solution)/shard_map/ppermute | solution.py:605
  450.6 17.0 %copy-start.27 = (bf16[2,128,960]{1,2,0:T(8,128)(2,1)}, bf16[2,128,960]{1,2,0:T(8,128)(2,1)S(1)}, u32[]{:S(2)}) copy-start(bf16[2,128,960]{1,2,0:T(8,128)(2,1)S(1)} %collective-permute-done.1) | copy-start | bytes 1474564
  450.7 8.9 %copy-start.41 = (bf16[256,960]{0,1:T(8,128)(2,1)}, bf16[256,960]{0,1:T(8,128)(2,1)S(1)}, u32[]{:S(2)}) copy-start(bf16[256,960]{0,1:T(8,128)(2,1)S(1)} %copy_bitcast_fusion.1) | copy-start | bytes 1474564
  486.9 8.1 %copy-start.16 = (bf16[2,128,960]{1,2,0:T(8,128)(2,1)S(1)}, bf16[2,128,960]{1,2,0:T(8,128)(2,1)}, u32[]{:S(2)}) copy-start(bf16[2,128,960]{1,2,0:T(8,128)(2,1)} %copy-done.15) | copy-start | bytes 1474564
  511.3 10.4 %copy-start.26 = (bf16[256,8,120]{0,2,1:T(8,128)(2,1)S(1)}, bf16[256,8,120]{0,2,1:T(8,128)(2,1)}, u32[]{:S(2)}) copy-start(bf16[256,8,120]{0,2,1:T(8,128)(2,1)} %copy-done.25) | copy-start | bytes 1474564
  511.3 11.3 %copy-start.23 = (bf16[256,8,120]{2,0,1:T(8,128)(2,1)S(1)}, bf16[256,8,120]{2,0,1:T(8,128)(2,1)}, u32[]{:S(2)}) copy-start(bf16[256,8,120]{2,0,1:T(8,128)(2,1)} %copy-done.22) | copy-start | bytes 1474564
  515.3 9.3 %collective-permute-start.2 = (bf16[256,1024]{0,1:T(8,128)(2,1)}, bf16[256,1024]{0,1:T(8,128)(2,1)S(1)}, u32[]{:S(2)}, u32[]{:S(2)}) collective-permute-start(bf16[256,1024]{0,1:T(8,128)(2,1)} %bitcast.529), channel_id=1, source_target_pairs={{0,8},{8,0},{16,24},{24,16},{32,40},{40,32},{48,56},{56,48},{1,9},... | collective-permute-start | bytes 1572872 | tf_op jit(solution)/shard_map/ppermute | solution.py:610
  522.6 65.2 %collective-permute-start.6 = (bf16[256,8,64]{0,2,1:T(8,128)(2,1)}, bf16[256,8,64]{0,2,1:T(8,128)(2,1)}, u32[]{:S(2)}, u32[]{:S(2)}) collective-permute-start(bf16[256,8,64]{0,2,1:T(8,128)(2,1)} %get-tuple-element.86), channel_id=1, source_target_pairs={{0,8},{8,0},{16,24},{24,16},{32,40},{40,32},{48,56},{56,48},{1,9},... | collective-permute-start | bytes 786440 | tf_op jit(solution)/shard_map/ppermute | solution.py:610
  524.1 21.8 %collective-permute-start.9 = (bf16[256,8,64]{2,0,1:T(8,128)(2,1)}, bf16[256,8,64]{2,0,1:T(8,128)(2,1)}, u32[]{:S(2)}, u32[]{:S(2)}) collective-permute-start(bf16[256,8,64]{2,0,1:T(8,128)(2,1)} %get-tuple-element.84), channel_id=1, source_target_pairs={{0,8},{8,0},{16,24},{24,16},{32,40},{40,32},{48,56},{56,48},{1,9},... | collective-permute-start | bytes 786440 | tf_op jit(solution)/shard_map/ppermute | solution.py:610
  525.6 20.5 %collective-permute-start.10 = (bf16[256,960]{0,1:T(8,128)(2,1)}, bf16[256,960]{0,1:T(8,128)(2,1)}, u32[]{:S(2)}, u32[]{:S(2)}) collective-permute-start(bf16[256,960]{0,1:T(8,128)(2,1)} %fusion.137), channel_id=1, source_target_pairs={{0,8},{8,0},{16,24},{24,16},{32,40},{40,32},{48,56},{56,48},{1,9},... | collective-permute-start | bytes 1474568 | tf_op jit(solution)/shard_map/ppermute | solution.py:610
  525.6 23.2 %collective-permute-start.4 = (bf16[256,2560]{1,0:T(8,128)(2,1)}, bf16[256,2560]{1,0:T(8,128)(2,1)}, u32[]{:S(2)}, u32[]{:S(2)}) collective-permute-start(bf16[256,2560]{1,0:T(8,128)(2,1)} %get-tuple-element.68), channel_id=1, source_target_pairs={{0,8},{8,0},{16,24},{24,16},{32,40},{40,32},{48,56},{56,48},{1,9},... | collective-permute-start | bytes 3932168 | tf_op jit(solution)/shard_map/ppermute | solution.py:610
  536.8 19.6 %collective-permute-start.3 = (bf16[256,2560]{1,0:T(8,128)(2,1)}, bf16[256,2560]{1,0:T(8,128)(2,1)}, u32[]{:S(2)}, u32[]{:S(2)}) collective-permute-start(bf16[256,2560]{1,0:T(8,128)(2,1)} %get-tuple-element.70), channel_id=1, source_target_pairs={{0,8},{8,0},{16,24},{24,16},{32,40},{40,32},{48,56},{56,48},{1,9},... | collective-permute-start | bytes 3932168 | tf_op jit(solution)/shard_map/ppermute | solution.py:610
  545.9 18.0 %collective-permute-start.5 = (bf16[256,512]{0,1:T(8,128)(2,1)}, bf16[256,512]{0,1:T(8,128)(2,1)}, u32[]{:S(2)}, u32[]{:S(2)}) collective-permute-start(bf16[256,512]{0,1:T(8,128)(2,1)} %get-tuple-element.88), channel_id=1, source_target_pairs={{0,8},{8,0},{16,24},{24,16},{32,40},{40,32},{48,56},{56,48},{1,9},... | collective-permute-start | bytes 786440 | tf_op jit(solution)/shard_map/ppermute | solution.py:610
  582.4 5.4 collective-permute-start.8
  582.7 5.1 collective-permute-start.7
  (56 other events, 214.2 us)
Sparse Core Ops, SparseCore 0:
  119.2 44.3 all-gather.2
  226.7 51.2 all-gather.4
  379.9 45.5 reduce-scatter.6
  511.4 43.6 reduce-scatter.8

commit v2 on v1

--- a/solution.py
+++ b/solution.py
@@ -383,6 +383,413 @@
     )(*terms)
 
 
+TOKENS = 1024
+LOCAL = TOKENS // SHARDS
+SLOTS = 2
+BLOCK = 256
+PAIR = 2 * HEAD_WIDTH
+NEGATIVE = -1e30
+
+
+def two_groups(device):
+    return (device == 1) | (device == 4)
+
+
+def group_lanes(device, which):
+    return pl.ds(pl.multiple_of(((2 * device) // 3 + which) * PAIR, PAIR), PAIR)
+
+
+def pair_lanes(device):
+    return pl.ds(pl.multiple_of(device * PAIR, PAIR), PAIR)
+
+
+def token_rows(device):
+    return pl.ds(pl.multiple_of(device * LOCAL, LOCAL), LOCAL)
+
+
+def ring(me):
+    return [(step, (me + step) % SHARDS, (me + SHARDS - step) % SHARDS) for step in range(1, SHARDS)]
+
+
+def greet_all(me):
+    barrier = pltpu.get_barrier_semaphore()
+    for _, target, _ in ring(me):
+        pl.semaphore_signal(barrier, inc=1, device_id={"fsdp": target}, device_id_type=MESH)
+    pl.semaphore_wait(barrier, SHARDS - 1)
+
+
+def sent(source, target, send_sem, recv_sem, device):
+    return pltpu.make_async_remote_copy(
+        src_ref=source,
+        dst_ref=target,
+        send_sem=send_sem,
+        recv_sem=recv_sem,
+        device_id={"fsdp": device},
+        device_id_type=MESH,
+    )
+
+
+def causal_mask(values):
+    length = values.shape[1]
+    row = lax.broadcasted_iota(jnp.int32, (BLOCK, BLOCK), 0)
+    column = lax.broadcasted_iota(jnp.int32, (BLOCK, BLOCK), 1)
+    own = jnp.where(column <= row, values[:, length - BLOCK :], NEGATIVE)
+    if length == BLOCK:
+        return own
+    return jnp.concatenate([values[:, : length - BLOCK], own], 1)
+
+
+def dot_t(left, right):
+    return lax.dot_general(
+        left, right, (((1,), (1,)), ((), ())), preferred_element_type=jnp.float32
+    )
+
+
+def dot_first(left, right):
+    return lax.dot_general(
+        left, right, (((0,), (0,)), ((), ())), preferred_element_type=jnp.float32
+    )
+
+
+def attend_kernel(
+    q_ref, kv_ref, mixed_ref, q_kept, kv_kept, lse_kept,
+    q_all, kv_all, lse_all, mixed_all, local_sem, send_sem, recv_sem,
+):
+    me = lax.axis_index("fsdp")
+    both = two_groups(me)
+    second = jnp.where(both, 1, 0)
+
+    def incoming(slot, step, device, sender):
+        rows = token_rows(sender)
+        return [
+            sent(
+                q_ref.at[slot, :, pair_lanes(device)], q_all.at[slot, rows, :],
+                send_sem.at[0, slot, step], recv_sem.at[0, slot, step], device,
+            ),
+            sent(
+                kv_ref.at[slot, :, group_lanes(device, 0)], kv_all.at[0, slot, rows, :],
+                send_sem.at[1, slot, step], recv_sem.at[1, slot, step], device,
+            ),
+        ]
+
+    def extra(slot, step, device, sender):
+        group = jnp.where(two_groups(device), 1, 0)
+        return sent(
+            kv_ref.at[slot, :, group_lanes(device, group)], kv_all.at[1, slot, token_rows(sender), :],
+            send_sem.at[2, slot, step], recv_sem.at[2, slot, step], device,
+        )
+
+    def outgoing(slot, step, device, sender):
+        return sent(
+            mixed_all.at[slot, token_rows(device), :], mixed_ref.at[slot, :, pair_lanes(sender)],
+            send_sem.at[3, slot, step], recv_sem.at[3, slot, step], device,
+        )
+
+    def own_copies(slot):
+        rows = token_rows(me)
+        group = jnp.where(both, 1, 0)
+        return [
+            pltpu.make_async_copy(
+                q_ref.at[slot, :, pair_lanes(me)], q_all.at[slot, rows, :], local_sem.at[0, slot]
+            ),
+            pltpu.make_async_copy(
+                kv_ref.at[slot, :, group_lanes(me, 0)], kv_all.at[0, slot, rows, :],
+                local_sem.at[1, slot],
+            ),
+            pltpu.make_async_copy(
+                kv_ref.at[slot, :, group_lanes(me, group)], kv_all.at[1, slot, rows, :],
+                local_sem.at[2, slot],
+            ),
+        ]
+
+    def own_result(slot):
+        return pltpu.make_async_copy(
+            mixed_all.at[slot, token_rows(me), :], mixed_ref.at[slot, :, pair_lanes(me)],
+            local_sem.at[3, slot],
+        )
+
+    greet_all(me)
+    for slot in range(SLOTS):
+        for step, target, _ in ring(me):
+            for copy in incoming(slot, step, target, me):
+                copy.start()
+
+            @pl.when(two_groups(target))
+            def _():
+                extra(slot, step, target, me).start()
+
+        for copy in own_copies(slot):
+            copy.start()
+
+    @pl.loop(0, SLOTS)
+    def _(slot):
+        for step, _, source in ring(me):
+            for copy in incoming(slot, step, source, source):
+                copy.wait_recv()
+
+            @pl.when(both)
+            def _():
+                extra(slot, step, source, source).wait_recv()
+
+        for copy in own_copies(slot):
+            copy.wait()
+        for block in range(TOKENS // BLOCK):
+            rows = pl.ds(block * BLOCK, BLOCK)
+            length = (block + 1) * BLOCK
+            outs, totals = [], []
+            for head in range(2):
+                group = 0 if head == 0 else second
+                lanes = slice(head * HEAD_WIDTH, (head + 1) * HEAD_WIDTH)
+                query = q_all[slot, rows, lanes]
+                keys = kv_all[group, slot, :length, :HEAD_WIDTH]
+                values = kv_all[group, slot, :length, HEAD_WIDTH:]
+                scores = causal_mask(dot_t(query, keys))
+                highest = jnp.max(scores, -1, keepdims=True)
+                weights = jnp.exp(scores - highest)
+                total = jnp.sum(weights, -1, keepdims=True)
+                out = jnp.dot(
+                    weights.astype(jnp.bfloat16), values, preferred_element_type=jnp.float32
+                )
+                outs.append(out / total)
+                totals.append(
+                    jnp.broadcast_to(highest + jnp.log(total), (BLOCK, HEAD_WIDTH))
+                )
+            mixed_all[slot, rows, :] = jnp.concatenate(outs, 1).astype(jnp.bfloat16)
+            lse_all[slot, rows, :] = jnp.concatenate(totals, 1)
+        for step, target, _ in ring(me):
+            outgoing(slot, step, target, me).start()
+        own_result(slot).start()
+
+    keep = [
+        pltpu.make_async_copy(q_all, q_kept, local_sem.at[4, 0]),
+        pltpu.make_async_copy(kv_all, kv_kept, local_sem.at[4, 1]),
+        pltpu.make_async_copy(lse_all, lse_kept, local_sem.at[5, 0]),
+    ]
+    for copy in keep:
+        copy.start()
+    for slot in range(SLOTS):
+        for step, target, source in ring(me):
+            outgoing(slot, step, source, source).wait_recv()
+            outgoing(slot, step, target, me).wait_send()
+            for copy in incoming(slot, step, target, me):
+                copy.wait_send()
+
+            @pl.when(two_groups(target))
+            def _():
+                extra(slot, step, target, me).wait_send()
+
+        own_result(slot).wait()
+    for copy in keep:
+        copy.wait()
+
+
+Q_ALL = (SLOTS, TOKENS, PAIR)
+KV_ALL = (2, SLOTS, TOKENS, PAIR)
+FULL = SHARDS * PAIR
+
+
+def attend(query_rows, key_values):
+    bf16 = jnp.bfloat16
+    return pl.pallas_call(
+        attend_kernel,
+        name="attend",
+        out_shape=[
+            jax.ShapeDtypeStruct((SLOTS, LOCAL, FULL), bf16),
+            jax.ShapeDtypeStruct(Q_ALL, bf16),
+            jax.ShapeDtypeStruct(KV_ALL, bf16),
+            jax.ShapeDtypeStruct(Q_ALL, jnp.float32),
+        ],
+        in_specs=[ANY] * 2,
+        out_specs=[ANY] * 4,
+        scratch_shapes=[
+            pltpu.VMEM(Q_ALL, bf16),
+            pltpu.VMEM(KV_ALL, bf16),
+            pltpu.VMEM(Q_ALL, jnp.float32),
+            pltpu.VMEM(Q_ALL, bf16),
+            pltpu.SemaphoreType.DMA((6, SLOTS)),
+            pltpu.SemaphoreType.DMA((4, SLOTS, SHARDS)),
+            pltpu.SemaphoreType.DMA((4, SLOTS, SHARDS)),
+        ],
+        compiler_params=pltpu.CompilerParams(
+            collective_id=2, has_side_effects=True, vmem_limit_bytes=40 * 2**20
+        ),
+    )(query_rows, key_values)
+
+
+def attend_back_kernel(
+    slope_ref, q_ref, kv_ref, lse_ref, dq_ref, dkv_ref, dkv_extra_ref,
+    slope_all, q_all, kv_all, lse_all, dq_all, dkv_total, dkv_all,
+    local_sem, send_sem, recv_sem,
+):
+    me = lax.axis_index("fsdp")
+    both = two_groups(me)
+    second = jnp.where(both, 1, 0)
+    extra_at = me // 4
+
+    def incoming(slot, step, device, sender):
+        return sent(
+            slope_ref.at[slot, :, pair_lanes(device)], slope_all.at[slot, token_rows(sender), :],
+            send_sem.at[0, slot, step], recv_sem.at[0, slot, step], device,
+        )
+
+    def outgoing(slot, step, device, sender):
+        rows = token_rows(device)
+        return [
+            sent(
+                dq_all.at[slot, rows, :], dq_ref.at[slot, :, pair_lanes(sender)],
+                send_sem.at[1, slot, step], recv_sem.at[1, slot, step], device,
+            ),
+            sent(
+                dkv_all.at[0, slot, rows, :], dkv_ref.at[sender, slot],
+                send_sem.at[2, slot, step], recv_sem.at[2, slot, step], device,
+            ),
+        ]
+
+    def extra(slot, step, device, sender):
+        return sent(
+            dkv_all.at[1, slot, token_rows(device), :], dkv_extra_ref.at[sender // 4, slot],
+            send_sem.at[3, slot, step], recv_sem.at[3, slot, step], device,
+        )
+
+    def own_slope(slot):
+        return pltpu.make_async_copy(
+            slope_ref.at[slot, :, pair_lanes(me)], slope_all.at[slot, token_rows(me), :],
+            local_sem.at[0, slot],
+        )
+
+    def own_results(slot):
+        rows = token_rows(me)
+        return [
+            pltpu.make_async_copy(
+                dq_all.at[slot, rows, :], dq_ref.at[slot, :, pair_lanes(me)], local_sem.at[1, slot]
+            ),
+            pltpu.make_async_copy(
+                dkv_all.at[0, slot, rows, :], dkv_ref.at[me, slot], local_sem.at[2, slot]
+            ),
+        ]
+
+    def own_extra(slot):
+        return pltpu.make_async_copy(
+            dkv_all.at[1, slot, token_rows(me), :], dkv_extra_ref.at[extra_at, slot],
+            local_sem.at[3, slot],
+        )
+
+    loads = [
+        pltpu.make_async_copy(q_ref, q_all, local_sem.at[4, 0]),
+        pltpu.make_async_copy(kv_ref, kv_all, local_sem.at[4, 1]),
+        pltpu.make_async_copy(lse_ref, lse_all, local_sem.at[5, 0]),
+    ]
+    for copy in loads:
+        copy.start()
+    greet_all(me)
+    for slot in range(SLOTS):
+        for step, target, _ in ring(me):
+            incoming(slot, step, target, me).start()
+        own_slope(slot).start()
+    for copy in loads:
+        copy.wait()
+
+    @pl.loop(0, SLOTS)
+    def _(slot):
+        for step, _, source in ring(me):
+            incoming(slot, step, source, source).wait_recv()
+        own_slope(slot).wait()
+        dkv_total[...] = jnp.zeros_like(dkv_total)
+        for block in range(TOKENS // BLOCK):
+            rows = pl.ds(block * BLOCK, BLOCK)
+            length = (block + 1) * BLOCK
+            outs = []
+            for head in range(2):
+                group = 0 if head == 0 else second
+                lanes = slice(head * HEAD_WIDTH, (head + 1) * HEAD_WIDTH)
+                query = q_all[slot, rows, lanes]
+                slope = slope_all[slot, rows, lanes]
+                lse = lse_all[slot, rows, head * HEAD_WIDTH : head * HEAD_WIDTH + 1]
+                keys = kv_all[group, slot, :length, :HEAD_WIDTH]
+                values = kv_all[group, slot, :length, HEAD_WIDTH:]
+                probs = jnp.exp(causal_mask(dot_t(query, keys)) - lse)
+                prob_slope = dot_t(slope, values)
+                inner = jnp.sum(probs * prob_slope, -1, keepdims=True)
+                score_slope = (probs * (prob_slope - inner)).astype(jnp.bfloat16)
+                outs.append(
+                    jnp.dot(score_slope, keys, preferred_element_type=jnp.float32)
+                    * HEAD_WIDTH ** (-0.5)
+                )
+                dkv_total[group, :length, :] += jnp.concatenate(
+                    [dot_first(score_slope, query), dot_first(probs.astype(jnp.bfloat16), slope)], 1
+                )
+            dq_all[slot, rows, :] = jnp.concatenate(outs, 1).astype(jnp.bfloat16)
+        dkv_all[0, slot] = dkv_total[0].astype(jnp.bfloat16)
+        dkv_all[1, slot] = dkv_total[1].astype(jnp.bfloat16)
+        for step, target, _ in ring(me):
+            for copy in outgoing(slot, step, target, me):
+                copy.start()
+
+            @pl.when(both)
+            def _():
+                extra(slot, step, target, me).start()
+
+        for copy in own_results(slot):
+            copy.start()
+
+        @pl.when(both)
+        def _():
+            own_extra(slot).start()
+
+    for slot in range(SLOTS):
+        for step, target, source in ring(me):
+            incoming(slot, step, target, me).wait_send()
+            for copy in outgoing(slot, step, source, source):
+                copy.wait_recv()
+            for copy in outgoing(slot, step, target, me):
+                copy.wait_send()
+
+            @pl.when(two_groups(source))
+            def _():
+                extra(slot, step, source, source).wait_recv()
+
+            @pl.when(both)
+            def _():
+                extra(slot, step, target, me).wait_send()
+
+        for copy in own_results(slot):
+            copy.wait()
+
+        @pl.when(both)
+        def _():
+            own_extra(slot).wait()
+
+
+def attend_back(slope, kept):
+    bf16 = jnp.bfloat16
+    return pl.pallas_call(
+        attend_back_kernel,
+        name="attend_back",
+        out_shape=[
+            jax.ShapeDtypeStruct((SLOTS, LOCAL, FULL), bf16),
+            jax.ShapeDtypeStruct((SHARDS, SLOTS, LOCAL, PAIR), bf16),
+            jax.ShapeDtypeStruct((2, SLOTS, LOCAL, PAIR), bf16),
+        ],
+        in_specs=[ANY] * 4,
+        out_specs=[ANY] * 3,
+        scratch_shapes=[
+            pltpu.VMEM(Q_ALL, bf16),
+            pltpu.VMEM(Q_ALL, bf16),
+            pltpu.VMEM(KV_ALL, bf16),
+            pltpu.VMEM(Q_ALL, jnp.float32),
+            pltpu.VMEM(Q_ALL, bf16),
+            pltpu.VMEM((2, TOKENS, PAIR), jnp.float32),
+            pltpu.VMEM(KV_ALL, bf16),
+            pltpu.SemaphoreType.DMA((6, SLOTS)),
+            pltpu.SemaphoreType.DMA((4, SLOTS, SHARDS)),
+            pltpu.SemaphoreType.DMA((4, SLOTS, SHARDS)),
+        ],
+        compiler_params=pltpu.CompilerParams(
+            collective_id=3, has_side_effects=True, vmem_limit_bytes=48 * 2**20
+        ),
+    )(slope, *kept)
+
+
 def rotary_tables(positions):
     half = HEAD_WIDTH // 2
     frequency = BASE ** (-(jnp.arange(half).astype(jnp.float32) * (2.0 / HEAD_WIDTH)))
@@ -434,22 +841,7 @@
     return values.reshape(values.shape[:-1] + (-1, HEAD_WIDTH))
 
 
-def masked_scores(query_matrix, key_value_pair, shard_index):
-    batches, local_count = query_matrix.shape[:2]
-    token_length = key_value_pair.shape[1]
-    grouped_heads = query_matrix.reshape(
-        batches, local_count, KEY_VALUE_HEADS, QUERY_HEADS // KEY_VALUE_HEADS, HEAD_WIDTH
-    )
-    key_rows = heads(key_value_pair[..., :KEY_WIDTH])
-    scores = jnp.einsum(
-        "btgqd,bsgd->bgqts", grouped_heads, key_rows, preferred_element_type=jnp.float32
-    ) * HEAD_WIDTH ** (-0.5)
-    query_rows = shard_index * local_count + jnp.arange(local_count)
-    causal = query_rows[:, None] >= jnp.arange(token_length)[None, :]
-    return jnp.where(causal, scores, -1e30)
-
-
-def forward_layer(layer_in, tables, weights, shard_index):
+def forward_layer(layer_in, tables, weights):
     attend_in, attend_out, gate_up, down_weight, gains = weights
     batches, local_count = layer_in.shape[:2]
     rows = batches * local_count
@@ -458,24 +850,16 @@
     projected = jnp.dot(first_norm, attend_in, preferred_element_type=jnp.float32)
     projected = projected.reshape(batches, local_count, QKV)
     rotated = apply_rotation(heads(projected[..., : QUERY_WIDTH + KEY_WIDTH]), *tables)
-    rotated = rotated.astype(jnp.bfloat16).reshape(batches, local_count, -1)
-    query_matrix = rotated[..., :QUERY_WIDTH]
-    own_pair = jnp.concatenate(
-        [rotated[..., QUERY_WIDTH:], projected[..., QUERY_WIDTH + KEY_WIDTH :].astype(jnp.bfloat16)],
-        -1,
-    )
-    key_value_pair = lax.all_gather(own_pair, "fsdp", axis=1, tiled=True)
-    scores = masked_scores(query_matrix, key_value_pair, shard_index)
-    highest = jnp.max(scores, -1)
-    totals = highest + jnp.log(jnp.sum(jnp.exp(scores - highest[..., None]), -1))
-    probs = jnp.exp(scores - totals[..., None]).astype(jnp.bfloat16)
-    mixed = jnp.einsum(
-        "bgqts,bsgd->btgqd",
-        probs,
-        heads(key_value_pair[..., KEY_WIDTH:]),
-        preferred_element_type=jnp.float32,
-    )
-    mixed = pad_shards(mixed.astype(jnp.bfloat16).reshape(rows, QUERY_WIDTH))
+    query_rows = rotated[..., :QUERY_HEADS, :].astype(jnp.bfloat16) * HEAD_WIDTH ** (-0.5)
+    query_rows = jnp.pad(
+        query_rows.reshape(batches, local_count, QUERY_WIDTH), ((0, 0), (0, 0), (0, HEAD_WIDTH))
+    )
+    key_values = jnp.concatenate(
+        [rotated[..., QUERY_HEADS:, :], heads(projected[..., QUERY_WIDTH + KEY_WIDTH :])], -1
+    )
+    key_values = key_values.astype(jnp.bfloat16).reshape(batches, local_count, 2 * KEY_WIDTH)
+    mixed, *attended = attend(query_rows, key_values)
+    mixed = mixed.reshape(rows, FULL)
     hidden = values + jnp.dot(mixed, attend_out, preferred_element_type=jnp.float32)
     second_norm = pad_shards(normed(hidden, gains[1]).astype(jnp.bfloat16))
     gated = jnp.dot(second_norm, gate_up, preferred_element_type=jnp.float32)
@@ -484,9 +868,7 @@
     kept = (
         values,
         first_norm,
-        query_matrix,
-        key_value_pair,
-        totals,
+        attended,
         mixed,
         hidden,
         second_norm,
@@ -496,14 +878,12 @@
     return (result.astype(jnp.bfloat16).reshape(layer_in.shape), kept)
 
 
-def backward_layer(upstream, kept, tables, weights, shard_index):
+def backward_layer(upstream, kept, tables, weights):
     attend_in, attend_out, gate_up, down_weight, gains = weights
     (
         values,
         first_norm,
-        query_matrix,
-        key_value_pair,
-        totals,
+        attended,
         mixed,
         hidden,
         second_norm,
@@ -512,8 +892,6 @@
     ) = kept
     batches, local_count = upstream.shape[:2]
     rows = batches * local_count
-    token_length = key_value_pair.shape[1]
-    scale = HEAD_WIDTH ** (-0.5)
     upstream = upstream.reshape(rows, D)
     down_in = jnp.pad(upstream, ((0, 0), (0, DOWN_COLUMNS - D)))
     upstream = upstream.astype(jnp.float32)
@@ -530,61 +908,34 @@
     hidden_part, second_gain = norm_backward(hidden, gains[1], second_slope)
     hidden_slope = upstream + hidden_part
     branch_slope = hidden_slope.astype(jnp.bfloat16)
-    mixed_gradient = unpad_shards(
-        jnp.einsum(
-            "td,qd->tq", branch_slope, attend_out, preferred_element_type=jnp.float32
-        ).astype(jnp.bfloat16)
-    )
-    mixed_gradient = mixed_gradient.reshape(
-        batches, local_count, KEY_VALUE_HEADS, QUERY_HEADS // KEY_VALUE_HEADS, HEAD_WIDTH
-    )
-    scores = masked_scores(query_matrix, key_value_pair, shard_index)
-    probs = jnp.exp(scores - totals[..., None])
-    probs_low = probs.astype(jnp.bfloat16)
-    complete_keys = heads(key_value_pair[..., :KEY_WIDTH])
-    complete_values = heads(key_value_pair[..., KEY_WIDTH:])
-    prob_slope = jnp.einsum(
-        "btgqd,bsgd->bgqts", mixed_gradient, complete_values, preferred_element_type=jnp.float32
-    )
-    score_slope = probs * (prob_slope - jnp.sum(probs * prob_slope, -1, keepdims=True))
-    score_slope = score_slope.astype(jnp.bfloat16)
-    query_slope = (
-        jnp.einsum(
-            "bgqts,bsgd->btgqd", score_slope, complete_keys, preferred_element_type=jnp.float32
-        )
-        * scale
-    )
-    grouped_heads = query_matrix.reshape(mixed_gradient.shape)
-    key_part = (
-        jnp.einsum(
-            "bgqts,btgqd->bsgd", score_slope, grouped_heads, preferred_element_type=jnp.float32
-        )
-        * scale
-    )
-    val_part = jnp.einsum(
-        "bgqts,btgqd->bsgd", probs_low, mixed_gradient, preferred_element_type=jnp.float32
-    )
-    owned_part = lax.psum_scatter(
-        jnp.concatenate(
-            [
-                key_part.reshape(batches, token_length, KEY_WIDTH),
-                val_part.reshape(batches, token_length, KEY_WIDTH),
-            ],
-            -1,
-        ).astype(jnp.bfloat16),
-        "fsdp",
-        scatter_dimension=1,
-        tiled=True,
-    ).astype(jnp.float32)
+    mixed_gradient = jnp.einsum(
+        "td,qd->tq", branch_slope, attend_out, preferred_element_type=jnp.float32
+    ).astype(jnp.bfloat16)
+    query_slope, pair_slopes, extra_slopes = attend_back(
+        mixed_gradient.reshape(batches, local_count, FULL), attended
+    )
+    pair_slopes = pair_slopes.astype(jnp.float32)
+    extra_slopes = extra_slopes.astype(jnp.float32)
+    group_slopes = jnp.stack(
+        [
+            pair_slopes[0] + pair_slopes[1],
+            extra_slopes[0] + pair_slopes[2],
+            pair_slopes[3] + pair_slopes[4],
+            extra_slopes[1] + pair_slopes[5],
+            pair_slopes[6] + pair_slopes[7],
+        ],
+        2,
+    )
+    query_slope = query_slope[..., :QUERY_WIDTH].astype(jnp.float32)
     query_raw = reverse_rotation(
         query_slope.reshape(batches, local_count, QUERY_HEADS, HEAD_WIDTH), *tables
     ).reshape(rows, QUERY_WIDTH)
-    unrotated_key = reverse_rotation(heads(owned_part[..., :KEY_WIDTH]), *tables)
+    unrotated_key = reverse_rotation(group_slopes[..., :HEAD_WIDTH], *tables)
     projected_slope = jnp.concatenate(
         [
             query_raw,
             unrotated_key.reshape(rows, KEY_WIDTH),
-            owned_part[..., KEY_WIDTH:].reshape(rows, KEY_WIDTH),
+            group_slopes[..., HEAD_WIDTH:].reshape(rows, KEY_WIDTH),
         ],
         1,
     ).astype(jnp.bfloat16)
@@ -613,7 +964,8 @@
 
 def weight_terms(kept, slopes, gain_slopes):
     core = lax.axis_index("dp") % 2
-    first_norm, mixed, second_norm, act = (kept[1], kept[5], kept[7], kept[9])
+    first_norm, mixed, second_norm, act = (kept[1], kept[3], kept[5], kept[7])
+    mixed = pad_shards(mixed[:, :QUERY_WIDTH])
     projected_slope, branch_slope, gated_slope, down_in = slopes
     tokens = act.shape[0]
 
@@ -652,7 +1004,6 @@
     inputs, positions, plan, attend_in, attend_out, gate_up, down_weight, norm_gains, cotangent
 ):
     section_index = lax.axis_index("section")
-    shard_index = lax.axis_index("fsdp")
     extra = PADDED - ROWS
     in_shard = jnp.concatenate(
         [
@@ -672,7 +1023,7 @@
     gains = gathered[2][:, ROWS : ROWS + 2, :ROWS].swapaxes(0, 1).reshape(2, D)
     weights = (
         gathered[2].reshape(-1, QKV),
-        gathered[3].reshape(-1, D),
+        jnp.pad(gathered[3][:, :ROWS].reshape(QUERY_WIDTH, D), ((0, FULL - QUERY_WIDTH), (0, 0))),
         gathered[0].reshape(-1, 2 * FF),
         gathered[1].reshape(-1, DOWN_COLUMNS),
         gains.astype(jnp.float32),
@@ -681,13 +1032,13 @@
     fresh = jnp.take(inputs[:, 0], plan_row, axis=0)
     tables = rotary_tables(jnp.take(positions[:, 0], plan_row, axis=0))
     given = cotangent[:, 0]
-    result, _ = forward_layer(fresh, tables, weights, shard_index)
+    result, _ = forward_layer(fresh, tables, weights)
     layer_in = jnp.where(section_index == 0, fresh, passed_along(result, 1))
-    outputs, kept = forward_layer(layer_in, tables, weights, shard_index)
-    input_slope, _, _ = backward_layer(given, kept, tables, weights, shard_index)
+    outputs, kept = forward_layer(layer_in, tables, weights)
+    input_slope, _, _ = backward_layer(given, kept, tables, weights)
     back = passed_along(input_slope.astype(jnp.bfloat16), -1)
     upstream = jnp.where(section_index == 1, given, back)
-    input_slope, slopes, gain_slopes = backward_layer(upstream, kept, tables, weights, shard_index)
+    input_slope, slopes, gain_slopes = backward_layer(upstream, kept, tables, weights)
     reported = jnp.where(
         section_index == 0, input_slope, input_slope.astype(jnp.bfloat16).astype(jnp.float32)
     )

time: 710 us -> 536 us (0.75)
  Pallas kernels: 193 us -> 336 us
  waiting for transfers between devices: 145 us -> 6.23 us
  matrix products: 160 us -> 73 us
  other arithmetic: 79.4 us -> 39.4 us
  local copies, waits for them, and re-layouts: 94.6 us -> 62.5 us
  between operations: 15.6 us -> 2.57 us
    pallas_call x0 -> x4, Pallas kernels: none -> 138 us  [the longest x2 75.3 us: attend_back(): pl.pallas_call(attend_back_kernel, name='attend_back', out_shape=[jax.Sha...]
    all_gather x2 -> x0, waiting for transfers between devices: 93.2 us -> none  [forward_layer(): key_value_pair = lax.all_gather(own_pair, 'fsdp', axis=1, tiled=True)]
    dot_general x12 -> x0, matrix products: 70.7 us -> none  [the longest x2 17.4 us: backward_layer(): jnp.einsum('btgqd,bsgd->bgqts', mixed_gradient, complete_values, preferre...]
    unnamed x6 -> x0, waiting for transfers between devices: 35.8 us -> none
    unnamed x157 -> x165, local copies, waits for them, and re-layouts: 39.7 us -> 11.4 us
    convert_element_type x5 -> x6, other arithmetic: 24.1 us -> 1.43 us  [the longest x2 1.19 us: backward_layer(): query_slope = query_slope[..., :QUERY_WIDTH].astype(jnp.float32)]
    reduce_sum x2 -> x0, other arithmetic: 17.5 us -> none  [forward_layer(): jnp.sum(jnp.exp(scores - highest[..., None]), -1)]
    ppermute x2, waiting for transfers between devices: 15.7 us -> 6.21 us  [passed_along(): return lax.ppermute(value, 'section', [(0, 1)] if steps > 0 else [(1, 0)])]
  transfers between devices with their start and end apart: 15 -> 11, of which waited for: 5 -> 1; matrix products, arithmetic and copies ran while one was open for 11% -> 14% of each run, Pallas kernels for 0% -> 6%
where the time goes in v2:
time: 536 us; the launch traced here: 535 us
  Pallas kernels  336 us (63%)
  matrix products  73 us (14%)
  local copies, waits for them, and re-layouts  62.5 us (12%)
  other arithmetic  39.4 us (7%)
  starting transfers between devices  16 us (3%)
  waiting for transfers between devices  6.23 us (1%)
    pallas_call x1, Pallas kernels, reduce_gradients(): pl.pallas_call(reduce_kernel, name='reduce_gradients', out_shape=[jax.Sha...  105 us
    pallas_call x1, Pallas kernels, gather_weights(): pl.pallas_call(gather_kernel, name='gather_weights', out_shape=[jax.Shape...  93.4 us
    pallas_call x2, Pallas kernels, attend_back(): pl.pallas_call(attend_back_kernel, name='attend_back', out_shape=[jax.Sha...  75.3 us
    pallas_call x2, Pallas kernels, attend(): pl.pallas_call(attend_kernel, name='attend', out_shape=[jax.ShapeDtypeStr...  62.3 us
    dot_general x2, matrix products, backward_layer(): jnp.einsum('td,fd->tf', down_in, down_weight, preferred_element_type=jnp....  15.8 us
    dot_general x4, matrix products, term(): jnp.einsum('tkr,tn->krn', split, right, preferred_element_type=jnp.float32)  15.3 us
    dot_general x2, matrix products, forward_layer(): gated = jnp.dot(second_norm, gate_up, preferred_element_type=jnp.float32)  11.5 us
    unnamed x165, local copies, waits for them, and re-layouts  11.4 us
  transfers between devices with their start and end apart: 11, of which 1 were waited for; matrix products, arithmetic and copies ran while one was open for 14% of the time, Pallas kernels for 6%

profile of v2, /device:TPU:1, one launch (start us, length us, event | category | flops | bytes accessed | tf_op | source)
XLA Modules:
  0.0 535.4 jit_solution(6684556314265117558)
XLA Ops:
  7.3 93.4 %gather_weights.1 = (bf16[8,128,5120]{2,1,0:T(8,128)(2,1)}, bf16[8,320,1024]{2,1,0:T(8,128)(2,1)}, bf16[8,128,1600]{2,1,0:T(8,128)(2,1)}, bf16[8,128,960]{2,1,0:T(8,128)(2,1)}) custom-call(bf16[128,5120]{1,0:T(8,128)(2,1)} %pad.54.refs_0_, bf16[320,1024]{1,0:T(8,128)(2,1)} %pad.55.refs_1_, bf16[128,1600]{1,0:T(8,128)(2,1)} %fusion.113.refs_2_, ...), custom_call_target="tpu_custom_call" | custom-call | tf_op jit(solution)/shard_map/gather_weights/pallas_call | solution.py:182
  102.2 3.4 fusion.104
  111.2 32.3 %attend.2 = (bf16[2,128,1024]{2,1,0:T(8,128)(2,1)S(1)}, bf16[2,1024,128]{2,1,0:T(8,128)(2,1)}, bf16[2,2,1024,128]{3,2,1,0:T(8,128)(2,1)}, f32[2,1024,128]{2,1,0:T(8,128)}) custom-call(bf16[2,128,1024]{2,1,0:T(8,128)(2,1)S(1)} %pad.59.q_ref, bf16[2,128,640]{2,1,0:T(8,128)(2,1)S(1)} %copy.59.kv_ref), custom_call_target="tpu_custom_call" | custom-call | tf_op jit(solution)/shard_map/attend/pallas_call | solution.py:593
  145.0 5.6 %convolution_bitcast_fusion.1 = f32[256,5120]{1,0:T(8,128)S(1)} fusion(bf16[8,128,5120]{2,1,0:T(8,128)(2,1)} %get-tuple-element.41, bf16[256,8,120]{2,0,1:T(8,128)(2,1)S(1)} %copy.60), kind=kOutput, calls=%fused_computation.8 | convolution fusion | flops 2684354560 | bytes 16220160 | tf_op jit(solution)/shard_map/dot_general | solution.py:865
  150.7 4.8 fusion.67
  155.6 3.9 collective-permute-start
  161.7 6.2 %collective-permute-done = bf16[2,128,960]{1,2,0:T(8,128)(2,1)S(1)} collective-permute-done((bf16[2,128,960]{1,2,0:T(8,128)(2,1)S(1)}, bf16[2,128,960]{1,2,0:T(8,128)(2,1)S(1)}, u32[]{:S(2)}, u32[]{:S(2)}) %collective-permute-start) | collective-permute-done | bytes 491552 | tf_op jit(solution)/shard_map/ppermute | solution.py:956
  171.8 3.4 fusion.102
  176.4 30.0 %attend.3 = (bf16[2,128,1024]{2,1,0:T(8,128)(2,1)S(1)}, bf16[2,1024,128]{2,1,0:T(8,128)(2,1)S(1)}, bf16[2,2,1024,128]{3,2,1,0:T(8,128)(2,1)S(1)}, f32[2,1024,128]{2,1,0:T(8,128)S(1)}) custom-call(bf16[2,128,1024]{2,1,0:T(8,128)(2,1)S(1)} %pad.63.q_ref, bf16[2,128,640]{2,1,0:T(8,128)(2,1)S(1)} %copy.67.kv_ref), custom_call_target="tpu_custom_call" | custom-call | tf_op jit(solution)/shard_map/attend/pallas_call | solution.py:593
  206.4 2.7 multiply_reduce_fusion.6
  213.2 5.9 %convolution_bitcast_fusion = f32[256,5120]{1,0:T(8,128)S(1)} fusion(bf16[8,128,5120]{2,1,0:T(8,128)(2,1)} %get-tuple-element.41, bf16[256,8,120]{2,0,1:T(8,128)(2,1)} %copy.68), kind=kOutput, calls=%fused_computation.7 | convolution fusion | flops 2684354560 | bytes 16220160 | tf_op jit(solution)/shard_map/dot_general | solution.py:865
  219.1 7.1 %multiply_convert_fusion.3 = (bf16[256,2560]{1,0:T(8,128)(2,1)S(1)}, bf16[256,2560]{1,0:T(8,128)(2,1)S(1)}) fusion(f32[256,5120]{1,0:T(8,128)S(1)} %convolution_bitcast_fusion, bf16[2560,1024]{1,0:T(8,128)(2,1)} %bitcast.380, bf16[256,960]{0,1:T(8,128)(2,1)S(1)} %bitcast.363), kind=kOutput, calls=%fused_computation.37 | convolution fusion | flops 1350696960 | bytes 13598720 | tf_op jit(solution)/shard_map/td,fd->tf/dot_general | solution.py:898
  226.3 3.0 fusion.2
  231.8 41.6 %attend_back.2 = (bf16[2,128,1024]{2,1,0:T(8,128)(2,1)S(1)}, bf16[8,2,128,128]{3,2,1,0:T(8,128)(2,1)S(1)}, bf16[2,2,128,128]{3,2,1,0:T(8,128)(2,1)S(1)}) custom-call(bf16[2,128,1024]{2,1,0:T(8,128)(2,1)S(1)} %bitcast.315, bf16[2,1024,128]{2,1,0:T(8,128)(2,1)S(1)} %get-tuple-element.44.q_ref, bf16[2,2,1024,128]{3,2,1,0:T(8,128)(2,1)S(1)} %get-tuple-element.45.kv_ref, ...), custom_call_target="tpu_custom_call" | custom-call | tf_op jit(solution)/shard_map/attend_back/pallas_call | solution.py:765
  277.3 2.5 copy.72
  283.1 2.5 copy.71
  295.0 2.1 fusion.76
  304.0 2.1 copy.88
  306.1 4.5 collective-permute-start.2
  315.7 8.7 %multiply_convert_fusion.1 = (bf16[256,2560]{1,0:T(8,128)(2,1)S(1)}, bf16[256,2560]{1,0:T(8,128)(2,1)S(1)}, bf16[256,2560]{1,0:T(8,128)(2,1)}) fusion(f32[256,5120]{1,0:T(8,128)} %copy-done.18, bf16[2560,1024]{1,0:T(8,128)(2,1)} %bitcast.381, bf16[256,960]{0,1:T(8,128)(2,1)S(1)} %copy_bitcast_fusion.1), kind=kOutput, calls=%fused_computation.35 | convolution fusion | flops 1352663040 | bytes 14909440 | tf_op jit(solution)/shard_map/td,fd->tf/dot_general | solution.py:898
  324.5 3.0 fusion
  327.9 2.7 fusion.151
  330.6 3.9 collective-permute-start.10
  336.3 33.7 %attend_back.3 = (bf16[2,128,1024]{2,1,0:T(8,128)(2,1)S(1)}, bf16[8,2,128,128]{3,2,1,0:T(8,128)(2,1)S(1)}, bf16[2,2,128,128]{3,2,1,0:T(8,128)(2,1)S(1)}) custom-call(bf16[2,128,1024]{2,1,0:T(8,128)(2,1)S(1)} %bitcast.314, bf16[2,1024,128]{2,1,0:T(8,128)(2,1)S(1)} %get-tuple-element.44.q_ref, bf16[2,2,1024,128]{3,2,1,0:T(8,128)(2,1)S(1)} %get-tuple-element.45.kv_ref, ...), custom_call_target="tpu_custom_call" | custom-call | tf_op jit(solution)/shard_map/attend_back/pallas_call | solution.py:765
  382.8 4.3 fusion.59
  387.8 3.9 fusion.46
  403.4 2.5 convolution_convert_fusion.1
  406.4 3.4 pad_maximum_fusion.1
  409.8 4.5 copy.91
  414.3 5.0 convolution_convert_fusion.2.refs_1_
  419.3 6.0 %convolution_convert_fusion.refs_0_ = bf16[8,128,2560]{2,1,0:T(8,128)(2,1)} fusion(bf16[256,2560]{1,0:T(8,128)(2,1)} %collective-permute-done.3, bf16[256,2560]{1,0:T(8,128)(2,1)S(1)} %copy-done.38, bf16[256,8,128]{2,0,1:T(8,128)(2,1)S(1)} %copy-done.46, bf16[256,8,128]{2,0,1:T(8,128)(2,1)S(1)} %copy-done.31), kind=kOutput, calls=%fused_computation.9 | convolution fusion | flops 2694316032 | bytes 8912896 | tf_op jit(solution)/shard_map/tkr,tn->krn/dot_general | solution.py:983
  425.3 104.6 %reduce_gradients.1 = (bf16[128,5120]{1,0:T(8,128)(2,1)S(1)}, bf16[320,1024]{1,0:T(8,128)(2,1)S(1)}, bf16[128,1600]{1,0:T(8,128)(2,1)S(1)}, bf16[128,960]{1,0:T(8,128)(2,1)S(1)}) custom-call(bf16[8,128,2560]{2,1,0:T(8,128)(2,1)} %convolution_convert_fusion.refs_0_, bf16[8,320,512]{2,1,0:T(8,128)(2,1)} %convolution_convert_fusion.2.refs_1_, ...), custom_call_target="tpu_custom_call" | custom-call | tf_op jit(solution)/shard_map/reduce_gradients/pallas_call | solution.py:363
  (330 shorter events, 89.8 us)
Async XLA Ops:
  2.1 165.8 %copy-start.64 = (pred[2]{0:T(512)(128)(4,1)}, pred[2]{0:T(512)(128)(4,1)S(1)}, u32[]{:S(2)}) copy-start(pred[2]{0:T(512)(128)(4,1)S(1)} %compare_and_fusion) | copy-start | bytes 10
  2.2 104.4 %copy-start.66 = (s32[1024]{0:T(1024)}, s32[1024]{0:T(1024)S(1)}, u32[]{:S(2)}) copy-start(s32[1024]{0:T(1024)S(1)} %pad_clamp_fusion) | copy-start | bytes 12292
  107.9 51.6 %copy-start.29 = (f32[2,128,64]{2,1,0:T(8,128)}, f32[2,128,64]{2,1,0:T(8,128)S(1)}, u32[]{:S(2)}) copy-start(f32[2,128,64]{2,1,0:T(8,128)S(1)} %get-tuple-element.114) | copy-start | bytes 196612
  111.2 33.2 %copy-start.12 = (bf16[8,120,960]{2,1,0:T(8,128)(2,1)}, bf16[8,120,960]{2,1,0:T(8,128)(2,1)S(1)}, u32[]{:S(2)}) copy-start(bf16[8,120,960]{2,1,0:T(8,128)(2,1)S(1)} %slice.259) | copy-start | bytes 5529604
  150.6 9.5 %copy-start.15 = (bf16[2,1,128,960]{2,3,1,0:T(8,128)(2,1)S(1)}, bf16[2,1,128,960]{2,3,1,0:T(8,128)(2,1)}, u32[]{:S(2)}) copy-start(bf16[2,1,128,960]{2,3,1,0:T(8,128)(2,1)} %param.19) | copy-start | bytes 1474564
  155.6 12.4 %collective-permute-start = (bf16[2,128,960]{1,2,0:T(8,128)(2,1)S(1)}, bf16[2,128,960]{1,2,0:T(8,128)(2,1)S(1)}, u32[]{:S(2)}, u32[]{:S(2)}) collective-permute-start(bf16[2,128,960]{1,2,0:T(8,128)(2,1)S(1)} %bitcast.364), channel_id=1, source_target_pairs={{0,64},{1,65},{2,66},{3,67},{4,68},{5,69},{6,70},{7,71},{8,72},{9,... | collective-permute-start | bytes 1474568 | tf_op jit(solution)/shard_map/ppermute | solution.py:956
  160.7 9.0 %copy-start.22 = (bf16[2,1,128,960]{2,0,3,1:T(2,128)(2,1)}, bf16[2,1,128,960]{2,0,3,1:T(2,128)(2,1)S(1)}, u32[]{:S(2)}) copy-start(bf16[2,1,128,960]{2,0,3,1:T(2,128)(2,1)S(1)} %copy.69) | copy-start | bytes 1474564
  161.7 136.5 %copy-start.57 = (f32[960]{0:T(1024)}, f32[960]{0:T(1024)S(1)}, u32[]{:S(2)}) copy-start(f32[960]{0:T(1024)S(1)} %mul.462) | copy-start | bytes 11524
  213.2 5.9 %copy-start.47 = (bf16[120,8,2,128]{3,1,2,0:T(8,128)(2,1)S(1)}, bf16[120,8,2,128]{3,1,2,0:T(8,128)(2,1)}, u32[]{:S(2)}) copy-start(bf16[120,8,2,128]{3,1,2,0:T(8,128)(2,1)} %copy.154) | copy-start | bytes 1474564
  213.2 13.1 %slice-start = ((s8[10485760]{0:T(1024)(128)(4,1)}), s8[4194304]{0:T(1024)(128)(4,1)S(1)}, s32[]{:S(2)}) async-start(s8[10485760]{0:T(1024)(128)(4,1)} %bitcast.317), calls=%async_computation | async-start | bytes 8388608
  213.2 13.1 %slice-start.1 = ((s8[10485760]{0:T(1024)(128)(4,1)}), s8[4194304]{0:T(1024)(128)(4,1)S(1)}, s32[]{:S(2)}) async-start(s8[10485760]{0:T(1024)(128)(4,1)} %bitcast.317), calls=%async_computation.1 | async-start | bytes 8388608
  219.1 7.2 %copy-start.18 = (f32[256,5120]{1,0:T(8,128)}, f32[256,5120]{1,0:T(8,128)S(1)}, u32[]{:S(2)}) copy-start(f32[256,5120]{1,0:T(8,128)S(1)} %convolution_bitcast_fusion) | copy-start | bytes 15728644
  219.1 7.2 %slice-start.2 = ((s8[10485760]{0:T(1024)(128)(4,1)}), s8[2097152]{0:T(1024)(128)(4,1)S(1)}, s32[]{:S(2)}) async-start(s8[10485760]{0:T(1024)(128)(4,1)} %bitcast.317), calls=%async_computation.2 | async-start | bytes 4194304
  287.2 7.3 %copy-start.53 = (f32[2,128,64]{1,0,2:T(2,128)S(1)}, f32[2,128,64]{1,0,2:T(2,128)}, u32[]{:S(2)}) copy-start(f32[2,128,64]{1,0,2:T(2,128)} %copy.70) | copy-start | bytes 196612
  299.7 14.9 %collective-permute-start.1 = (bf16[2,128,960]{1,2,0:T(8,128)(2,1)}, bf16[2,128,960]{1,2,0:T(8,128)(2,1)}, u32[]{:S(2)}, u32[]{:S(2)}) collective-permute-start(bf16[2,128,960]{1,2,0:T(8,128)(2,1)} %copy_bitcast_fusion.2), channel_id=1, source_target_pairs={{64,0},{65,1},{66,2},{67,3},{68,4},{69,5},{70,6},{71,7},{72,8},{73... | collective-permute-start | bytes 1474568 | tf_op jit(solution)/shard_map/ppermute | solution.py:956
  303.9 10.6 %copy-start.16 = (bf16[2,1,128,960]{2,3,1,0:T(8,128)(2,1)S(1)}, bf16[2,1,128,960]{2,3,1,0:T(8,128)(2,1)}, u32[]{:S(2)}) copy-start(bf16[2,1,128,960]{2,3,1,0:T(8,128)(2,1)} %param.19) | copy-start | bytes 1474564
  306.1 91.4 %collective-permute-start.2 = (bf16[256,1024]{0,1:T(8,128)(2,1)}, bf16[256,1024]{0,1:T(8,128)(2,1)}, u32[]{:S(2)}, u32[]{:S(2)}) collective-permute-start(bf16[256,1024]{0,1:T(8,128)(2,1)} %bitcast.362), channel_id=1, source_target_pairs={{0,8},{8,0},{16,24},{24,16},{32,40},{40,32},{48,56},{56,48},{1,9},... | collective-permute-start | bytes 1572872 | tf_op jit(solution)/shard_map/ppermute | solution.py:961
  310.6 13.9 %slice-start.3 = ((s8[10485760]{0:T(1024)(128)(4,1)}), s8[4194304]{0:T(1024)(128)(4,1)S(1)}, s32[]{:S(2)}) async-start(s8[10485760]{0:T(1024)(128)(4,1)} %bitcast.319), calls=%async_computation.3 | async-start | bytes 8388608
  315.7 8.7 %copy-start.36 = (bf16[256,960]{0,1:T(8,128)(2,1)}, bf16[256,960]{0,1:T(8,128)(2,1)S(1)}, u32[]{:S(2)}) copy-start(bf16[256,960]{0,1:T(8,128)(2,1)S(1)} %copy_bitcast_fusion.1) | copy-start | bytes 1474564
  315.7 8.7 %slice-start.4 = ((s8[10485760]{0:T(1024)(128)(4,1)}), s8[4194304]{0:T(1024)(128)(4,1)S(1)}, s32[]{:S(2)}) async-start(s8[10485760]{0:T(1024)(128)(4,1)} %bitcast.319), calls=%async_computation.4 | async-start | bytes 8388608
  315.7 8.7 %slice-start.5 = ((s8[10485760]{0:T(1024)(128)(4,1)}), s8[2097152]{0:T(1024)(128)(4,1)S(1)}, s32[]{:S(2)}) async-start(s8[10485760]{0:T(1024)(128)(4,1)} %bitcast.319), calls=%async_computation.5 | async-start | bytes 4194304
  327.5 7.0 %copy-start.14 = (bf16[8,120,960]{2,1,0:T(8,128)(2,1)S(1)}, bf16[8,120,960]{2,1,0:T(8,128)(2,1)}, u32[]{:S(2)}) copy-start(bf16[8,120,960]{2,1,0:T(8,128)(2,1)} %copy-done.12) | copy-start | bytes 5529604
  330.6 69.6 %collective-permute-start.10 = (bf16[256,960]{0,1:T(8,128)(2,1)}, bf16[256,960]{0,1:T(8,128)(2,1)}, u32[]{:S(2)}, u32[]{:S(2)}) collective-permute-start(bf16[256,960]{0,1:T(8,128)(2,1)} %fusion.151), channel_id=1, source_target_pairs={{0,8},{8,0},{16,24},{24,16},{32,40},{40,32},{48,56},{56,48},{1,9},... | collective-permute-start | bytes 1474568 | tf_op jit(solution)/shard_map/ppermute | solution.py:961
  382.1 5.7 %copy-start.40 = (bf16[256,2560]{1,0:T(8,128)(2,1)S(1)}, bf16[256,2560]{1,0:T(8,128)(2,1)}, u32[]{:S(2)}) copy-start(bf16[256,2560]{1,0:T(8,128)(2,1)} %copy-done.39) | copy-start | bytes 3932164
  382.1 24.3 %collective-permute-start.4 = (bf16[256,2560]{1,0:T(8,128)(2,1)}, bf16[256,2560]{1,0:T(8,128)(2,1)}, u32[]{:S(2)}, u32[]{:S(2)}) collective-permute-start(bf16[256,2560]{1,0:T(8,128)(2,1)} %get-tuple-element.83), channel_id=1, source_target_pairs={{0,8},{8,0},{16,24},{24,16},{32,40},{40,32},{48,56},{56,48},{1,9},... | collective-permute-start | bytes 3932168 | tf_op jit(solution)/shard_map/ppermute | solution.py:961
  387.1 8.3 %collective-permute-start.8 = (f32[2,960]{1,0:T(2,128)S(1)}, f32[2,960]{1,0:T(2,128)S(1)}, u32[]{:S(2)}, u32[]{:S(2)}) collective-permute-start(f32[2,960]{1,0:T(2,128)S(1)} %pad_maximum_fusion.9), channel_id=1, source_target_pairs={{0,8},{8,0},{16,24},{24,16},{32,40},{40,32},{48,56},{56,48},{1,9},... | collective-permute-start | bytes 23048 | tf_op jit(solution)/shard_map/ppermute | solution.py:961
  387.4 15.4 %collective-permute-start.7 = (bf16[256,1600]{0,1:T(8,128)(2,1)}, bf16[256,1600]{0,1:T(8,128)(2,1)}, u32[]{:S(2)}, u32[]{:S(2)}) collective-permute-start(bf16[256,1600]{0,1:T(8,128)(2,1)} %pad_maximum_fusion.4), channel_id=1, source_target_pairs={{0,8},{8,0},{16,24},{24,16},{32,40},{40,32},{48,56},{56,48},{1,9},... | collective-permute-start | bytes 2457608 | tf_op jit(solution)/shard_map/ppermute | solution.py:961
  395.5 4.6 collective-permute-start.9
  397.5 6.0 %copy-start.35 = (bf16[256,960]{0,1:T(8,128)(2,1)S(1)}, bf16[256,960]{0,1:T(8,128)(2,1)}, u32[]{:S(2)}) copy-start(bf16[256,960]{0,1:T(8,128)(2,1)} %copy-done.34) | copy-start | bytes 1474564
  397.5 5.2 collective-permute-start.6
  400.1 14.2 %collective-permute-start.5 = (bf16[256,512]{0,1:T(8,128)(2,1)}, bf16[256,512]{0,1:T(8,128)(2,1)}, u32[]{:S(2)}, u32[]{:S(2)}) collective-permute-start(bf16[256,512]{0,1:T(8,128)(2,1)} %get-tuple-element.103), channel_id=1, source_target_pairs={{0,8},{8,0},{16,24},{24,16},{32,40},{40,32},{48,56},{56,48},{1,9},... | collective-permute-start | bytes 786440 | tf_op jit(solution)/shard_map/ppermute | solution.py:961
  400.2 19.1 %collective-permute-start.3 = (bf16[256,2560]{1,0:T(8,128)(2,1)}, bf16[256,2560]{1,0:T(8,128)(2,1)}, u32[]{:S(2)}, u32[]{:S(2)}) collective-permute-start(bf16[256,2560]{1,0:T(8,128)(2,1)} %get-tuple-element.85), channel_id=1, source_target_pairs={{0,8},{8,0},{16,24},{24,16},{32,40},{40,32},{48,56},{56,48},{1,9},... | collective-permute-start | bytes 3932168 | tf_op jit(solution)/shard_map/ppermute | solution.py:961
  (58 other events, 171.0 us)

commit v3 on v2

--- a/solution.py
+++ b/solution.py
@@ -105,6 +105,12 @@
     return (0, rows) if part == "f" else (part * (rows // 2), rows // 2)
 
 
+SPREAD = 0
+UPWARD = (0, 1, 3, 5, 7)
+PLAIN_EDGES = 22
+SPREAD_EDGES = 88
+
+
 def gather_kernel(*refs):
     count = len(SHAPES)
     shards, outs = refs[:count], refs[count : 2 * count]
@@ -116,35 +122,58 @@
     def owner(column, step):
         return ((x + column) % 2) * 4 + (y + step) % 4
 
-    def view(array, column, step, part, which):
+    def index(array, part, which, plane):
         start, rows = part_rows(SHAPES[array], part)
-        return outs[array].at[(owner(column, step),) + half_view(SHAPES[array], which, start, rows)]
+        if array == SPREAD:
+            quarter = half_shape(SHAPES[array])[0] // 4
+            start, rows = plane * quarter + start // 4, rows // 4
+        return half_view(SHAPES[array], which, start, rows)
+
+    def view(array, column, step, part, which, plane):
+        return outs[array].at[(owner(column, step),) + index(array, part, which, plane)]
+
+    def received(edge):
+        group, base = edge // 11, edge % 11
+        peer, column, step, part = GATHER[base]
+        column, step = seen_by_receiver(peer, column, step)
+        away = {0: 0, 1: 0, 2: 3, 3: 1, 4: 2, 5: 3, 6: 1, 7: 2}[group]
+        return column, step, part, away
+
+    def peer_of(edge):
+        group, base = edge // 11, edge % 11
+        if group == 0:
+            return GATHER[base][0]
+        if group in (1, 5, 6, 7):
+            return "C"
+        return {2: "Z1", 3: "Z3", 4: "Z1" if base in UPWARD else "Z3"}[group]
 
     def copy(array, edge):
-        peer, column, step, part = GATHER[edge % 11]
-        if edge < 11:
-            target = view(array, column, step, part, core)
-            source = target
-            if (column, step) == (0, 0):
-                start, rows = part_rows(SHAPES[array], part)
-                source = shards[array].at[half_view(SHAPES[array], core, start, rows)]
+        group, base = edge // 11, edge % 11
+        if group == 0:
+            _, column, step, part = GATHER[base]
+            away = 0
         else:
-            peer, (column, step) = "C", seen_by_receiver(peer, column, step)
-            source = target = view(array, column, step, part, core)
+            column, step, part, away = received(edge)
+            if group in (2, 3):
+                away = 0
+            elif group == 4:
+                away = 3 if base in UPWARD else 1
+        target = source = view(array, column, step, part, core, (z + away) % 4)
+        if group == 0 and (column, step) == (0, 0):
+            source = shards[array].at[index(array, part, core, z)]
         return pltpu.make_async_remote_copy(
             src_ref=source,
             dst_ref=target,
             send_sem=send_sem.at[array, edge],
             recv_sem=recv_sem.at[array, edge],
-            device_id=ids[peer],
+            device_id=ids[peer_of(edge)],
             device_id_type=MESH,
         )
 
     def wait_for(array, edge):
-        peer, column, step, part = GATHER[edge % 11]
-        column, step = seen_by_receiver(peer, column, step)
-        which = core if edge < 11 else 1 - core
-        landed = view(array, column, step, part, which)
+        column, step, part, away = received(edge)
+        which = 1 - core if edge // 11 in (1, 5, 6, 7) else core
+        landed = view(array, column, step, part, which, (z + away) % 4)
         pltpu.make_async_remote_copy(
             src_ref=landed,
             dst_ref=landed,
@@ -154,7 +183,17 @@
             device_id_type=MESH,
         ).wait_recv()
 
-    greet(ids, ("X", "Yp", "Ym", "C"))
+    def within_plane(array):
+        for edge in GATHER_ORDER:
+            wait_for(array, edge)
+            for later in GATHER_NEXT.get(edge, ()):
+                copy(array, later).start()
+            if array == SPREAD:
+                copy(array, 22 + edge).start()
+                copy(array, 33 + edge).start()
+            copy(array, 11 + edge).start()
+
+    greet(ids, ("X", "Yp", "Ym", "C", "Z1", "Z3"))
     own = [
         pltpu.make_async_copy(shards[array], outs[array].at[mine], local_sem.at[array])
         for array in range(count)
@@ -163,16 +202,25 @@
         for edge in (0, 1, 2):
             copy(array, edge).start()
         own[array].start()
+    within_plane(SPREAD)
+    within_plane(1)
+    for edge in GATHER_ORDER:
+        for group in (2, 3):
+            wait_for(SPREAD, 11 * group + edge)
+            if (group == 2) == (edge in UPWARD):
+                copy(SPREAD, 44 + edge).start()
+            copy(SPREAD, 11 * (group + 3) + edge).start()
+    within_plane(2)
+    within_plane(3)
+    for edge in GATHER_ORDER:
+        wait_for(SPREAD, 44 + edge)
+        copy(SPREAD, 77 + edge).start()
     for array in range(count):
-        for edge in GATHER_ORDER:
-            wait_for(array, edge)
-            for later in GATHER_NEXT.get(edge, ()):
-                copy(array, later).start()
-            copy(array, 11 + edge).start()
-    for array in range(count):
-        for edge in range(11):
-            wait_for(array, 11 + edge)
-        for edge in range(22):
+        last = SPREAD_EDGES if array == SPREAD else PLAIN_EDGES
+        for edge in range(last):
+            if edge // 11 in (1, 5, 6, 7):
+                wait_for(array, edge)
+        for edge in range(last):
             copy(array, edge).wait_send()
         own[array].wait()
 
@@ -190,8 +238,8 @@
         out_specs=[ANY] * count,
         scratch_shapes=[
             pltpu.SemaphoreType.DMA((count,)),
-            pltpu.SemaphoreType.DMA((count, 22)),
-            pltpu.SemaphoreType.DMA((count, 22)),
+            pltpu.SemaphoreType.DMA((count, SPREAD_EDGES)),
+            pltpu.SemaphoreType.DMA((count, SPREAD_EDGES)),
         ],
         compiler_params=pltpu.CompilerParams(collective_id=0, has_side_effects=True),
     )(*shards)
@@ -211,6 +259,8 @@
     ("X", 1, 0, "f", (5, 7)),
 )
 REDUCE_STAGES = ((0, 1, 2, 3, 4, 5), (6, 7), (8, 9, 10))
+SHARD_ORDER = ((0, 2), (1, 2), (1, 3), (1, 1), (0, 1), (0, 3), (1, 0), (0, 0))
+REDUCE_EDGES = 45
 
 
 def reduce_kernel(*refs):
@@ -221,7 +271,7 @@
     wholes = scratch[count : 2 * count]
     parts = scratch[2 * count : 3 * count]
     quarters = scratch[3 * count : 4 * count]
-    local_sem, send_sem, recv_sem = scratch[4 * count :]
+    rounds, local_sem, send_sem, recv_sem = scratch[4 * count :]
     z, core, x, y = places()
     ids = peer_ids()
     mine = x * 4 + y
@@ -229,9 +279,15 @@
     def owner(column, step):
         return ((x + column) % 2) * 4 + (y + step) % 4
 
+    def piece_rows(array, part):
+        start, rows = part_rows(SHAPES[array], part)
+        if array == SPREAD:
+            start, rows = pl.multiple_of(z * (half_shape(SHAPES[array])[0] // 4) + start // 4, 16), rows // 4
+        return start, rows
+
     def piece(array, edge):
         _, column, step, part, _ = REDUCE[edge]
-        start, rows = part_rows(SHAPES[array], part)
+        start, rows = piece_rows(array, part)
         return totals[array].at[owner(column, step), pl.ds(start, rows), :]
 
     def slot(array, edge):
@@ -269,13 +325,20 @@
             start, rows = quarter(array, z)
             source = totals[array].at[mine, pl.ds(start, rows), :]
             target = out_view(array, z, core)
-        else:
+        elif edge < 21:
             peer = "C"
             at = (z + edge - 17) % 4
             source = target = out_view(array, at, core)
             if edge == 17:
                 start, rows = quarter(array, z)
                 source = totals[array].at[mine, pl.ds(start, rows), :]
+        else:
+            kind, shard = (edge - 21) // 8, (edge - 21) % 8
+            away = (2, 1, 3)[kind]
+            peer = ("Z1" if shard % 2 == 0 else "Z3", "Z1", "Z3")[kind]
+            start, rows = quarter(array, (z + away) % 4)
+            source = totals[array].at[owner(*SHARD_ORDER[shard]), pl.ds(start, rows), :]
+            target = rounds.at[edge - 21]
         return pltpu.make_async_remote_copy(
             src_ref=source,
             dst_ref=target,
@@ -292,8 +355,10 @@
             landed = quarters[array].at[edge - 11]
         elif edge < 17:
             landed = out_view(array, (z + 4 - (edge - 13)) % 4, core)
+        elif edge < 21:
+            landed = out_view(array, (z + edge - 17) % 4, 1 - core)
         else:
-            landed = out_view(array, (z + edge - 17) % 4, 1 - core)
+            landed = rounds.at[edge - 21]
         pltpu.make_async_remote_copy(
             src_ref=landed,
             dst_ref=landed,
@@ -307,9 +372,23 @@
         wait_for(array, edge)
         peer, column, step, part, _ = REDUCE[edge]
         column, step = seen_by_receiver(peer, column, step)
-        start, rows = part_rows(SHAPES[array], part)
+        start, rows = piece_rows(array, part)
         add(array, owner(column, step), start, rows, slot(array, edge))
 
+    def receive_round(kind, shard):
+        edge = 21 + 8 * kind + shard
+        wait_for(SPREAD, edge)
+        away = 0 if kind > 0 else (1 if shard % 2 == 0 else 3)
+        start, rows = quarter(SPREAD, (z + away) % 4)
+        add(SPREAD, owner(*SHARD_ORDER[shard]), start, rows, rounds.at[edge - 21])
+
+    def stage(array, number):
+        for edge in REDUCE_STAGES[number]:
+            for earlier in REDUCE[edge][4]:
+                receive(array, earlier)
+            copy(array, edge).start()
+
+    plain = [array for array in range(count) if array != SPREAD]
     loads = [
         pltpu.make_async_copy(terms[array], totals[array], local_sem.at[array])
         for array in range(count)
@@ -317,23 +396,40 @@
     for load in loads:
         load.start()
     greet(ids, ("X", "Yp", "Ym", "C", "Z1", "Z2", "Z3"))
-    for stage in REDUCE_STAGES:
-        for array in range(count):
-            if stage == REDUCE_STAGES[0]:
-                loads[array].wait()
-            for edge in stage:
-                for earlier in REDUCE[edge][4]:
-                    receive(array, earlier)
-                copy(array, edge).start()
-    for array in range(count):
+    loads[SPREAD].wait()
+    for shard in range(SHARDS):
+        copy(SPREAD, 21 + shard).start()
+    for array in plain:
+        loads[array].wait()
+        stage(array, 0)
+    for shard in range(SHARDS):
+        receive_round(0, shard)
+        copy(SPREAD, 29 + shard).start()
+        copy(SPREAD, 37 + shard).start()
+    for array in plain:
+        stage(array, 1)
+    for shard in range(4):
+        receive_round(1, shard)
+        receive_round(2, shard)
+    stage(SPREAD, 0)
+    for shard in range(4, SHARDS):
+        receive_round(1, shard)
+        receive_round(2, shard)
+    for array in plain:
+        stage(array, 2)
+    stage(SPREAD, 1)
+    stage(SPREAD, 2)
+    for array in plain:
         for edge in (8, 9, 10):
             receive(array, edge)
         for edge in (11, 12, 13):
             copy(array, edge).start()
+    for edge in (8, 9, 10):
+        receive(SPREAD, edge)
     stores = []
     for array in range(count):
         start, rows = quarter(array, z)
-        for edge in (11, 12, 13):
+        for edge in (11, 12, 13) if array != SPREAD else ():
             wait_for(array, edge)
             add(array, mine, start, rows, quarters[array].at[edge - 11])
         for edge in (14, 15, 16, 17):
@@ -352,14 +448,18 @@
     for array in range(count):
         for edge in range(17, 21):
             wait_for(array, edge)
-        for edge in range(21):
-            copy(array, edge).wait_send()
+        for edge in range(REDUCE_EDGES):
+            if (edge not in (11, 12, 13)) if array == SPREAD else (edge < 21):
+                copy(array, edge).wait_send()
         stores[array].wait()
 
 
 def reduce_gradients(terms):
     count = len(SHAPES)
     halves = [half_shape(shape) for shape in SHAPES]
+    pieces = [
+        (half[0] // 4, half[1]) if array == SPREAD else half for array, half in enumerate(halves)
+    ]
     return pl.pallas_call(
         reduce_kernel,
         name="reduce_gradients",
@@ -369,13 +469,14 @@
         in_specs=[ANY] * count,
         out_specs=[ANY] * count,
         scratch_shapes=[pltpu.VMEM((SHARDS,) + half, jnp.bfloat16) for half in halves]
-        + [pltpu.VMEM((3,) + half, jnp.bfloat16) for half in halves]
-        + [pltpu.VMEM((8, half[0] // 2, half[1]), jnp.bfloat16) for half in halves]
+        + [pltpu.VMEM((3, half[0], half[1]), jnp.bfloat16) for half in pieces]
+        + [pltpu.VMEM((8, half[0] // 2, half[1]), jnp.bfloat16) for half in pieces]
         + [pltpu.VMEM((3, half[0] // 4, half[1]), jnp.bfloat16) for half in halves]
         + [
+            pltpu.VMEM((3 * SHARDS,) + pieces[SPREAD], jnp.bfloat16),
             pltpu.SemaphoreType.DMA((count,)),
-            pltpu.SemaphoreType.DMA((count, 21)),
-            pltpu.SemaphoreType.DMA((count, 21)),
+            pltpu.SemaphoreType.DMA((count, REDUCE_EDGES)),
+            pltpu.SemaphoreType.DMA((count, REDUCE_EDGES)),
         ],
         compiler_params=pltpu.CompilerParams(
             collective_id=1, has_side_effects=True, vmem_limit_bytes=48 * 2**20

time: 536 us -> 522 us (0.974); the launches traced: 535 us -> 514 us
  Pallas kernels: 336 us -> 316 us
    pallas_call x2, Pallas kernels: 75.3 us -> 63.2 us  [attend_back(): pl.pallas_call(attend_back_kernel, name='attend_back', out_shape=[jax.Sha...]
    pallas_call x1, Pallas kernels: 105 us -> 97.4 us  [reduce_gradients(): pl.pallas_call(reduce_kernel, name='reduce_gradients', out_shape=[jax.Sha...]
  transfers between devices with their start and end apart: 11 -> 11, of which waited for: 1 -> 1; matrix products, arithmetic and copies ran while one was open for 14% -> 14% of each run, Pallas kernels for 6% -> 7%
where the time goes in v3:
time: 522 us; the launch traced here: 514 us
  Pallas kernels  316 us (61%)
  matrix products  73 us (14%)
  local copies, waits for them, and re-layouts  62.5 us (12%)
  other arithmetic  39.4 us (8%)
  starting transfers between devices  15.7 us (3%)
    pallas_call x1, Pallas kernels, reduce_gradients(): pl.pallas_call(reduce_kernel, name='reduce_gradients', out_shape=[jax.Sha...  97.4 us
    pallas_call x1, Pallas kernels, gather_weights(): pl.pallas_call(gather_kernel, name='gather_weights', out_shape=[jax.Shape...  92.4 us
    pallas_call x2, Pallas kernels, attend_back(): pl.pallas_call(attend_back_kernel, name='attend_back', out_shape=[jax.Sha...  63.2 us
    pallas_call x2, Pallas kernels, attend(): pl.pallas_call(attend_kernel, name='attend', out_shape=[jax.ShapeDtypeStr...  62.7 us
    dot_general x2, matrix products, backward_layer(): jnp.einsum('td,fd->tf', down_in, down_weight, preferred_element_type=jnp....  15.8 us
    dot_general x4, matrix products, term(): jnp.einsum('tkr,tn->krn', split, right, preferred_element_type=jnp.float32)  15.3 us
    dot_general x2, matrix products, forward_layer(): gated = jnp.dot(second_norm, gate_up, preferred_element_type=jnp.float32)  11.5 us
    unnamed x165, local copies, waits for them, and re-layouts  11.4 us
  transfers between devices with their start and end apart: 11, of which 1 were waited for; matrix products, arithmetic and copies ran while one was open for 14% of the time, Pallas kernels for 7%

profile of v3, /device:TPU:1, one launch (start us, length us, event | category | flops | bytes accessed | tf_op | source)
XLA Modules:
  0.0 514.1 jit_solution(9078205131147172200)
XLA Ops:
  7.3 92.4 %gather_weights.1 = (bf16[8,128,5120]{2,1,0:T(8,128)(2,1)}, bf16[8,320,1024]{2,1,0:T(8,128)(2,1)}, bf16[8,128,1600]{2,1,0:T(8,128)(2,1)}, bf16[8,128,960]{2,1,0:T(8,128)(2,1)}) custom-call(bf16[128,5120]{1,0:T(8,128)(2,1)} %pad.54.refs_0_, bf16[320,1024]{1,0:T(8,128)(2,1)} %pad.55.refs_1_, bf16[128,1600]{1,0:T(8,128)(2,1)} %fusion.113.refs_2_, ...), custom_call_target="tpu_custom_call" | custom-call | tf_op jit(solution)/shard_map/gather_weights/pallas_call | solution.py:230
  101.2 3.4 fusion.104
  110.2 31.1 %attend.2 = (bf16[2,128,1024]{2,1,0:T(8,128)(2,1)S(1)}, bf16[2,1024,128]{2,1,0:T(8,128)(2,1)}, bf16[2,2,1024,128]{3,2,1,0:T(8,128)(2,1)}, f32[2,1024,128]{2,1,0:T(8,128)}) custom-call(bf16[2,128,1024]{2,1,0:T(8,128)(2,1)S(1)} %pad.59.q_ref, bf16[2,128,640]{2,1,0:T(8,128)(2,1)S(1)} %copy.59.kv_ref), custom_call_target="tpu_custom_call" | custom-call | tf_op jit(solution)/shard_map/attend/pallas_call | solution.py:694
  142.9 5.6 %convolution_bitcast_fusion.1 = f32[256,5120]{1,0:T(8,128)S(1)} fusion(bf16[8,128,5120]{2,1,0:T(8,128)(2,1)} %get-tuple-element.41, bf16[256,8,120]{2,0,1:T(8,128)(2,1)S(1)} %copy.60), kind=kOutput, calls=%fused_computation.8 | convolution fusion | flops 2684354560 | bytes 16220160 | tf_op jit(solution)/shard_map/dot_general | solution.py:966
  148.5 4.8 fusion.67
  153.4 4.3 collective-permute-start
  160.0 5.1 collective-permute-done
  168.9 3.4 fusion.102
  173.5 31.6 %attend.3 = (bf16[2,128,1024]{2,1,0:T(8,128)(2,1)S(1)}, bf16[2,1024,128]{2,1,0:T(8,128)(2,1)S(1)}, bf16[2,2,1024,128]{3,2,1,0:T(8,128)(2,1)S(1)}, f32[2,1024,128]{2,1,0:T(8,128)S(1)}) custom-call(bf16[2,128,1024]{2,1,0:T(8,128)(2,1)S(1)} %pad.63.q_ref, bf16[2,128,640]{2,1,0:T(8,128)(2,1)S(1)} %copy.67.kv_ref), custom_call_target="tpu_custom_call" | custom-call | tf_op jit(solution)/shard_map/attend/pallas_call | solution.py:694
  205.1 2.7 multiply_reduce_fusion.6
  211.9 5.9 %convolution_bitcast_fusion = f32[256,5120]{1,0:T(8,128)S(1)} fusion(bf16[8,128,5120]{2,1,0:T(8,128)(2,1)} %get-tuple-element.41, bf16[256,8,120]{2,0,1:T(8,128)(2,1)} %copy.68), kind=kOutput, calls=%fused_computation.7 | convolution fusion | flops 2684354560 | bytes 16220160 | tf_op jit(solution)/shard_map/dot_general | solution.py:966
  217.8 7.1 %multiply_convert_fusion.3 = (bf16[256,2560]{1,0:T(8,128)(2,1)S(1)}, bf16[256,2560]{1,0:T(8,128)(2,1)S(1)}) fusion(f32[256,5120]{1,0:T(8,128)S(1)} %convolution_bitcast_fusion, bf16[2560,1024]{1,0:T(8,128)(2,1)} %bitcast.380, bf16[256,960]{0,1:T(8,128)(2,1)S(1)} %bitcast.363), kind=kOutput, calls=%fused_computation.37 | convolution fusion | flops 1350696960 | bytes 13598720 | tf_op jit(solution)/shard_map/td,fd->tf/dot_general | solution.py:999
  225.0 3.0 fusion.2
  230.5 29.0 %attend_back.2 = (bf16[2,128,1024]{2,1,0:T(8,128)(2,1)S(1)}, bf16[8,2,128,128]{3,2,1,0:T(8,128)(2,1)S(1)}, bf16[2,2,128,128]{3,2,1,0:T(8,128)(2,1)S(1)}) custom-call(bf16[2,128,1024]{2,1,0:T(8,128)(2,1)S(1)} %bitcast.315, bf16[2,1024,128]{2,1,0:T(8,128)(2,1)S(1)} %get-tuple-element.44.q_ref, bf16[2,2,1024,128]{3,2,1,0:T(8,128)(2,1)S(1)} %get-tuple-element.45.kv_ref, ...), custom_call_target="tpu_custom_call" | custom-call | tf_op jit(solution)/shard_map/attend_back/pallas_call | solution.py:866
  263.4 2.5 copy.72
  269.2 2.5 copy.71
  281.1 2.1 fusion.76
  290.1 2.1 copy.88
  292.2 4.5 collective-permute-start.2
  301.8 8.7 %multiply_convert_fusion.1 = (bf16[256,2560]{1,0:T(8,128)(2,1)S(1)}, bf16[256,2560]{1,0:T(8,128)(2,1)S(1)}, bf16[256,2560]{1,0:T(8,128)(2,1)}) fusion(f32[256,5120]{1,0:T(8,128)} %copy-done.18, bf16[2560,1024]{1,0:T(8,128)(2,1)} %bitcast.381, bf16[256,960]{0,1:T(8,128)(2,1)S(1)} %copy_bitcast_fusion.1), kind=kOutput, calls=%fused_computation.35 | convolution fusion | flops 1352663040 | bytes 14909440 | tf_op jit(solution)/shard_map/td,fd->tf/dot_general | solution.py:999
  310.6 3.0 fusion
  314.1 2.7 fusion.151
  316.7 3.1 collective-permute-start.10
  321.7 34.2 %attend_back.3 = (bf16[2,128,1024]{2,1,0:T(8,128)(2,1)S(1)}, bf16[8,2,128,128]{3,2,1,0:T(8,128)(2,1)S(1)}, bf16[2,2,128,128]{3,2,1,0:T(8,128)(2,1)S(1)}) custom-call(bf16[2,128,1024]{2,1,0:T(8,128)(2,1)S(1)} %bitcast.314, bf16[2,1024,128]{2,1,0:T(8,128)(2,1)S(1)} %get-tuple-element.44.q_ref, bf16[2,2,1024,128]{3,2,1,0:T(8,128)(2,1)S(1)} %get-tuple-element.45.kv_ref, ...), custom_call_target="tpu_custom_call" | custom-call | tf_op jit(solution)/shard_map/attend_back/pallas_call | solution.py:866
  368.6 4.3 fusion.59
  373.7 3.9 fusion.46
  389.3 2.5 convolution_convert_fusion.1
  392.3 3.4 pad_maximum_fusion.1
  395.7 4.5 copy.91
  400.2 5.0 convolution_convert_fusion.2.refs_1_
  405.2 6.0 %convolution_convert_fusion.refs_0_ = bf16[8,128,2560]{2,1,0:T(8,128)(2,1)} fusion(bf16[256,2560]{1,0:T(8,128)(2,1)} %collective-permute-done.3, bf16[256,2560]{1,0:T(8,128)(2,1)S(1)} %copy-done.38, bf16[256,8,128]{2,0,1:T(8,128)(2,1)S(1)} %copy-done.46, bf16[256,8,128]{2,0,1:T(8,128)(2,1)S(1)} %copy-done.31), kind=kOutput, calls=%fused_computation.9 | convolution fusion | flops 2694316032 | bytes 8912896 | tf_op jit(solution)/shard_map/tkr,tn->krn/dot_general | solution.py:1084
  411.1 97.4 %reduce_gradients.1 = (bf16[128,5120]{1,0:T(8,128)(2,1)S(1)}, bf16[320,1024]{1,0:T(8,128)(2,1)S(1)}, bf16[128,1600]{1,0:T(8,128)(2,1)S(1)}, bf16[128,960]{1,0:T(8,128)(2,1)S(1)}) custom-call(bf16[8,128,2560]{2,1,0:T(8,128)(2,1)} %convolution_convert_fusion.refs_0_, bf16[8,320,512]{2,1,0:T(8,128)(2,1)} %convolution_convert_fusion.2.refs_1_, ...), custom_call_target="tpu_custom_call" | custom-call | tf_op jit(solution)/shard_map/reduce_gradients/pallas_call | solution.py:463
  (330 shorter events, 89.8 us)
Async XLA Ops:
  2.1 162.9 %copy-start.64 = (pred[2]{0:T(512)(128)(4,1)}, pred[2]{0:T(512)(128)(4,1)S(1)}, u32[]{:S(2)}) copy-start(pred[2]{0:T(512)(128)(4,1)S(1)} %compare_and_fusion) | copy-start | bytes 10
  2.2 103.4 %copy-start.66 = (s32[1024]{0:T(1024)}, s32[1024]{0:T(1024)S(1)}, u32[]{:S(2)}) copy-start(s32[1024]{0:T(1024)S(1)} %pad_clamp_fusion) | copy-start | bytes 12292
  106.9 50.9 %copy-start.29 = (f32[2,128,64]{2,1,0:T(8,128)}, f32[2,128,64]{2,1,0:T(8,128)S(1)}, u32[]{:S(2)}) copy-start(f32[2,128,64]{2,1,0:T(8,128)S(1)} %get-tuple-element.114) | copy-start | bytes 196612
  110.2 32.1 %copy-start.12 = (bf16[8,120,960]{2,1,0:T(8,128)(2,1)}, bf16[8,120,960]{2,1,0:T(8,128)(2,1)S(1)}, u32[]{:S(2)}) copy-start(bf16[8,120,960]{2,1,0:T(8,128)(2,1)S(1)} %slice.259) | copy-start | bytes 5529604
  148.5 9.9 %copy-start.15 = (bf16[2,1,128,960]{2,3,1,0:T(8,128)(2,1)S(1)}, bf16[2,1,128,960]{2,3,1,0:T(8,128)(2,1)}, u32[]{:S(2)}) copy-start(bf16[2,1,128,960]{2,3,1,0:T(8,128)(2,1)} %param.19) | copy-start | bytes 1474564
  153.4 11.6 %collective-permute-start = (bf16[2,128,960]{1,2,0:T(8,128)(2,1)S(1)}, bf16[2,128,960]{1,2,0:T(8,128)(2,1)S(1)}, u32[]{:S(2)}, u32[]{:S(2)}) collective-permute-start(bf16[2,128,960]{1,2,0:T(8,128)(2,1)S(1)} %bitcast.364), channel_id=1, source_target_pairs={{0,64},{1,65},{2,66},{3,67},{4,68},{5,69},{6,70},{7,71},{8,72},{9,... | collective-permute-start | bytes 1474568 | tf_op jit(solution)/shard_map/ppermute | solution.py:1057
  159.0 7.9 %copy-start.22 = (bf16[2,1,128,960]{2,0,3,1:T(2,128)(2,1)}, bf16[2,1,128,960]{2,0,3,1:T(2,128)(2,1)S(1)}, u32[]{:S(2)}) copy-start(bf16[2,1,128,960]{2,0,3,1:T(2,128)(2,1)S(1)} %copy.69) | copy-start | bytes 1474564
  160.0 124.4 %copy-start.57 = (f32[960]{0:T(1024)}, f32[960]{0:T(1024)S(1)}, u32[]{:S(2)}) copy-start(f32[960]{0:T(1024)S(1)} %mul.462) | copy-start | bytes 11524
  211.9 5.9 %copy-start.47 = (bf16[120,8,2,128]{3,1,2,0:T(8,128)(2,1)S(1)}, bf16[120,8,2,128]{3,1,2,0:T(8,128)(2,1)}, u32[]{:S(2)}) copy-start(bf16[120,8,2,128]{3,1,2,0:T(8,128)(2,1)} %copy.154) | copy-start | bytes 1474564
  211.9 13.1 %slice-start = ((s8[10485760]{0:T(1024)(128)(4,1)}), s8[4194304]{0:T(1024)(128)(4,1)S(1)}, s32[]{:S(2)}) async-start(s8[10485760]{0:T(1024)(128)(4,1)} %bitcast.317), calls=%async_computation | async-start | bytes 8388608
  211.9 13.1 %slice-start.1 = ((s8[10485760]{0:T(1024)(128)(4,1)}), s8[4194304]{0:T(1024)(128)(4,1)S(1)}, s32[]{:S(2)}) async-start(s8[10485760]{0:T(1024)(128)(4,1)} %bitcast.317), calls=%async_computation.1 | async-start | bytes 8388608
  217.8 7.2 %copy-start.18 = (f32[256,5120]{1,0:T(8,128)}, f32[256,5120]{1,0:T(8,128)S(1)}, u32[]{:S(2)}) copy-start(f32[256,5120]{1,0:T(8,128)S(1)} %convolution_bitcast_fusion) | copy-start | bytes 15728644
  217.8 7.2 %slice-start.2 = ((s8[10485760]{0:T(1024)(128)(4,1)}), s8[2097152]{0:T(1024)(128)(4,1)S(1)}, s32[]{:S(2)}) async-start(s8[10485760]{0:T(1024)(128)(4,1)} %bitcast.317), calls=%async_computation.2 | async-start | bytes 4194304
  273.3 7.3 %copy-start.53 = (f32[2,128,64]{1,0,2:T(2,128)S(1)}, f32[2,128,64]{1,0,2:T(2,128)}, u32[]{:S(2)}) copy-start(f32[2,128,64]{1,0,2:T(2,128)} %copy.70) | copy-start | bytes 196612
  285.8 14.9 %collective-permute-start.1 = (bf16[2,128,960]{1,2,0:T(8,128)(2,1)}, bf16[2,128,960]{1,2,0:T(8,128)(2,1)}, u32[]{:S(2)}, u32[]{:S(2)}) collective-permute-start(bf16[2,128,960]{1,2,0:T(8,128)(2,1)} %copy_bitcast_fusion.2), channel_id=1, source_target_pairs={{64,0},{65,1},{66,2},{67,3},{68,4},{69,5},{70,6},{71,7},{72,8},{73... | collective-permute-start | bytes 1474568 | tf_op jit(solution)/shard_map/ppermute | solution.py:1057
  290.1 10.6 %copy-start.16 = (bf16[2,1,128,960]{2,3,1,0:T(8,128)(2,1)S(1)}, bf16[2,1,128,960]{2,3,1,0:T(8,128)(2,1)}, u32[]{:S(2)}) copy-start(bf16[2,1,128,960]{2,3,1,0:T(8,128)(2,1)} %param.19) | copy-start | bytes 1474564
  292.2 91.2 %collective-permute-start.2 = (bf16[256,1024]{0,1:T(8,128)(2,1)}, bf16[256,1024]{0,1:T(8,128)(2,1)}, u32[]{:S(2)}, u32[]{:S(2)}) collective-permute-start(bf16[256,1024]{0,1:T(8,128)(2,1)} %bitcast.362), channel_id=1, source_target_pairs={{0,8},{8,0},{16,24},{24,16},{32,40},{40,32},{48,56},{56,48},{1,9},... | collective-permute-start | bytes 1572872 | tf_op jit(solution)/shard_map/ppermute | solution.py:1062
  296.7 13.9 %slice-start.3 = ((s8[10485760]{0:T(1024)(128)(4,1)}), s8[4194304]{0:T(1024)(128)(4,1)S(1)}, s32[]{:S(2)}) async-start(s8[10485760]{0:T(1024)(128)(4,1)} %bitcast.319), calls=%async_computation.3 | async-start | bytes 8388608
  301.8 8.7 %copy-start.36 = (bf16[256,960]{0,1:T(8,128)(2,1)}, bf16[256,960]{0,1:T(8,128)(2,1)S(1)}, u32[]{:S(2)}) copy-start(bf16[256,960]{0,1:T(8,128)(2,1)S(1)} %copy_bitcast_fusion.1) | copy-start | bytes 1474564
  301.8 8.7 %slice-start.4 = ((s8[10485760]{0:T(1024)(128)(4,1)}), s8[4194304]{0:T(1024)(128)(4,1)S(1)}, s32[]{:S(2)}) async-start(s8[10485760]{0:T(1024)(128)(4,1)} %bitcast.319), calls=%async_computation.4 | async-start | bytes 8388608
  301.8 8.7 %slice-start.5 = ((s8[10485760]{0:T(1024)(128)(4,1)}), s8[2097152]{0:T(1024)(128)(4,1)S(1)}, s32[]{:S(2)}) async-start(s8[10485760]{0:T(1024)(128)(4,1)} %bitcast.319), calls=%async_computation.5 | async-start | bytes 4194304
  313.6 6.3 %copy-start.14 = (bf16[8,120,960]{2,1,0:T(8,128)(2,1)S(1)}, bf16[8,120,960]{2,1,0:T(8,128)(2,1)}, u32[]{:S(2)}) copy-start(bf16[8,120,960]{2,1,0:T(8,128)(2,1)} %copy-done.12) | copy-start | bytes 5529604
  316.7 69.4 %collective-permute-start.10 = (bf16[256,960]{0,1:T(8,128)(2,1)}, bf16[256,960]{0,1:T(8,128)(2,1)}, u32[]{:S(2)}, u32[]{:S(2)}) collective-permute-start(bf16[256,960]{0,1:T(8,128)(2,1)} %fusion.151), channel_id=1, source_target_pairs={{0,8},{8,0},{16,24},{24,16},{32,40},{40,32},{48,56},{56,48},{1,9},... | collective-permute-start | bytes 1474568 | tf_op jit(solution)/shard_map/ppermute | solution.py:1062
  368.0 5.7 %copy-start.40 = (bf16[256,2560]{1,0:T(8,128)(2,1)S(1)}, bf16[256,2560]{1,0:T(8,128)(2,1)}, u32[]{:S(2)}) copy-start(bf16[256,2560]{1,0:T(8,128)(2,1)} %copy-done.39) | copy-start | bytes 3932164
  368.0 24.3 %collective-permute-start.4 = (bf16[256,2560]{1,0:T(8,128)(2,1)}, bf16[256,2560]{1,0:T(8,128)(2,1)}, u32[]{:S(2)}, u32[]{:S(2)}) collective-permute-start(bf16[256,2560]{1,0:T(8,128)(2,1)} %get-tuple-element.83), channel_id=1, source_target_pairs={{0,8},{8,0},{16,24},{24,16},{32,40},{40,32},{48,56},{56,48},{1,9},... | collective-permute-start | bytes 3932168 | tf_op jit(solution)/shard_map/ppermute | solution.py:1062
  373.0 8.3 %collective-permute-start.8 = (f32[2,960]{1,0:T(2,128)S(1)}, f32[2,960]{1,0:T(2,128)S(1)}, u32[]{:S(2)}, u32[]{:S(2)}) collective-permute-start(f32[2,960]{1,0:T(2,128)S(1)} %pad_maximum_fusion.9), channel_id=1, source_target_pairs={{0,8},{8,0},{16,24},{24,16},{32,40},{40,32},{48,56},{56,48},{1,9},... | collective-permute-start | bytes 23048 | tf_op jit(solution)/shard_map/ppermute | solution.py:1062
  373.2 15.4 %collective-permute-start.7 = (bf16[256,1600]{0,1:T(8,128)(2,1)}, bf16[256,1600]{0,1:T(8,128)(2,1)}, u32[]{:S(2)}, u32[]{:S(2)}) collective-permute-start(bf16[256,1600]{0,1:T(8,128)(2,1)} %pad_maximum_fusion.4), channel_id=1, source_target_pairs={{0,8},{8,0},{16,24},{24,16},{32,40},{40,32},{48,56},{56,48},{1,9},... | collective-permute-start | bytes 2457608 | tf_op jit(solution)/shard_map/ppermute | solution.py:1062
  381.4 4.6 collective-permute-start.9
  383.3 6.0 %copy-start.35 = (bf16[256,960]{0,1:T(8,128)(2,1)S(1)}, bf16[256,960]{0,1:T(8,128)(2,1)}, u32[]{:S(2)}) copy-start(bf16[256,960]{0,1:T(8,128)(2,1)} %copy-done.34) | copy-start | bytes 1474564
  383.4 5.2 %collective-permute-start.6 = (bf16[256,8,64]{0,2,1:T(8,128)(2,1)S(1)}, bf16[256,8,64]{0,2,1:T(8,128)(2,1)S(1)}, u32[]{:S(2)}, u32[]{:S(2)}) collective-permute-start(bf16[256,8,64]{0,2,1:T(8,128)(2,1)S(1)} %copy-done.50), channel_id=1, source_target_pairs={{0,8},{8,0},{16,24},{24,16},{32,40},{40,32},{48,56},{56,48},{1,9},... | collective-permute-start | bytes 786440 | tf_op jit(solution)/shard_map/ppermute | solution.py:1062
  386.0 14.2 %collective-permute-start.5 = (bf16[256,512]{0,1:T(8,128)(2,1)}, bf16[256,512]{0,1:T(8,128)(2,1)}, u32[]{:S(2)}, u32[]{:S(2)}) collective-permute-start(bf16[256,512]{0,1:T(8,128)(2,1)} %get-tuple-element.103), channel_id=1, source_target_pairs={{0,8},{8,0},{16,24},{24,16},{32,40},{40,32},{48,56},{56,48},{1,9},... | collective-permute-start | bytes 786440 | tf_op jit(solution)/shard_map/ppermute | solution.py:1062
  386.1 19.1 %collective-permute-start.3 = (bf16[256,2560]{1,0:T(8,128)(2,1)}, bf16[256,2560]{1,0:T(8,128)(2,1)}, u32[]{:S(2)}, u32[]{:S(2)}) collective-permute-start(bf16[256,2560]{1,0:T(8,128)(2,1)} %get-tuple-element.85), channel_id=1, source_target_pairs={{0,8},{8,0},{16,24},{24,16},{32,40},{40,32},{48,56},{56,48},{1,9},... | collective-permute-start | bytes 3932168 | tf_op jit(solution)/shard_map/ppermute | solution.py:1062
  (58 other events, 171.0 us)

commit v4 on v2

--- a/solution.py
+++ b/solution.py
@@ -25,12 +25,14 @@
 
 MESH = pl.DeviceIdType.MESH
 ANY = pl.BlockSpec(memory_space=pl.ANY)
+VMEM = pl.BlockSpec(memory_space=pltpu.VMEM)
 
 GATE_UP = (PADDED, 2 * FF, "columns")
 DOWN = (FF // SHARDS, DOWN_COLUMNS, "columns")
 ATTEND_IN = (PADDED, QKV, "rows")
 ATTEND_OUT = (PADDED, D, "rows")
-SHAPES = (GATE_UP, DOWN, ATTEND_IN, ATTEND_OUT)
+FEED_FORWARD = (GATE_UP, DOWN)
+ATTENTION = (ATTEND_IN, ATTEND_OUT)
 
 
 def half_shape(shape):
@@ -87,6 +89,7 @@
     ("Yp", 1, 3, 1),
 )
 GATHER_NEXT = {1: (5, 6), 2: (3, 4), 0: (7, 8), 4: (9,), 7: (10,)}
+GATHER_STAGES = ((1, 2, 0), (4, 7, 3, 5, 6, 8), (9, 10))
 GATHER_ORDER = (1, 2, 0, 4, 7, 3, 5, 6, 8, 9, 10)
 
 
@@ -105,94 +108,178 @@
     return (0, rows) if part == "f" else (part * (rows // 2), rows // 2)
 
 
-def gather_kernel(*refs):
-    count = len(SHAPES)
-    shards, outs = refs[:count], refs[count : 2 * count]
-    local_sem, send_sem, recv_sem = refs[2 * count :]
-    z, core, x, y = places()
-    ids = peer_ids()
-    mine = x * 4 + y
-
-    def owner(column, step):
-        return ((x + column) % 2) * 4 + (y + step) % 4
-
-    def view(array, column, step, part, which):
-        start, rows = part_rows(SHAPES[array], part)
-        return outs[array].at[(owner(column, step),) + half_view(SHAPES[array], which, start, rows)]
-
-    def copy(array, edge):
-        peer, column, step, part = GATHER[edge % 11]
-        if edge < 11:
-            target = view(array, column, step, part, core)
-            source = target
-            if (column, step) == (0, 0):
-                start, rows = part_rows(SHAPES[array], part)
-                source = shards[array].at[half_view(SHAPES[array], core, start, rows)]
+UPWARD = (0, 1, 3, 5, 7)
+PLAIN_EDGES = 22
+SPREAD_EDGES = 88
+
+
+class Gather:
+    def __init__(self, shapes, spread, shards, outs, sems):
+        self.shapes, self.spread, self.shards, self.outs = shapes, spread, shards, outs
+        self.local_sem, self.send_sem, self.recv_sem = sems
+        self.z, self.core, self.x, self.y = places()
+        self.ids = peer_ids()
+
+    def owner(self, column, step):
+        return ((self.x + column) % 2) * 4 + (self.y + step) % 4
+
+    def index(self, array, part, which, plane):
+        shape = self.shapes[array]
+        start, rows = part_rows(shape, part)
+        if array == self.spread:
+            quarter = half_shape(shape)[0] // 4
+            start, rows = plane * quarter + start // 4, rows // 4
+        return half_view(shape, which, start, rows)
+
+    def view(self, array, column, step, part, which, plane):
+        return self.outs[array].at[
+            (self.owner(column, step),) + self.index(array, part, which, plane)
+        ]
+
+    def received(self, edge):
+        group, base = edge // 11, edge % 11
+        peer, column, step, part = GATHER[base]
+        column, step = seen_by_receiver(peer, column, step)
+        return column, step, part, (0, 0, 3, 1, 2, 3, 1, 2)[group]
+
+    def peer_of(self, edge):
+        group, base = edge // 11, edge % 11
+        if group == 0:
+            return GATHER[base][0]
+        if group in (1, 5, 6, 7):
+            return "C"
+        return {2: "Z1", 3: "Z3", 4: "Z1" if base in UPWARD else "Z3"}[group]
+
+    def copy(self, array, edge):
+        group, base = edge // 11, edge % 11
+        if group == 0:
+            _, column, step, part = GATHER[base]
+            away = 0
         else:
-            peer, (column, step) = "C", seen_by_receiver(peer, column, step)
-            source = target = view(array, column, step, part, core)
+            column, step, part, away = self.received(edge)
+            if group in (2, 3):
+                away = 0
+            elif group == 4:
+                away = 3 if base in UPWARD else 1
+        target = source = self.view(array, column, step, part, self.core, (self.z + away) % 4)
+        if group == 0 and (column, step) == (0, 0):
+            source = self.shards[array].at[self.index(array, part, self.core, self.z)]
         return pltpu.make_async_remote_copy(
             src_ref=source,
             dst_ref=target,
-            send_sem=send_sem.at[array, edge],
-            recv_sem=recv_sem.at[array, edge],
-            device_id=ids[peer],
+            send_sem=self.send_sem.at[array, edge],
+            recv_sem=self.recv_sem.at[array, edge],
+            device_id=self.ids[self.peer_of(edge)],
             device_id_type=MESH,
         )
 
-    def wait_for(array, edge):
-        peer, column, step, part = GATHER[edge % 11]
-        column, step = seen_by_receiver(peer, column, step)
-        which = core if edge < 11 else 1 - core
-        landed = view(array, column, step, part, which)
+    def wait_for(self, array, edge):
+        column, step, part, away = self.received(edge)
+        which = 1 - self.core if edge // 11 in (1, 5, 6, 7) else self.core
+        landed = self.view(array, column, step, part, which, (self.z + away) % 4)
         pltpu.make_async_remote_copy(
             src_ref=landed,
             dst_ref=landed,
-            send_sem=send_sem.at[array, edge],
-            recv_sem=recv_sem.at[array, edge],
-            device_id=ids["C"],
+            send_sem=self.send_sem.at[array, edge],
+            recv_sem=self.recv_sem.at[array, edge],
+            device_id=self.ids["C"],
             device_id_type=MESH,
         ).wait_recv()
 
-    greet(ids, ("X", "Yp", "Ym", "C"))
-    own = [
-        pltpu.make_async_copy(shards[array], outs[array].at[mine], local_sem.at[array])
-        for array in range(count)
-    ]
-    for array in range(count):
-        for edge in (0, 1, 2):
-            copy(array, edge).start()
-        own[array].start()
-    for array in range(count):
-        for edge in GATHER_ORDER:
-            wait_for(array, edge)
+    def own(self, array):
+        return pltpu.make_async_copy(
+            self.shards[array],
+            self.outs[array].at[self.x * 4 + self.y],
+            self.local_sem.at[array],
+        )
+
+    def start(self):
+        for array in range(len(self.shapes)):
+            for edge in (0, 1, 2):
+                self.copy(array, edge).start()
+            self.own(array).start()
+
+    def within_plane(self, array, edges):
+        for edge in edges:
+            self.wait_for(array, edge)
             for later in GATHER_NEXT.get(edge, ()):
-                copy(array, later).start()
-            copy(array, 11 + edge).start()
-    for array in range(count):
-        for edge in range(11):
-            wait_for(array, 11 + edge)
-        for edge in range(22):
-            copy(array, edge).wait_send()
-        own[array].wait()
+                self.copy(array, later).start()
+            if array == self.spread:
+                self.copy(array, 22 + edge).start()
+                self.copy(array, 33 + edge).start()
+            self.copy(array, 11 + edge).start()
+
+    def round_z(self, edges):
+        if self.spread is None:
+            return
+        for edge in edges:
+            for group in (2, 3):
+                self.wait_for(self.spread, 11 * group + edge)
+                if (group == 2) == (edge in UPWARD):
+                    self.copy(self.spread, 44 + edge).start()
+                self.copy(self.spread, 11 * (group + 3) + edge).start()
+
+    def steps(self):
+        first, second, third = GATHER_STAGES
+        arrays = range(len(self.shapes))
+        steps = [functools.partial(self.within_plane, array, first) for array in arrays]
+        steps.append(functools.partial(self.round_z, first))
+        steps += [functools.partial(self.within_plane, array, second) for array in arrays]
+        steps.append(functools.partial(self.round_z, second))
+        steps += [functools.partial(self.within_plane, array, third) for array in arrays]
+        steps.append(functools.partial(self.round_z, third))
+        steps.append(self.finish)
+        return steps
+
+    def finish(self):
+        if self.spread is not None:
+            for edge in GATHER_ORDER:
+                self.wait_for(self.spread, 44 + edge)
+                self.copy(self.spread, 77 + edge).start()
+        for array in range(len(self.shapes)):
+            last = SPREAD_EDGES if array == self.spread else PLAIN_EDGES
+            for edge in range(last):
+                if edge // 11 in (1, 5, 6, 7):
+                    self.wait_for(array, edge)
+            for edge in range(last):
+                self.copy(array, edge).wait_send()
+            self.own(array).wait()
+
+    @staticmethod
+    def out_shapes(shapes):
+        return [
+            jax.ShapeDtypeStruct((SHARDS, rows, columns), jnp.bfloat16)
+            for rows, columns, _ in shapes
+        ]
+
+    @staticmethod
+    def scratch(shapes, spread):
+        edges = PLAIN_EDGES if spread is None else SPREAD_EDGES
+        return [
+            pltpu.SemaphoreType.DMA((len(shapes),)),
+            pltpu.SemaphoreType.DMA((len(shapes), edges)),
+            pltpu.SemaphoreType.DMA((len(shapes), edges)),
+        ]
+
+
+def gather_kernel(shapes, *refs):
+    count = len(shapes)
+    gather = Gather(shapes, None, refs[:count], refs[count : 2 * count], refs[2 * count :])
+    greet(gather.ids, ("X", "Yp", "Ym", "C"))
+    gather.start()
+    for step in gather.steps():
+        step()
 
 
 def gather_weights(shards):
-    count = len(SHAPES)
+    count = len(ATTENTION)
     return pl.pallas_call(
-        gather_kernel,
+        functools.partial(gather_kernel, ATTENTION),
         name="gather_weights",
-        out_shape=[
-            jax.ShapeDtypeStruct((SHARDS, rows, columns), jnp.bfloat16)
-            for rows, columns, _ in SHAPES
-        ],
-        in_specs=[ANY] * count,
+        out_shape=Gather.out_shapes(ATTENTION),
+        in_specs=[VMEM] * count,
         out_specs=[ANY] * count,
-        scratch_shapes=[
-            pltpu.SemaphoreType.DMA((count,)),
-            pltpu.SemaphoreType.DMA((count, 22)),
-            pltpu.SemaphoreType.DMA((count, 22)),
-        ],
+        scratch_shapes=Gather.scratch(ATTENTION, None),
         compiler_params=pltpu.CompilerParams(collective_id=0, has_side_effects=True),
     )(*shards)
 
@@ -211,172 +298,288 @@
     ("X", 1, 0, "f", (5, 7)),
 )
 REDUCE_STAGES = ((0, 1, 2, 3, 4, 5), (6, 7), (8, 9, 10))
-
-
-def reduce_kernel(*refs):
-    count = len(SHAPES)
-    terms, outs = refs[:count], refs[count : 2 * count]
-    scratch = refs[2 * count :]
-    totals = scratch[:count]
-    wholes = scratch[count : 2 * count]
-    parts = scratch[2 * count : 3 * count]
-    quarters = scratch[3 * count : 4 * count]
-    local_sem, send_sem, recv_sem = scratch[4 * count :]
-    z, core, x, y = places()
-    ids = peer_ids()
-    mine = x * 4 + y
-
-    def owner(column, step):
-        return ((x + column) % 2) * 4 + (y + step) % 4
-
-    def piece(array, edge):
+SHARD_ORDER = ((0, 2), (1, 2), (1, 3), (1, 1), (0, 1), (0, 3), (1, 0), (0, 0))
+REDUCE_EDGES = 45
+
+
+class Reduce:
+    def __init__(self, shapes, spread, terms, outs, scratch):
+        count = len(shapes)
+        self.shapes, self.spread, self.terms, self.outs = shapes, spread, terms, outs
+        self.totals = scratch[:count]
+        self.wholes = scratch[count : 2 * count]
+        self.parts = scratch[2 * count : 3 * count]
+        self.quarters = scratch[3 * count : 4 * count]
+        self.rounds = None if spread is None else scratch[4 * count]
+        self.local_sem, self.send_sem, self.recv_sem = scratch[-3:]
+        self.z, self.core, self.x, self.y = places()
+        self.mine = self.x * 4 + self.y
+        self.ids = peer_ids()
+        self.plain = [array for array in range(count) if array != spread]
+
+    @staticmethod
+    def piece_shapes(shapes, spread):
+        halves = [half_shape(shape) for shape in shapes]
+        return halves, [
+            (half[0], half[1] // 4) if array == spread else half
+            for array, half in enumerate(halves)
+        ]
+
+    @staticmethod
+    def out_shapes(shapes):
+        return [jax.ShapeDtypeStruct((rows, columns), jnp.bfloat16) for rows, columns, _ in shapes]
+
+    @staticmethod
+    def scratch(shapes, spread):
+        halves, pieces = Reduce.piece_shapes(shapes, spread)
+        bf16 = jnp.bfloat16
+        buffers = [pltpu.VMEM((SHARDS,) + half, bf16) for half in halves]
+        buffers += [pltpu.VMEM((3,) + piece, bf16) for piece in pieces]
+        buffers += [pltpu.VMEM((8, piece[0] // 2, piece[1]), bf16) for piece in pieces]
+        buffers += [pltpu.VMEM((3, half[0] // 4, half[1]), bf16) for half in halves]
+        if spread is not None:
+            buffers.append(pltpu.VMEM((3 * SHARDS,) + pieces[spread], bf16))
+        return buffers + [
+            pltpu.SemaphoreType.DMA((len(shapes),)),
+            pltpu.SemaphoreType.DMA((len(shapes), REDUCE_EDGES)),
+            pltpu.SemaphoreType.DMA((len(shapes), REDUCE_EDGES)),
+        ]
+
+    def owner(self, column, step):
+        return ((self.x + column) % 2) * 4 + (self.y + step) % 4
+
+    def lanes(self, array, plane):
+        columns = half_shape(self.shapes[array])[1]
+        if array != self.spread:
+            return pl.ds(0, columns)
+        return pl.ds(pl.multiple_of(plane * (columns // 4), 128), columns // 4)
+
+    def piece(self, array, edge):
         _, column, step, part, _ = REDUCE[edge]
-        start, rows = part_rows(SHAPES[array], part)
-        return totals[array].at[owner(column, step), pl.ds(start, rows), :]
-
-    def slot(array, edge):
-        return parts[array].at[edge] if edge < 8 else wholes[array].at[edge - 8]
-
-    def add(array, into, start, rows, source):
+        start, rows = part_rows(self.shapes[array], part)
+        return self.totals[array].at[
+            self.owner(column, step), pl.ds(start, rows), self.lanes(array, self.z)
+        ]
+
+    def slot(self, array, edge):
+        return self.parts[array].at[edge] if edge < 8 else self.wholes[array].at[edge - 8]
+
+    def add(self, array, into, start, rows, lanes, source):
+        total = self.totals[array]
+
         @pl.loop(0, rows // 16)
         def _(index):
             offset = pl.multiple_of(index * 16, 16)
             at = pl.ds(pl.multiple_of(start + offset, 16), 16)
-            totals[array][into, at, :] = (
-                totals[array][into, at, :].astype(jnp.float32)
+            total[into, at, lanes] = (
+                total[into, at, lanes].astype(jnp.float32)
                 + source[pl.ds(offset, 16), :].astype(jnp.float32)
             ).astype(jnp.bfloat16)
 
-    def quarter(array, index):
-        rows = half_shape(SHAPES[array])[0] // 4
-        return pl.multiple_of(index * rows, 16), rows
-
-    def out_view(array, index, which):
-        start, rows = quarter(array, index)
-        return outs[array].at[half_view(SHAPES[array], which, start, rows)]
-
-    def copy(array, edge):
+    def quarter(self, array, plane):
+        rows = half_shape(self.shapes[array])[0]
+        if array == self.spread:
+            return 0, rows, self.lanes(array, plane)
+        return pl.multiple_of(plane * (rows // 4), 16), rows // 4, self.lanes(array, plane)
+
+    def summed(self, array, plane):
+        start, rows, lanes = self.quarter(array, plane)
+        return self.totals[array].at[self.mine, pl.ds(start, rows), lanes]
+
+    def out_view(self, array, plane, which):
+        shape = self.shapes[array]
+        if array == self.spread:
+            rows, columns = half_shape(shape)
+            first = pl.multiple_of(which * columns + plane * (columns // 4), 128)
+            return self.outs[array].at[pl.ds(0, rows), pl.ds(first, columns // 4)]
+        start, rows, _ = self.quarter(array, plane)
+        return self.outs[array].at[half_view(shape, which, start, rows)]
+
+    def copy(self, array, edge):
+        z = self.z
         if edge < 11:
-            peer, source, target = REDUCE[edge][0], piece(array, edge), slot(array, edge)
+            peer, source, target = REDUCE[edge][0], self.piece(array, edge), self.slot(array, edge)
         elif edge < 14:
             step = edge - 10
-            peer = f"Z{step}"
-            start, rows = quarter(array, (z + step) % 4)
-            source = totals[array].at[mine, pl.ds(start, rows), :]
-            target = quarters[array].at[step - 1]
+            peer, source = f"Z{step}", self.summed(array, (z + step) % 4)
+            target = self.quarters[array].at[step - 1]
         elif edge < 17:
-            peer = f"Z{edge - 13}"
-            start, rows = quarter(array, z)
-            source = totals[array].at[mine, pl.ds(start, rows), :]
-            target = out_view(array, z, core)
+            peer, source = f"Z{edge - 13}", self.summed(array, z)
+            target = self.out_view(array, z, self.core)
+        elif edge < 21:
+            peer = "C"
+            source = target = self.out_view(array, (z + edge - 17) % 4, self.core)
+            if edge == 17:
+                source = self.summed(array, z)
         else:
-            peer = "C"
-            at = (z + edge - 17) % 4
-            source = target = out_view(array, at, core)
-            if edge == 17:
-                start, rows = quarter(array, z)
-                source = totals[array].at[mine, pl.ds(start, rows), :]
+            kind, shard = (edge - 21) // 8, (edge - 21) % 8
+            peer = ("Z1" if shard % 2 == 0 else "Z3", "Z1", "Z3")[kind]
+            lanes = self.lanes(array, (z + (2, 1, 3)[kind]) % 4)
+            source = self.totals[array].at[self.owner(*SHARD_ORDER[shard]), :, lanes]
+            target = self.rounds.at[edge - 21]
         return pltpu.make_async_remote_copy(
             src_ref=source,
             dst_ref=target,
-            send_sem=send_sem.at[array, edge],
-            recv_sem=recv_sem.at[array, edge],
-            device_id=ids[peer],
+            send_sem=self.send_sem.at[array, edge],
+            recv_sem=self.recv_sem.at[array, edge],
+            device_id=self.ids[peer],
             device_id_type=MESH,
         )
 
-    def wait_for(array, edge):
+    def wait_for(self, array, edge):
+        z = self.z
         if edge < 11:
-            landed = slot(array, edge)
+            landed = self.slot(array, edge)
         elif edge < 14:
-            landed = quarters[array].at[edge - 11]
+            landed = self.quarters[array].at[edge - 11]
         elif edge < 17:
-            landed = out_view(array, (z + 4 - (edge - 13)) % 4, core)
+            landed = self.out_view(array, (z + 4 - (edge - 13)) % 4, self.core)
+        elif edge < 21:
+            landed = self.out_view(array, (z + edge - 17) % 4, 1 - self.core)
         else:
-            landed = out_view(array, (z + edge - 17) % 4, 1 - core)
+            landed = self.rounds.at[edge - 21]
         pltpu.make_async_remote_copy(
             src_ref=landed,
             dst_ref=landed,
-            send_sem=send_sem.at[array, edge],
-            recv_sem=recv_sem.at[array, edge],
-            device_id=ids["C"],
+            send_sem=self.send_sem.at[array, edge],
+            recv_sem=self.recv_sem.at[array, edge],
+            device_id=self.ids["C"],
             device_id_type=MESH,
         ).wait_recv()
 
-    def receive(array, edge):
-        wait_for(array, edge)
+    def receive(self, array, edge):
+        self.wait_for(array, edge)
         peer, column, step, part, _ = REDUCE[edge]
         column, step = seen_by_receiver(peer, column, step)
-        start, rows = part_rows(SHAPES[array], part)
-        add(array, owner(column, step), start, rows, slot(array, edge))
-
-    loads = [
-        pltpu.make_async_copy(terms[array], totals[array], local_sem.at[array])
-        for array in range(count)
-    ]
-    for load in loads:
-        load.start()
-    greet(ids, ("X", "Yp", "Ym", "C", "Z1", "Z2", "Z3"))
-    for stage in REDUCE_STAGES:
-        for array in range(count):
-            if stage == REDUCE_STAGES[0]:
-                loads[array].wait()
-            for edge in stage:
-                for earlier in REDUCE[edge][4]:
-                    receive(array, earlier)
-                copy(array, edge).start()
-    for array in range(count):
+        start, rows = part_rows(self.shapes[array], part)
+        lanes = self.lanes(array, self.z)
+        self.add(array, self.owner(column, step), start, rows, lanes, self.slot(array, edge))
+
+    def receive_round(self, kind, shard):
+        edge = 21 + 8 * kind + shard
+        array = self.spread
+        self.wait_for(array, edge)
+        away = 0 if kind > 0 else (1 if shard % 2 == 0 else 3)
+        rows = half_shape(self.shapes[array])[0]
+        lanes = self.lanes(array, (self.z + away) % 4)
+        self.add(
+            array, self.owner(*SHARD_ORDER[shard]), 0, rows, lanes, self.rounds.at[edge - 21]
+        )
+
+    def stage(self, array, number):
+        for edge in REDUCE_STAGES[number]:
+            for earlier in REDUCE[edge][4]:
+                self.receive(array, earlier)
+            self.copy(array, edge).start()
+
+    def load(self, array):
+        return pltpu.make_async_copy(
+            self.terms[array], self.totals[array], self.local_sem.at[array]
+        )
+
+    def store(self, array):
+        return pltpu.make_async_copy(
+            self.summed(array, self.z), self.out_view(array, self.z, self.core),
+            self.local_sem.at[array],
+        )
+
+    def start_loads(self):
+        for array in range(len(self.shapes)):
+            self.load(array).start()
+
+    def start(self):
+        if self.spread is not None:
+            self.load(self.spread).wait()
+            for shard in range(SHARDS):
+                self.copy(self.spread, 21 + shard).start()
+        for array in self.plain:
+            self.load(array).wait()
+            self.stage(array, 0)
+
+    def first_round(self):
+        for shard in range(SHARDS):
+            self.receive_round(0, shard)
+            self.copy(self.spread, 29 + shard).start()
+            self.copy(self.spread, 37 + shard).start()
+
+    def second_round(self, shards):
+        for shard in shards:
+            self.receive_round(1, shard)
+            self.receive_round(2, shard)
+
+    def end_plane(self, array):
         for edge in (8, 9, 10):
-            receive(array, edge)
-        for edge in (11, 12, 13):
-            copy(array, edge).start()
-    stores = []
-    for array in range(count):
-        start, rows = quarter(array, z)
-        for edge in (11, 12, 13):
-            wait_for(array, edge)
-            add(array, mine, start, rows, quarters[array].at[edge - 11])
+            self.receive(array, edge)
+        for edge in (11, 12, 13) if array != self.spread else ():
+            self.copy(array, edge).start()
+
+    def end_z(self, array):
+        if array != self.spread:
+            start, rows, lanes = self.quarter(array, self.z)
+            for edge in (11, 12, 13):
+                self.wait_for(array, edge)
+                self.add(
+                    array, self.mine, start, rows, lanes, self.quarters[array].at[edge - 11]
+                )
         for edge in (14, 15, 16, 17):
-            copy(array, edge).start()
-        store = pltpu.make_async_copy(
-            totals[array].at[mine, pl.ds(start, rows), :],
-            out_view(array, z, core),
-            local_sem.at[array],
-        )
-        store.start()
-        stores.append(store)
-    for array in range(count):
-        for edge in (14, 15, 16):
-            wait_for(array, edge)
-            copy(array, 17 + (17 - edge)).start()
-    for array in range(count):
-        for edge in range(17, 21):
-            wait_for(array, edge)
-        for edge in range(21):
-            copy(array, edge).wait_send()
-        stores[array].wait()
+            self.copy(array, edge).start()
+        self.store(array).start()
+
+    def finish(self):
+        for array in range(len(self.shapes)):
+            for edge in (14, 15, 16):
+                self.wait_for(array, edge)
+                self.copy(array, 34 - edge).start()
+        for array in range(len(self.shapes)):
+            for edge in range(17, 21):
+                self.wait_for(array, edge)
+            for edge in range(REDUCE_EDGES):
+                if (edge not in (11, 12, 13)) if array == self.spread else (edge < 21):
+                    self.copy(array, edge).wait_send()
+            self.store(array).wait()
+
+    def steps(self):
+        call = functools.partial
+        steps = []
+        if self.spread is not None:
+            steps.append(self.first_round)
+        steps += [call(self.stage, array, 1) for array in self.plain]
+        if self.spread is not None:
+            steps.append(call(self.second_round, range(4)))
+            steps.append(call(self.stage, self.spread, 0))
+            steps.append(call(self.second_round, range(4, SHARDS)))
+            steps.append(call(self.stage, self.spread, 1))
+        steps += [call(self.stage, array, 2) for array in self.plain]
+        if self.spread is not None:
+            steps.append(call(self.stage, self.spread, 2))
+        steps += [call(self.end_plane, array) for array in self.plain]
+        if self.spread is not None:
+            steps.append(call(self.end_plane, self.spread))
+            steps.append(call(self.end_z, self.spread))
+        steps += [call(self.end_z, array) for array in self.plain]
+        steps.append(self.finish)
+        return steps
+
+
+def reduce_kernel(shapes, *refs):
+    count = len(shapes)
+    reduce = Reduce(shapes, None, refs[:count], refs[count : 2 * count], refs[2 * count :])
+    reduce.start_loads()
+    greet(reduce.ids, ("X", "Yp", "Ym", "C", "Z1", "Z2", "Z3"))
+    reduce.start()
+    for step in reduce.steps():
+        step()
 
 
 def reduce_gradients(terms):
-    count = len(SHAPES)
-    halves = [half_shape(shape) for shape in SHAPES]
+    count = len(ATTENTION)
     return pl.pallas_call(
-        reduce_kernel,
+        functools.partial(reduce_kernel, ATTENTION),
         name="reduce_gradients",
-        out_shape=[
-            jax.ShapeDtypeStruct((rows, columns), jnp.bfloat16) for rows, columns, _ in SHAPES
-        ],
+        out_shape=Reduce.out_shapes(ATTENTION),
         in_specs=[ANY] * count,
         out_specs=[ANY] * count,
-        scratch_shapes=[pltpu.VMEM((SHARDS,) + half, jnp.bfloat16) for half in halves]
-        + [pltpu.VMEM((3,) + half, jnp.bfloat16) for half in halves]
-        + [pltpu.VMEM((8, half[0] // 2, half[1]), jnp.bfloat16) for half in halves]
-        + [pltpu.VMEM((3, half[0] // 4, half[1]), jnp.bfloat16) for half in halves]
-        + [
-            pltpu.SemaphoreType.DMA((count,)),
-            pltpu.SemaphoreType.DMA((count, 21)),
-            pltpu.SemaphoreType.DMA((count, 21)),
-        ],
+        scratch_shapes=Reduce.scratch(ATTENTION, None),
         compiler_params=pltpu.CompilerParams(
             collective_id=1, has_side_effects=True, vmem_limit_bytes=48 * 2**20
         ),
@@ -411,11 +614,12 @@
     return [(step, (me + step) % SHARDS, (me + SHARDS - step) % SHARDS) for step in range(1, SHARDS)]
 
 
-def greet_all(me):
+def greet_all(me, others=()):
     barrier = pltpu.get_barrier_semaphore()
-    for _, target, _ in ring(me):
-        pl.semaphore_signal(barrier, inc=1, device_id={"fsdp": target}, device_id_type=MESH)
-    pl.semaphore_wait(barrier, SHARDS - 1)
+    ids = peer_ids()
+    for device in [{"fsdp": target} for _, target, _ in ring(me)] + [ids[name] for name in others]:
+        pl.semaphore_signal(barrier, inc=1, device_id=device, device_id_type=MESH)
+    pl.semaphore_wait(barrier, SHARDS - 1 + len(others))
 
 
 def sent(source, target, send_sem, recv_sem, device):
@@ -451,10 +655,17 @@
     )
 
 
-def attend_kernel(
-    q_ref, kv_ref, mixed_ref, q_kept, kv_kept, lse_kept,
-    q_all, kv_all, lse_all, mixed_all, local_sem, send_sem, recv_sem,
-):
+def attend_kernel(with_gather, *refs):
+    count = len(FEED_FORWARD) if with_gather else 0
+    q_ref, kv_ref, mixed_ref, q_kept, kv_kept, lse_kept = refs[:2] + refs[2 + count : 6 + count]
+    q_all, kv_all, lse_all, mixed_all, local_sem, send_sem, recv_sem = refs[
+        6 + 2 * count : 13 + 2 * count
+    ]
+    background = None
+    if with_gather:
+        background = Gather(
+            FEED_FORWARD, 0, refs[2 : 2 + count], refs[6 + count : 6 + 2 * count], refs[-3:]
+        )
     me = lax.axis_index("fsdp")
     both = two_groups(me)
     second = jnp.where(both, 1, 0)
@@ -508,7 +719,7 @@
             local_sem.at[3, slot],
         )
 
-    greet_all(me)
+    greet_all(me, ("C", "Z1", "Z3") if background else ())
     for slot in range(SLOTS):
         for step, target, _ in ring(me):
             for copy in incoming(slot, step, target, me):
@@ -521,8 +732,16 @@
         for copy in own_copies(slot):
             copy.start()
 
-    @pl.loop(0, SLOTS)
-    def _(slot):
+    pending = []
+    if background:
+        background.start()
+        pending = background.steps()
+
+    def do_pending(number):
+        for _ in range(min(number, len(pending))):
+            pending.pop(0)()
+
+    def work(slot):
         for step, _, source in ring(me):
             for copy in incoming(slot, step, source, source):
                 copy.wait_recv()
@@ -533,6 +752,8 @@
 
         for copy in own_copies(slot):
             copy.wait()
+        if background and slot == 0:
+            do_pending(1)
         for block in range(TOKENS // BLOCK):
             rows = pl.ds(block * BLOCK, BLOCK)
             length = (block + 1) * BLOCK
@@ -560,6 +781,13 @@
             outgoing(slot, step, target, me).start()
         own_result(slot).start()
 
+    if background:
+        work(0)
+        do_pending(3)
+        work(1)
+    else:
+        pl.loop(0, SLOTS)(work)
+    do_pending(len(pending))
     keep = [
         pltpu.make_async_copy(q_all, q_kept, local_sem.at[4, 0]),
         pltpu.make_async_copy(kv_all, kv_kept, local_sem.at[4, 1]),
@@ -588,19 +816,21 @@
 FULL = SHARDS * PAIR
 
 
-def attend(query_rows, key_values):
+def attend(query_rows, key_values, shards=()):
     bf16 = jnp.bfloat16
+    with_gather = bool(shards)
     return pl.pallas_call(
-        attend_kernel,
-        name="attend",
+        functools.partial(attend_kernel, with_gather),
+        name="attend_gather" if with_gather else "attend",
         out_shape=[
             jax.ShapeDtypeStruct((SLOTS, LOCAL, FULL), bf16),
             jax.ShapeDtypeStruct(Q_ALL, bf16),
             jax.ShapeDtypeStruct(KV_ALL, bf16),
             jax.ShapeDtypeStruct(Q_ALL, jnp.float32),
-        ],
-        in_specs=[ANY] * 2,
-        out_specs=[ANY] * 4,
+        ]
+        + (Gather.out_shapes(FEED_FORWARD) if with_gather else []),
+        in_specs=[ANY] * 2 + [VMEM] * len(shards),
+        out_specs=[ANY] * (4 + len(shards)),
         scratch_shapes=[
             pltpu.VMEM(Q_ALL, bf16),
             pltpu.VMEM(KV_ALL, bf16),
@@ -609,18 +839,28 @@
             pltpu.SemaphoreType.DMA((6, SLOTS)),
             pltpu.SemaphoreType.DMA((4, SLOTS, SHARDS)),
             pltpu.SemaphoreType.DMA((4, SLOTS, SHARDS)),
-        ],
+        ]
+        + (Gather.scratch(FEED_FORWARD, 0) if with_gather else []),
         compiler_params=pltpu.CompilerParams(
-            collective_id=2, has_side_effects=True, vmem_limit_bytes=40 * 2**20
+            collective_id=4 if with_gather else 2,
+            has_side_effects=True,
+            vmem_limit_bytes=40 * 2**20,
         ),
-    )(query_rows, key_values)
-
-
-def attend_back_kernel(
-    slope_ref, q_ref, kv_ref, lse_ref, dq_ref, dkv_ref, dkv_extra_ref,
-    slope_all, q_all, kv_all, lse_all, dq_all, dkv_total, dkv_all,
-    local_sem, send_sem, recv_sem,
-):
+    )(query_rows, key_values, *shards)
+
+
+def attend_back_kernel(with_reduce, *refs):
+    count = len(FEED_FORWARD) if with_reduce else 0
+    slope_ref, q_ref, kv_ref, lse_ref = refs[:4]
+    dq_ref, dkv_ref, dkv_extra_ref = refs[4 + count : 7 + count]
+    scratch = refs[7 + 2 * count :]
+    slope_all, q_all, kv_all, lse_all, dq_all, dkv_total, dkv_all = scratch[:7]
+    local_sem, send_sem, recv_sem = scratch[7:10]
+    background = None
+    if with_reduce:
+        background = Reduce(
+            FEED_FORWARD, None, refs[4 : 4 + count], refs[7 + count : 7 + 2 * count], scratch[10:]
+        )
     me = lax.axis_index("fsdp")
     both = two_groups(me)
     second = jnp.where(both, 1, 0)
@@ -681,16 +921,21 @@
     ]
     for copy in loads:
         copy.start()
-    greet_all(me)
+    if background:
+        background.start_loads()
+    greet_all(me, ("C", "Z1", "Z2", "Z3") if background else ())
     for slot in range(SLOTS):
         for step, target, _ in ring(me):
             incoming(slot, step, target, me).start()
         own_slope(slot).start()
+    pending = []
+    if background:
+        background.start()
+        pending = background.steps()
     for copy in loads:
         copy.wait()
 
-    @pl.loop(0, SLOTS)
-    def _(slot):
+    def work(slot):
         for step, _, source in ring(me):
             incoming(slot, step, source, source).wait_recv()
         own_slope(slot).wait()
@@ -736,6 +981,16 @@
         def _():
             own_extra(slot).start()
 
+    if background:
+        work(0)
+        for step in pending[:2]:
+            step()
+        work(1)
+        for step in pending[2:]:
+            step()
+    else:
+        pl.loop(0, SLOTS)(work)
+
     for slot in range(SLOTS):
         for step, target, source in ring(me):
             incoming(slot, step, target, me).wait_send()
@@ -760,18 +1015,20 @@
             own_extra(slot).wait()
 
 
-def attend_back(slope, kept):
+def attend_back(slope, kept, terms=()):
     bf16 = jnp.bfloat16
+    with_reduce = bool(terms)
     return pl.pallas_call(
-        attend_back_kernel,
-        name="attend_back",
+        functools.partial(attend_back_kernel, with_reduce),
+        name="attend_back_reduce" if with_reduce else "attend_back",
         out_shape=[
             jax.ShapeDtypeStruct((SLOTS, LOCAL, FULL), bf16),
             jax.ShapeDtypeStruct((SHARDS, SLOTS, LOCAL, PAIR), bf16),
             jax.ShapeDtypeStruct((2, SLOTS, LOCAL, PAIR), bf16),
-        ],
-        in_specs=[ANY] * 4,
-        out_specs=[ANY] * 3,
+        ]
+        + (Reduce.out_shapes(FEED_FORWARD) if with_reduce else []),
+        in_specs=[ANY] * (4 + len(terms)),
+        out_specs=[ANY] * (3 + len(terms)),
         scratch_shapes=[
             pltpu.VMEM(Q_ALL, bf16),
             pltpu.VMEM(Q_ALL, bf16),
@@ -783,11 +1040,14 @@
             pltpu.SemaphoreType.DMA((6, SLOTS)),
             pltpu.SemaphoreType.DMA((4, SLOTS, SHARDS)),
             pltpu.SemaphoreType.DMA((4, SLOTS, SHARDS)),
-        ],
+        ]
+        + (Reduce.scratch(FEED_FORWARD, None) if with_reduce else []),
         compiler_params=pltpu.CompilerParams(
-            collective_id=3, has_side_effects=True, vmem_limit_bytes=48 * 2**20
+            collective_id=5 if with_reduce else 3,
+            has_side_effects=True,
+            vmem_limit_bytes=(56 if with_reduce else 48) * 2**20,
         ),
-    )(slope, *kept)
+    )(slope, *kept, *terms)
 
 
 def rotary_tables(positions):
@@ -841,7 +1101,7 @@
     return values.reshape(values.shape[:-1] + (-1, HEAD_WIDTH))
 
 
-def forward_layer(layer_in, tables, weights):
+def forward_layer(layer_in, tables, weights, shards=()):
     attend_in, attend_out, gate_up, down_weight, gains = weights
     batches, local_count = layer_in.shape[:2]
     rows = batches * local_count
@@ -858,7 +1118,11 @@
         [rotated[..., QUERY_HEADS:, :], heads(projected[..., QUERY_WIDTH + KEY_WIDTH :])], -1
     )
     key_values = key_values.astype(jnp.bfloat16).reshape(batches, local_count, 2 * KEY_WIDTH)
-    mixed, *attended = attend(query_rows, key_values)
+    mixed, *attended = attend(query_rows, key_values, shards)
+    if shards:
+        *attended, gate_up, down_weight = attended
+        gate_up = gate_up.reshape(-1, 2 * FF)
+        down_weight = down_weight.reshape(-1, DOWN_COLUMNS)
     mixed = mixed.reshape(rows, FULL)
     hidden = values + jnp.dot(mixed, attend_out, preferred_element_type=jnp.float32)
     second_norm = pad_shards(normed(hidden, gains[1]).astype(jnp.bfloat16))
@@ -875,10 +1139,11 @@
         gated,
         act,
     )
-    return (result.astype(jnp.bfloat16).reshape(layer_in.shape), kept)
-
-
-def backward_layer(upstream, kept, tables, weights):
+    weights = (attend_in, attend_out, gate_up, down_weight, gains)
+    return (result.astype(jnp.bfloat16).reshape(layer_in.shape), kept, weights)
+
+
+def backward_layer(upstream, kept, tables, weights, last=False):
     attend_in, attend_out, gate_up, down_weight, gains = weights
     (
         values,
@@ -911,8 +1176,9 @@
     mixed_gradient = jnp.einsum(
         "td,qd->tq", branch_slope, attend_out, preferred_element_type=jnp.float32
     ).astype(jnp.bfloat16)
-    query_slope, pair_slopes, extra_slopes = attend_back(
-        mixed_gradient.reshape(batches, local_count, FULL), attended
+    terms = feed_forward_terms(second_norm, act, gated_slope, down_in) if last else ()
+    query_slope, pair_slopes, extra_slopes, *summed = attend_back(
+        mixed_gradient.reshape(batches, local_count, FULL), attended, terms
     )
     pair_slopes = pair_slopes.astype(jnp.float32)
     extra_slopes = extra_slopes.astype(jnp.float32)
@@ -944,12 +1210,12 @@
     )
     input_part, first_gain = norm_backward(values, gains[0], first_slope)
     input_slope = hidden_slope + input_part
-    slopes = (projected_slope, branch_slope, gated_slope, down_in)
-    return (
-        input_slope.reshape(batches, local_count, D),
-        slopes,
-        jnp.stack([first_gain, second_gain]),
-    )
+    input_slope = input_slope.reshape(batches, local_count, D)
+    if not last:
+        return input_slope
+    gain_slopes = jnp.stack([first_gain, second_gain])
+    terms = attention_terms(first_norm, mixed, projected_slope, branch_slope, gain_slopes)
+    return (input_slope, (*reduce_gradients(terms), *summed))
 
 
 def passed_along(value, steps):
@@ -962,42 +1228,44 @@
     return other
 
 
-def weight_terms(kept, slopes, gain_slopes):
+def halved(values, axis):
     core = lax.axis_index("dp") % 2
-    first_norm, mixed, second_norm, act = (kept[1], kept[3], kept[5], kept[7])
-    mixed = pad_shards(mixed[:, :QUERY_WIDTH])
-    projected_slope, branch_slope, gated_slope, down_in = slopes
-    tokens = act.shape[0]
-
-    def halved(values, axis):
-        extent = values.shape[axis] // 2
-        keep = lax.dynamic_slice_in_dim(values, core * extent, extent, axis)
-        send = lax.dynamic_slice_in_dim(values, (1 - core) * extent, extent, axis)
-        return jnp.concatenate([keep, with_other_core(send)], 0)
-
-    def whole(values):
-        return jnp.concatenate([values, with_other_core(values)], 0)
-
-    def term(left, right):
-        split = left.reshape(2 * tokens, SHARDS, -1)
-        return jnp.einsum(
-            "tkr,tn->krn", split, right, preferred_element_type=jnp.float32
-        ).astype(jnp.bfloat16)
-
-    in_rows = halved(first_norm.reshape(tokens, SHARDS, PADDED), 2)
-    out_rows = halved(mixed.reshape(tokens, SHARDS, PADDED), 2)
+    extent = values.shape[axis] // 2
+    keep = lax.dynamic_slice_in_dim(values, core * extent, extent, axis)
+    send = lax.dynamic_slice_in_dim(values, (1 - core) * extent, extent, axis)
+    return jnp.concatenate([keep, with_other_core(send)], 0)
+
+
+def whole(values):
+    return jnp.concatenate([values, with_other_core(values)], 0)
+
+
+def term(left, right):
+    split = left.reshape(left.shape[0], SHARDS, -1)
+    return jnp.einsum("tkr,tn->krn", split, right, preferred_element_type=jnp.float32).astype(
+        jnp.bfloat16
+    )
+
+
+def feed_forward_terms(second_norm, act, gated_slope, down_in):
+    return (
+        term(whole(second_norm), halved(gated_slope, 1)),
+        term(whole(act), halved(down_in, 1)),
+    )
+
+
+def attention_terms(first_norm, mixed, projected_slope, branch_slope, gain_slopes):
+    core = lax.axis_index("dp") % 2
+    by_shard = (-1, SHARDS, PADDED)
+    in_rows = halved(first_norm.reshape(by_shard), 2)
+    out_rows = halved(pad_shards(mixed[:, :QUERY_WIDTH]).reshape(by_shard), 2)
     in_term = term(in_rows, whole(projected_slope))
     gains = (gain_slopes + with_other_core(gain_slopes)).reshape(2, SHARDS, ROWS).swapaxes(0, 1)
     spare = PADDED // 2 - (PADDED - ROWS)
     in_term = in_term.at[:, spare : spare + 2, :ROWS].add(
         jnp.where(core == 1, gains, 0.0).astype(jnp.bfloat16)
     )
-    return (
-        term(whole(second_norm), halved(gated_slope, 1)),
-        term(whole(act), halved(down_in, 1)),
-        in_term,
-        term(out_rows, whole(branch_slope)),
-    )
+    return (in_term, term(out_rows, whole(branch_slope)))
 
 
 def body(
@@ -1012,47 +1280,44 @@
         ],
         0,
     )
-    gathered = gather_weights(
-        (
-            jnp.pad(gate_up[0], ((0, extra), (0, 0))),
-            jnp.pad(down_weight[0], ((0, 0), (0, DOWN_COLUMNS - D))),
-            in_shard,
-            jnp.pad(attend_out[0], ((0, extra), (0, 0))),
-        )
-    )
-    gains = gathered[2][:, ROWS : ROWS + 2, :ROWS].swapaxes(0, 1).reshape(2, D)
+    gathered = gather_weights((in_shard, jnp.pad(attend_out[0], ((0, extra), (0, 0)))))
+    gains = gathered[0][:, ROWS : ROWS + 2, :ROWS].swapaxes(0, 1).reshape(2, D)
+    out_weight = gathered[1][:, :ROWS].reshape(QUERY_WIDTH, D)
     weights = (
-        gathered[2].reshape(-1, QKV),
-        jnp.pad(gathered[3][:, :ROWS].reshape(QUERY_WIDTH, D), ((0, FULL - QUERY_WIDTH), (0, 0))),
-        gathered[0].reshape(-1, 2 * FF),
-        gathered[1].reshape(-1, DOWN_COLUMNS),
+        gathered[0].reshape(-1, QKV),
+        jnp.pad(out_weight, ((0, FULL - QUERY_WIDTH), (0, 0))),
+        None,
+        None,
         gains.astype(jnp.float32),
+    )
+    shards = (
+        jnp.pad(gate_up[0], ((0, extra), (0, 0))),
+        jnp.pad(down_weight[0], ((0, 0), (0, DOWN_COLUMNS - D))),
     )
     plan_row = plan[0]
     fresh = jnp.take(inputs[:, 0], plan_row, axis=0)
     tables = rotary_tables(jnp.take(positions[:, 0], plan_row, axis=0))
     given = cotangent[:, 0]
-    result, _ = forward_layer(fresh, tables, weights)
+    result, _, weights = forward_layer(fresh, tables, weights, shards)
     layer_in = jnp.where(section_index == 0, fresh, passed_along(result, 1))
-    outputs, kept = forward_layer(layer_in, tables, weights)
-    input_slope, _, _ = backward_layer(given, kept, tables, weights)
+    outputs, kept, _ = forward_layer(layer_in, tables, weights)
+    input_slope = backward_layer(given, kept, tables, weights)
     back = passed_along(input_slope.astype(jnp.bfloat16), -1)
     upstream = jnp.where(section_index == 1, given, back)
-    input_slope, slopes, gain_slopes = backward_layer(upstream, kept, tables, weights)
+    input_slope, summed = backward_layer(upstream, kept, tables, weights, True)
     reported = jnp.where(
         section_index == 0, input_slope, input_slope.astype(jnp.bfloat16).astype(jnp.float32)
     )
     input_slopes = jnp.take(reported, plan_row, axis=0)
-    summed = reduce_gradients(weight_terms(kept, slopes, gain_slopes))
     full = [value.astype(jnp.float32) for value in summed]
     return (
         outputs[None, :, None],
         input_slopes[None, :, None],
+        full[0][None, :ROWS],
+        full[1][None, :ROWS],
         full[2][None, :ROWS],
-        full[3][None, :ROWS],
-        full[0][None, :ROWS],
-        full[1][None, :, :D],
-        full[2][None, ROWS : ROWS + 2, :ROWS],
+        full[3][None, :, :D],
+        full[0][None, ROWS : ROWS + 2, :ROWS],
     )
 
 

time: 536 us -> 522 us (0.974); the launches traced: 535 us -> 515 us
  Pallas kernels: 336 us -> 307 us
  other arithmetic: 39.4 us -> 46.2 us
    pallas_call x6, Pallas kernels: 336 us -> 307 us  [the longest x2 135 us: attend_back(): pl.pallas_call(functools.partial(attend_back_kernel, with_reduce), name='...]
    unnamed x165 -> x147, local copies, waits for them, and re-layouts: 11.4 us -> 11.7 us
  transfers between devices with their start and end apart: 11 -> 11, of which waited for: 1 -> 2; matrix products, arithmetic and copies ran while one was open for 14% -> 18% of each run, Pallas kernels for 6% -> 21%
where the time goes in v4:
time: 522 us; the launch traced here: 515 us
  Pallas kernels  307 us (59%)
  matrix products  75.5 us (14%)
  local copies, waits for them, and re-layouts  58.3 us (11%)
  other arithmetic  46.2 us (9%)
  starting transfers between devices  17.5 us (3%)
  waiting for transfers between devices  8.53 us (2%)
    pallas_call x2, Pallas kernels, attend_back(): pl.pallas_call(functools.partial(attend_back_kernel, with_reduce), name='...  135 us
    pallas_call x2, Pallas kernels, attend(): pl.pallas_call(functools.partial(attend_kernel, with_gather), name='atten...  107 us
    pallas_call x1, Pallas kernels, reduce_gradients(): pl.pallas_call(functools.partial(reduce_kernel, ATTENTION), name='reduce_...  36 us
    pallas_call x1, Pallas kernels, gather_weights(): pl.pallas_call(functools.partial(gather_kernel, ATTENTION), name='gather_...  28.7 us
    dot_general x2, matrix products, backward_layer(): jnp.einsum('td,fd->tf', down_in, down_weight, preferred_element_type=jnp....  15.7 us
    dot_general x4, matrix products, term(): jnp.einsum('tkr,tn->krn', split, right, preferred_element_type=jnp.float32)  15.6 us
    dot_general x2, matrix products, forward_layer(): gated = jnp.dot(second_norm, gate_up, preferred_element_type=jnp.float32)  11.8 us
    ppermute x9, starting transfers between devices, with_other_core(): lax.ppermute(value, 'dp', [(index, index ^ 1) for index in range(size)])  11.7 us
  transfers between devices with their start and end apart: 11, of which 2 were waited for; matrix products, arithmetic and copies ran while one was open for 18% of the time, Pallas kernels for 21%

profile of v4, /device:TPU:1, one launch (start us, length us, event | category | flops | bytes accessed | tf_op | source)
XLA Modules:
  0.0 515.3 jit_solution(7170619054542458839)
XLA Ops:
  5.8 28.7 %gather_weights.1 = (bf16[8,128,1600]{2,1,0:T(8,128)(2,1)}, bf16[8,128,960]{2,1,0:T(8,128)(2,1)}) custom-call(bf16[128,1600]{1,0:T(8,128)(2,1)} %fusion.113.refs_0_, bf16[128,960]{1,0:T(8,128)(2,1)} %pad.55.refs_1_), custom_call_target="tpu_custom_call" | custom-call | tf_op jit(solution)/shard_map/gather_weights/pallas_call | solution.py:276
  35.9 3.4 fusion.104
  46.9 71.6 %attend_gather.1 = (bf16[2,128,1024]{2,1,0:T(8,128)(2,1)S(1)}, bf16[2,1024,128]{2,1,0:T(8,128)(2,1)}, bf16[2,2,1024,128]{3,2,1,0:T(8,128)(2,1)}, f32[2,1024,128]...) custom-call(bf16[2,128,1024]{2,1,0:T(8,128)(2,1)S(1)} %pad.57.refs_0_, ...), custom_call_target="tpu_custom_call" | custom-call | tf_op jit(solution)/shard_map/attend_gather/pallas_call | solution.py:822
  123.1 5.9 %convolution_bitcast_fusion.1 = f32[256,5120]{1,0:T(8,128)S(1)} fusion(bf16[8,128,5120]{2,1,0:T(8,128)(2,1)} %get-tuple-element.41, bf16[256,8,120]{2,0,1:T(8,128)(2,1)S(1)} %copy.60), kind=kOutput, calls=%fused_computation.8 | convolution fusion | flops 2684354560 | bytes 16220160 | tf_op jit(solution)/shard_map/dot_general | solution.py:1129
  131.4 4.4 collective-permute-start
  138.8 7.6 %collective-permute-done = bf16[2,128,960]{1,2,0:T(8,128)(2,1)S(1)} collective-permute-done((bf16[2,128,960]{1,2,0:T(8,128)(2,1)S(1)}, bf16[2,128,960]{1,2,0:T(8,128)(2,1)S(1)}, u32[]{:S(2)}, u32[]{:S(2)}) %collective-permute-start) | collective-permute-done | bytes 491552 | tf_op jit(solution)/shard_map/ppermute | solution.py:1222
  150.2 3.4 fusion.102
  154.8 35.1 %attend.1 = (bf16[2,128,1024]{2,1,0:T(8,128)(2,1)S(1)}, bf16[2,1024,128]{2,1,0:T(8,128)(2,1)S(1)}, bf16[2,2,1024,128]{3,2,1,0:T(8,128)(2,1)S(1)}, f32[2,1024,128]{2,1,0:T(8,128)S(1)}) custom-call(bf16[2,128,1024]{2,1,0:T(8,128)(2,1)S(1)} %pad.63.refs_0_, bf16[2,128,640]{2,1,0:T(8,128)(2,1)S(1)} %copy.67.refs_1_), custom_call_target="tpu_custom_call" | custom-call | tf_op jit(solution)/shard_map/attend/pallas_call | solution.py:822
  189.9 3.7 multiply_reduce_fusion.6
  197.6 5.9 %convolution_bitcast_fusion = f32[256,5120]{1,0:T(8,128)S(1)} fusion(bf16[8,128,5120]{2,1,0:T(8,128)(2,1)} %get-tuple-element.41, bf16[256,8,120]{2,0,1:T(8,128)(2,1)} %copy.68), kind=kOutput, calls=%fused_computation.7 | convolution fusion | flops 2684354560 | bytes 16220160 | tf_op jit(solution)/shard_map/dot_general | solution.py:1129
  203.6 7.1 %multiply_convert_fusion.3 = (bf16[256,2560]{1,0:T(8,128)(2,1)S(1)}, bf16[256,2560]{1,0:T(8,128)(2,1)S(1)}) fusion(f32[256,5120]{1,0:T(8,128)S(1)} %convolution_bitcast_fusion, bf16[2560,1024]{1,0:T(8,128)(2,1)} %bitcast.315, bf16[256,960]{0,1:T(8,128)(2,1)S(1)} %bitcast.370), kind=kOutput, calls=%fused_computation.37 | convolution fusion | flops 1350696960 | bytes 13598720 | tf_op jit(solution)/shard_map/td,fd->tf/dot_general | solution.py:1163
  210.8 3.0 fusion.2
  216.3 29.3 %attend_back.1 = (bf16[2,128,1024]{2,1,0:T(8,128)(2,1)S(1)}, bf16[8,2,128,128]{3,2,1,0:T(8,128)(2,1)S(1)}, bf16[2,2,128,128]{3,2,1,0:T(8,128)(2,1)S(1)}) custom-call(bf16[2,128,1024]{2,1,0:T(8,128)(2,1)S(1)} %bitcast.314, bf16[2,1024,128]{2,1,0:T(8,128)(2,1)S(1)} %get-tuple-element.44.refs_1_, bf16[2,2,1024,128]{3,2,1,0:T(8,128)(2,1)S(1)} %get-tuple-element.45.refs_2_, ...), custom_call_target="tpu_custom_call" | custom-call | tf_op jit(solution)/shard_map/attend_back/pallas_call | solution.py:1021
  264.0 4.6 collective-permute-start.9
  274.8 8.6 %multiply_convert_fusion.1 = (bf16[256,2560]{1,0:T(8,128)(2,1)S(1)}, bf16[256,2560]{1,0:T(8,128)(2,1)S(1)}, bf16[256,2560]{1,0:T(8,128)(2,1)}) fusion(f32[256,5120]{1,0:T(8,128)} %copy-done.17, bf16[2560,1024]{1,0:T(8,128)(2,1)} %bitcast.316, bf16[256,960]{0,1:T(8,128)(2,1)S(1)} %copy_bitcast_fusion.1), kind=kOutput, calls=%fused_computation.35 | convolution fusion | flops 1352663040 | bytes 14909440 | tf_op jit(solution)/shard_map/td,fd->tf/dot_general | solution.py:1163
  283.5 3.0 fusion
  286.9 2.9 fusion.151
  289.8 5.1 collective-permute-start.10
  294.9 2.5 fusion.46
  297.9 3.5 fusion.59
  303.3 3.3 fusion.56
  311.4 3.4 pad_maximum_fusion.1
  314.8 4.4 copy.83
  319.3 5.1 convolution_convert_fusion.2.refs_5_
  324.3 6.0 %convolution_convert_fusion.refs_4_ = bf16[8,128,2560]{2,1,0:T(8,128)(2,1)} fusion(bf16[256,2560]{1,0:T(8,128)(2,1)} %collective-permute-done.3, bf16[256,2560]{1,0:T(8,128)(2,1)S(1)} %copy-done.38, bf16[256,8,128]{2,0,1:T(8,128)(2,1)S(1)} %copy-done.44, bf16[256,8,128]{2,0,1:T(8,128)(2,1)S(1)} %copy-done.32), kind=kOutput, calls=%fused_computation.9 | convolution fusion | flops 2694316032 | bytes 8912896 | tf_op jit(solution)/shard_map/tkr,tn->krn/dot_general | solution.py:1245
  330.3 106.1 %attend_back_reduce.1 = (bf16[2,128,1024]{2,1,0:T(8,128)(2,1)}, bf16[8,2,128,128]{3,2,1,0:T(8,128)(2,1)}, bf16[2,2,128,128]{3,2,1,0:T(8,128)(2,1)}, bf16[128,5120]{1,0:T(8,128)(2,1)}, bf16[320,1024]{1,0:T(8,128)(2,1)}) custom-call(bf16[2,128,1024]{2,1,0:T(8,128)(2,1)} %bitcast.369, bf16[2,1024,128]{2,1,0:T(8,128)(2,1)} %copy-done.4, ...), custom_call_target="tpu_custom_call" | custom-call | tf_op jit(solution)/shard_map/attend_back_reduce/pallas_call | solution.py:1021
  441.8 2.5 copy.86
  447.5 2.5 copy.85
  458.7 4.1 multiply_reduce_fusion.1
  464.6 3.0 bitcast_convert_fusion
  473.8 2.5 convolution_convert_fusion.1
  476.8 36.0 %reduce_gradients.1 = (bf16[128,1600]{1,0:T(8,128)(2,1)S(1)}, bf16[128,960]{1,0:T(8,128)(2,1)S(1)}) custom-call(bf16[8,64,1600]{2,1,0:T(8,128)(2,1)S(1)} %scatter-add.4.refs_0_, bf16[8,64,960]{2,1,0:T(8,128)(2,1)S(1)} %convolution_convert_fusion.3.refs_1_), custom_call_target="tpu_custom_call" | custom-call | tf_op jit(solution)/shard_map/reduce_gradients/pallas_call | solution.py:576
  (313 shorter events, 94.8 us)
Async XLA Ops:
  2.1 39.0 %copy-start.53 = (pred[2]{0:T(512)(128)(4,1)}, pred[2]{0:T(512)(128)(4,1)S(1)}, u32[]{:S(2)}) copy-start(pred[2]{0:T(512)(128)(4,1)S(1)} %compare_and_fusion) | copy-start | bytes 10
  2.1 38.4 %copy-start.56 = (s32[1024]{0:T(1024)}, s32[1024]{0:T(1024)S(1)}, u32[]{:S(2)}) copy-start(s32[1024]{0:T(1024)S(1)} %pad_clamp_fusion) | copy-start | bytes 12292
  3.6 32.4 %copy-start.57 = (pred[256]{0:T(512)(128)(4,1)}, pred[256]{0:T(512)(128)(4,1)S(1)}, u32[]{:S(2)}) copy-start(pred[256]{0:T(512)(128)(4,1)S(1)} %broadcast_bitcast_fusion) | copy-start | bytes 772
  41.8 94.0 %copy-start.30 = (f32[2,128,64]{2,1,0:T(8,128)}, f32[2,128,64]{2,1,0:T(8,128)S(1)}, u32[]{:S(2)}) copy-start(f32[2,128,64]{2,1,0:T(8,128)S(1)} %get-tuple-element.114) | copy-start | bytes 196612
  46.7 74.2 %copy-start.58 = (pred[256]{0:T(512)(128)(4,1)S(1)}, pred[256]{0:T(512)(128)(4,1)}, u32[]{:S(2)}) copy-start(pred[256]{0:T(512)(128)(4,1)} %copy-done.57) | copy-start | bytes 772
  46.9 74.9 %copy-start.13 = (bf16[8,120,960]{2,1,0:T(8,128)(2,1)}, bf16[8,120,960]{2,1,0:T(8,128)(2,1)S(1)}, u32[]{:S(2)}) copy-start(bf16[8,120,960]{2,1,0:T(8,128)(2,1)S(1)} %slice.259) | copy-start | bytes 5529604
  129.0 7.5 %copy-start.15 = (bf16[2,1,128,960]{2,3,1,0:T(8,128)(2,1)S(1)}, bf16[2,1,128,960]{2,3,1,0:T(8,128)(2,1)}, u32[]{:S(2)}) copy-start(bf16[2,1,128,960]{2,3,1,0:T(8,128)(2,1)} %param.19) | copy-start | bytes 1474564
  131.4 15.0 %copy-start.54 = (pred[2]{0:T(512)(128)(4,1)S(1)}, pred[2]{0:T(512)(128)(4,1)}, u32[]{:S(2)}) copy-start(pred[2]{0:T(512)(128)(4,1)} %copy-done.53) | copy-start | bytes 10
  131.4 15.0 %collective-permute-start = (bf16[2,128,960]{1,2,0:T(8,128)(2,1)S(1)}, bf16[2,128,960]{1,2,0:T(8,128)(2,1)S(1)}, u32[]{:S(2)}, u32[]{:S(2)}) collective-permute-start(bf16[2,128,960]{1,2,0:T(8,128)(2,1)S(1)} %bitcast.371), channel_id=1, source_target_pairs={{0,64},{1,65},{2,66},{3,67},{4,68},{5,69},{6,70},{7,71},{8,72},{9,... | collective-permute-start | bytes 1474568 | tf_op jit(solution)/shard_map/ppermute | solution.py:1222
  189.9 26.3 %copy-start.2 = (bf16[2,2,1024,128]{3,2,1,0:T(8,128)(2,1)}, bf16[2,2,1024,128]{3,2,1,0:T(8,128)(2,1)S(1)}, u32[]{:S(2)}) copy-start(bf16[2,2,1024,128]{3,2,1,0:T(8,128)(2,1)S(1)} %get-tuple-element.45.refs_2_) | copy-start | bytes 3145732
  189.9 26.3 %copy-start.3 = (f32[2,1024,128]{2,1,0:T(8,128)}, f32[2,1024,128]{2,1,0:T(8,128)S(1)}, u32[]{:S(2)}) copy-start(f32[2,1024,128]{2,1,0:T(8,128)S(1)} %get-tuple-element.46.refs_3_) | copy-start | bytes 3145732
  189.9 26.3 %copy-start.4 = (bf16[2,1024,128]{2,1,0:T(8,128)(2,1)}, bf16[2,1024,128]{2,1,0:T(8,128)(2,1)S(1)}, u32[]{:S(2)}) copy-start(bf16[2,1024,128]{2,1,0:T(8,128)(2,1)S(1)} %get-tuple-element.44.refs_1_) | copy-start | bytes 1572868
  197.6 13.1 %slice-start.4 = ((s8[10485760]{0:T(1024)(128)(4,1)}), s8[4194304]{0:T(1024)(128)(4,1)S(1)}, s32[]{:S(2)}) async-start(s8[10485760]{0:T(1024)(128)(4,1)} %bitcast.324), calls=%async_computation.4 | async-start | bytes 8388608
  197.6 13.1 %slice-start.5 = ((s8[10485760]{0:T(1024)(128)(4,1)}), s8[4194304]{0:T(1024)(128)(4,1)S(1)}, s32[]{:S(2)}) async-start(s8[10485760]{0:T(1024)(128)(4,1)} %bitcast.324), calls=%async_computation.5 | async-start | bytes 8388608
  203.6 7.2 %slice-start.6 = ((s8[10485760]{0:T(1024)(128)(4,1)}), s8[2097152]{0:T(1024)(128)(4,1)S(1)}, s32[]{:S(2)}) async-start(s8[10485760]{0:T(1024)(128)(4,1)} %bitcast.324), calls=%async_computation.6 | async-start | bytes 4194304
  260.6 13.1 %copy-start.16 = (bf16[2,1,128,960]{2,3,1,0:T(8,128)(2,1)S(1)}, bf16[2,1,128,960]{2,3,1,0:T(8,128)(2,1)}, u32[]{:S(2)}) copy-start(bf16[2,1,128,960]{2,3,1,0:T(8,128)(2,1)} %param.19) | copy-start | bytes 1474564
  260.6 13.1 %collective-permute-start.1 = (bf16[2,128,960]{1,2,0:T(8,128)(2,1)}, bf16[2,128,960]{1,2,0:T(8,128)(2,1)}, u32[]{:S(2)}, u32[]{:S(2)}) collective-permute-start(bf16[2,128,960]{1,2,0:T(8,128)(2,1)} %copy_bitcast_fusion.2), channel_id=1, source_target_pairs={{64,0},{65,1},{66,2},{67,3},{68,4},{69,5},{70,6},{71,7},{72,8},{73... | collective-permute-start | bytes 1474568 | tf_op jit(solution)/shard_map/ppermute | solution.py:1222
  264.0 44.6 %collective-permute-start.9 = (bf16[256,8,64]{0,2,1:T(8,128)(2,1)}, bf16[256,8,64]{0,2,1:T(8,128)(2,1)}, u32[]{:S(2)}, u32[]{:S(2)}) collective-permute-start(bf16[256,8,64]{0,2,1:T(8,128)(2,1)} %get-tuple-element.99), channel_id=1, source_target_pairs={{0,8},{8,0},{16,24},{24,16},{32,40},{40,32},{48,56},{56,48},{1,9},... | collective-permute-start | bytes 786440 | tf_op jit(solution)/shard_map/ppermute | solution.py:1227
  270.7 35.8 %collective-permute-start.2 = (bf16[256,1024]{0,1:T(8,128)(2,1)}, bf16[256,1024]{0,1:T(8,128)(2,1)}, u32[]{:S(2)}, u32[]{:S(2)}) collective-permute-start(bf16[256,1024]{0,1:T(8,128)(2,1)} %bitcast.50), channel_id=1, source_target_pairs={{0,8},{8,0},{16,24},{24,16},{32,40},{40,32},{48,56},{56,48},{1,9},... | collective-permute-start | bytes 1572872 | tf_op jit(solution)/shard_map/ppermute | solution.py:1227
  270.7 12.7 %slice-start.7 = ((s8[10485760]{0:T(1024)(128)(4,1)}), s8[4194304]{0:T(1024)(128)(4,1)S(1)}, s32[]{:S(2)}) async-start(s8[10485760]{0:T(1024)(128)(4,1)} %bitcast.326), calls=%async_computation.7 | async-start | bytes 8388608
  274.8 8.6 %slice-start.8 = ((s8[10485760]{0:T(1024)(128)(4,1)}), s8[4194304]{0:T(1024)(128)(4,1)S(1)}, s32[]{:S(2)}) async-start(s8[10485760]{0:T(1024)(128)(4,1)} %bitcast.326), calls=%async_computation.8 | async-start | bytes 8388608
  274.8 8.6 %slice-start.9 = ((s8[10485760]{0:T(1024)(128)(4,1)}), s8[2097152]{0:T(1024)(128)(4,1)S(1)}, s32[]{:S(2)}) async-start(s8[10485760]{0:T(1024)(128)(4,1)} %bitcast.326), calls=%async_computation.9 | async-start | bytes 4194304
  286.4 11.5 %slice-start.2 = ((s8[5242880]{0:T(1024)(128)(4,1)}), s8[4194304]{0:T(1024)(128)(4,1)S(1)}, s32[]{:S(2)}) async-start(s8[5242880]{0:T(1024)(128)(4,1)} %bitcast.320), calls=%async_computation.2 | async-start | bytes 8388608
  286.9 11.0 %slice-start.3 = ((s8[5242880]{0:T(1024)(128)(4,1)}), s8[1048576]{0:T(1024)(128)(4,1)S(1)}, s32[]{:S(2)}) async-start(s8[5242880]{0:T(1024)(128)(4,1)} %bitcast.320), calls=%async_computation.3 | async-start | bytes 2097152
  289.8 19.5 %collective-permute-start.10 = (bf16[256,960]{0,1:T(8,128)(2,1)}, bf16[256,960]{0,1:T(8,128)(2,1)}, u32[]{:S(2)}, u32[]{:S(2)}) collective-permute-start(bf16[256,960]{0,1:T(8,128)(2,1)} %fusion.151), channel_id=1, source_target_pairs={{0,8},{8,0},{16,24},{24,16},{32,40},{40,32},{48,56},{56,48},{1,9},... | collective-permute-start | bytes 1474568 | tf_op jit(solution)/shard_map/ppermute | solution.py:1227
  294.9 16.5 %collective-permute-start.4 = (bf16[256,2560]{1,0:T(8,128)(2,1)}, bf16[256,2560]{1,0:T(8,128)(2,1)}, u32[]{:S(2)}, u32[]{:S(2)}) collective-permute-start(bf16[256,2560]{1,0:T(8,128)(2,1)} %get-tuple-element.83), channel_id=1, source_target_pairs={{0,8},{8,0},{16,24},{24,16},{32,40},{40,32},{48,56},{56,48},{1,9},... | collective-permute-start | bytes 3932168 | tf_op jit(solution)/shard_map/ppermute | solution.py:1227
  297.4 26.9 %collective-permute-start.3 = (bf16[256,2560]{1,0:T(8,128)(2,1)}, bf16[256,2560]{1,0:T(8,128)(2,1)}, u32[]{:S(2)}, u32[]{:S(2)}) collective-permute-start(bf16[256,2560]{1,0:T(8,128)(2,1)} %get-tuple-element.85), channel_id=1, source_target_pairs={{0,8},{8,0},{16,24},{24,16},{32,40},{40,32},{48,56},{56,48},{1,9},... | collective-permute-start | bytes 3932168 | tf_op jit(solution)/shard_map/ppermute | solution.py:1227
  306.6 167.2 %collective-permute-start.6 = (bf16[256,8,64]{0,2,1:T(8,128)(2,1)}, bf16[256,8,64]{0,2,1:T(8,128)(2,1)}, u32[]{:S(2)}, u32[]{:S(2)}) collective-permute-start(bf16[256,8,64]{0,2,1:T(8,128)(2,1)} %get-tuple-element.101), channel_id=1, source_target_pairs={{0,8},{8,0},{16,24},{24,16},{32,40},{40,32},{48,56},{56,48},{1,9},... | collective-permute-start | bytes 786440 | tf_op jit(solution)/shard_map/ppermute | solution.py:1227
  308.6 10.6 %collective-permute-start.5 = (bf16[256,512]{0,1:T(8,128)(2,1)}, bf16[256,512]{0,1:T(8,128)(2,1)}, u32[]{:S(2)}, u32[]{:S(2)}) collective-permute-start(bf16[256,512]{0,1:T(8,128)(2,1)} %get-tuple-element.103), channel_id=1, source_target_pairs={{0,8},{8,0},{16,24},{24,16},{32,40},{40,32},{48,56},{56,48},{1,9},... | collective-permute-start | bytes 786440 | tf_op jit(solution)/shard_map/ppermute | solution.py:1227
  463.9 9.8 %collective-permute-start.8 = (f32[2,960]{1,0:T(2,128)S(1)}, f32[2,960]{1,0:T(2,128)S(1)}, u32[]{:S(2)}, u32[]{:S(2)}) collective-permute-start(f32[2,960]{1,0:T(2,128)S(1)} %pad_maximum_fusion.9), channel_id=1, source_target_pairs={{0,8},{8,0},{16,24},{24,16},{32,40},{40,32},{48,56},{56,48},{1,9},... | collective-permute-start | bytes 23048 | tf_op jit(solution)/shard_map/ppermute | solution.py:1227
  464.2 9.5 %collective-permute-start.7 = (bf16[256,1600]{0,1:T(8,128)(2,1)}, bf16[256,1600]{0,1:T(8,128)(2,1)}, u32[]{:S(2)}, u32[]{:S(2)}) collective-permute-start(bf16[256,1600]{0,1:T(8,128)(2,1)} %pad_maximum_fusion.4), channel_id=1, source_target_pairs={{0,8},{8,0},{16,24},{24,16},{32,40},{40,32},{48,56},{56,48},{1,9},... | collective-permute-start | bytes 2457608 | tf_op jit(solution)/shard_map/ppermute | solution.py:1227
  476.3 38.8 %copy-start.1 = (bf16[2,1,128,960]{2,3,1,0:T(8,128)(2,1)S(1)}, bf16[2,1,128,960]{2,3,1,0:T(8,128)(2,1)}, u32[]{:S(2)}) copy-start(bf16[2,1,128,960]{2,3,1,0:T(8,128)(2,1)} %param.11) | copy-start | bytes 1474564
  (49 other events, 151.5 us)
